TPU v7x, 32 devices: a whole 2x2x4 slice. The times are simulated.
32 devices in a mesh: row: 4 (over y, x), col: 8 (over z, core).
Axes of the slice: x: 2, y: 2, z: 4, core: 2. Of those that a mesh axis runs over, the one named last changes fastest.
Arguments:
- features: bfloat16 [16384, 256], P(('row', 'col')), may hold values from -6 to 6
- weight: bfloat16 [256, 256], replicated, may hold values from -0.375 to 0.375
- adjacency: bfloat16 [4, 8, 384, 128, 128], P('row', 'col'), may hold values from -0.0546875 to 0.0546875
- block_rows: int32 [4, 8, 384], P('row', 'col'), may hold values from 0 to 31
- block_cols: int32 [4, 8, 384], P('row', 'col'), may hold values from 0 to 15
- live_blocks: int32 [4, 8], P('row', 'col'), may hold values from 96 to 384, as said below
- part_gains: float32 [16, 256], replicated, may hold values from 0.5 to 2
- partition: int32 [16384], P(('row', 'col')), may hold values from 0 to 15, never falling along the last dimension, each value on 1 to 2048 neighbouring positions
- cotangent: bfloat16 [16384, 256], P(('row', 'col')), may hold values from -6 to 6
Outputs:
- layer_out: bfloat16 [16384, 256], P(('row', 'col'))
- feature_grad: bfloat16 [16384, 256], P(('row', 'col'))
- weight_grad: float32 [256, 256], replicated
- gain_grad: float32 [16, 256], replicated
Inputs may be any that keep to these rules, and one draw needn't show every extreme that they name: Only the first live_blocks[i, j] slots of tile (i, j) are used; some tile uses all 384 slots. partition numbers never fall along the nodes; every partition has 1 to 2048 nodes, one exactly that many.
All inputs are finite; a program needn't handle non-finite values.
Results may differ from a plain program's by a relative error of at most 0.024.
Values may be sent and summed in bfloat16 or wider, within the bound.
No kernel may reach another device: no remote copies, remote signals or barrier semaphores. Data moves between devices by JAX's collectives and lax.ppermute only.
A program may use at most 128 MiB of HBM per device.

v0:
```python
import math

import jax
import jax.numpy as jnp
from jax import lax
from jax.sharding import PartitionSpec as P

BLOCK = 128


def silu_slope(values):
    sig = jax.nn.sigmoid(values)
    return sig * (1.0 + values * (1.0 - sig))


def tile_sum(tile_values, row_index, col_index, live_count, panels, out_blocks, forward):
    slot_count = tile_values.shape[0]
    group_size = math.gcd(slot_count, 64)
    feature_width = panels.shape[1]
    panel_blocks = panels.reshape(-1, BLOCK, feature_width)
    group_count = (live_count + group_size - 1) // group_size

    def one_group(position, totals):
        first_slot = position * group_size
        values_here = lax.dynamic_slice_in_dim(tile_values, first_slot, group_size, 0)
        rows_here = lax.dynamic_slice_in_dim(row_index, first_slot, group_size, 0)
        cols_here = lax.dynamic_slice_in_dim(col_index, first_slot, group_size, 0)
        slot_mask = (first_slot + jnp.arange(group_size, dtype=jnp.int32) < live_count).astype(
            jnp.float32
        )
        if forward:
            products = jnp.einsum(
                "kab,kbf->kaf",
                values_here,
                panel_blocks[cols_here],
                preferred_element_type=jnp.float32,
            )
            targets = rows_here
        else:
            products = jnp.einsum(
                "kab,kaf->kbf",
                values_here,
                panel_blocks[rows_here],
                preferred_element_type=jnp.float32,
            )
            targets = cols_here
        return totals.at[targets].add(products * slot_mask[:, None, None])

    start_totals = jnp.zeros((out_blocks, BLOCK, feature_width), jnp.float32)
    totals = lax.fori_loop(0, group_count, one_group, start_totals)
    return totals.reshape(out_blocks * BLOCK, feature_width)


def per_device(
    features,
    weight,
    adjacency,
    block_rows,
    block_cols,
    live_blocks,
    part_gains,
    partition,
    cotangent,
):
    node_count = features.shape[0]
    live_count = live_blocks[0, 0]
    tile_values = adjacency[0, 0]
    row_index = block_rows[0, 0]
    col_index = block_cols[0, 0]
    hidden = jnp.dot(features, weight, preferred_element_type=jnp.float32).astype(jnp.bfloat16)
    panels = lax.all_gather(hidden, "row", axis=0, tiled=True)
    member = (
        partition[:, None] == jnp.arange(part_gains.shape[0], dtype=jnp.int32)[None, :]
    ).astype(jnp.float32)
    row_gains = jnp.dot(member, part_gains, precision=lax.Precision.HIGHEST)
    upstream = cotangent.astype(jnp.float32) * row_gains
    partial_rows = tile_sum(
        tile_values,
        row_index,
        col_index,
        live_count,
        panels,
        node_count * lax.axis_size("col") // BLOCK,
        True,
    )
    summed = lax.psum_scatter(
        partial_rows.astype(jnp.bfloat16), "col", scatter_dimension=0, tiled=True
    ).astype(jnp.float32)
    local_grad = (upstream * silu_slope(summed)).astype(jnp.bfloat16)
    agg_grad = lax.all_gather(local_grad, "col", axis=0, tiled=True)
    activated = jax.nn.silu(summed)
    layer_out = (activated * row_gains).astype(jnp.bfloat16)
    partial_cols = tile_sum(
        tile_values,
        row_index,
        col_index,
        live_count,
        agg_grad,
        node_count * lax.axis_size("row") // BLOCK,
        False,
    )
    hidden_grad = lax.psum_scatter(
        partial_cols.astype(jnp.bfloat16), "row", scatter_dimension=0, tiled=True
    )
    feature_grad = lax.dot_general(
        hidden_grad, weight, (((1,), (1,)), ((), ())), preferred_element_type=jnp.float32
    ).astype(jnp.bfloat16)
    weight_part = lax.dot_general(
        features, hidden_grad, (((0,), (0,)), ((), ())), preferred_element_type=jnp.float32
    )
    part_terms = jnp.dot(
        member.T, cotangent.astype(jnp.float32) * activated, precision=lax.Precision.HIGHEST
    )
    part_sizes = jnp.sum(member, axis=0)
    weight_total, part_total, size_total = lax.psum(
        (weight_part, part_terms, part_sizes), ("row", "col")
    )
    total_nodes = node_count * lax.axis_size("row") * lax.axis_size("col")
    weight_grad = weight_total / jnp.sqrt(jnp.float32(total_nodes))
    gain_grad = part_total / jnp.sqrt(size_total)[:, None]
    return (layer_out, feature_grad, weight_grad, gain_grad)


def solution(mesh):
    in_specs = (
        P(("row", "col"), None),
        P(),
        P("row", "col", None, None, None),
        P("row", "col", None),
        P("row", "col", None),
        P("row", "col"),
        P(),
        P(("row", "col")),
        P(("row", "col"), None),
    )
    out_specs = (P(("row", "col"), None), P(("row", "col"), None), P(), P())
    return jax.shard_map(
        per_device, mesh=mesh, in_specs=in_specs, out_specs=out_specs, check_vma=False
    )
```

profile of v0, /device:TPU:0, one launch (start us, length us, event | category | flops | bytes accessed | tf_op | source)
XLA Modules:
  0.0 618.1 jit_solution(14715299193632505659)
XLA Ops:
  7.2 0.9 copy-done
  8.1 1.8 convolution_convert_fusion.1
  10.7 0.7 reduce
  11.4 0.7 reduce.1
  12.1 27.7 %all-gather.3.cloned.1.call-done = bf16[2048,256]{1,0:T(8,128)(2,1)} async-done(((bf16[512,256]{1,0:T(8,128)(2,1)}), bf16[2048,256]{1,0:T(8,128)(2,1)}) %all-gather.3.cloned.1.call-update) | async-done | bytes 1048592 | tf_op jit(solution)/shard_map/all_gather | solution.py:71
  39.8 2.4 broadcast_in_dim.23
  42.2 120.0 %while.20 = (s32[]{:T(128)}, f32[32,128,256]{2,1,0:T(8,128)}, s32[]{:T(128)}, s32[384]{0:T(512)S(1)}, bf16[384,128,128]{2,1,0:T(8,128)(2,1)}, /*index=5*/s32[384...) while((s32[]{:T(128)}, f32[32,128,256]{2,1,0:T(8,128)}, ...), condition=%wide.region_2.3_spmd, body=%wide.region_0.2_spmd.sunk | while | flops 541066816 | bytes 48241072 | solution.py:50
  43.0 2.8 gather_fusion
  45.8 7.3 %broadcast_multiply_fusion.5 = f32[64,128,256]{2,1,0:T(8,128)} fusion(f32[64]{0:T(128)S(1)} %compare_convert_fusion.4, bf16[64,128,256]{2,1,0:T(8,128)(2,1)} %gather_fusion, bf16[384,128,128]{2,1,0:T(8,128)(2,1)} %get-tuple-element.292, s32[]{:T(128)S(6)} %select_n.38), kind=kOutput, calls=%fused_computation.4.clone.1 | convolution fusion | flops 538968064 | bytes 14680324 | tf_op jit(solution)/shard_map/while/body/kab,kbf->kaf/dot_general | solution.py:32
  53.0 19.3 %scatter_fusion = f32[32,128,256]{2,1,0:T(8,128)} fusion(f32[32,128,256]{2,1,0:T(8,128)} %get-tuple-element.277, s32[64]{0:T(128)S(1)} %get-tuple-element.252, f32[64,128,256]{2,1,0:T(8,128)} %broadcast_multiply_fusion.5), kind=kCustom, calls=%fused_computation.2.clone.1 | custom fusion | flops 2097152 | bytes 25166080 | tf_op jit(solution)/shard_map/while/body/scatter-add | solution.py:47
  73.0 2.8 gather_fusion
  75.8 7.3 %broadcast_multiply_fusion.5 = f32[64,128,256]{2,1,0:T(8,128)} fusion(f32[64]{0:T(128)S(1)} %compare_convert_fusion.4, bf16[64,128,256]{2,1,0:T(8,128)(2,1)} %gather_fusion, bf16[384,128,128]{2,1,0:T(8,128)(2,1)} %get-tuple-element.292, s32[]{:T(128)S(6)} %select_n.38), kind=kOutput, calls=%fused_computation.4.clone.1 | convolution fusion | flops 538968064 | bytes 14680324 | tf_op jit(solution)/shard_map/while/body/kab,kbf->kaf/dot_general | solution.py:32
  83.1 19.2 %scatter_fusion = f32[32,128,256]{2,1,0:T(8,128)} fusion(f32[32,128,256]{2,1,0:T(8,128)} %get-tuple-element.277, s32[64]{0:T(128)S(1)} %get-tuple-element.252, f32[64,128,256]{2,1,0:T(8,128)} %broadcast_multiply_fusion.5), kind=kCustom, calls=%fused_computation.2.clone.1 | custom fusion | flops 2097152 | bytes 25166080 | tf_op jit(solution)/shard_map/while/body/scatter-add | solution.py:47
  103.0 2.8 gather_fusion
  105.8 7.3 %broadcast_multiply_fusion.5 = f32[64,128,256]{2,1,0:T(8,128)} fusion(f32[64]{0:T(128)S(1)} %compare_convert_fusion.4, bf16[64,128,256]{2,1,0:T(8,128)(2,1)} %gather_fusion, bf16[384,128,128]{2,1,0:T(8,128)(2,1)} %get-tuple-element.292, s32[]{:T(128)S(6)} %select_n.38), kind=kOutput, calls=%fused_computation.4.clone.1 | convolution fusion | flops 538968064 | bytes 14680324 | tf_op jit(solution)/shard_map/while/body/kab,kbf->kaf/dot_general | solution.py:32
  113.0 19.2 %scatter_fusion = f32[32,128,256]{2,1,0:T(8,128)} fusion(f32[32,128,256]{2,1,0:T(8,128)} %get-tuple-element.277, s32[64]{0:T(128)S(1)} %get-tuple-element.252, f32[64,128,256]{2,1,0:T(8,128)} %broadcast_multiply_fusion.5), kind=kCustom, calls=%fused_computation.2.clone.1 | custom fusion | flops 2097152 | bytes 25166080 | tf_op jit(solution)/shard_map/while/body/scatter-add | solution.py:47
  133.0 2.8 gather_fusion
  135.7 7.3 %broadcast_multiply_fusion.5 = f32[64,128,256]{2,1,0:T(8,128)} fusion(f32[64]{0:T(128)S(1)} %compare_convert_fusion.4, bf16[64,128,256]{2,1,0:T(8,128)(2,1)} %gather_fusion, bf16[384,128,128]{2,1,0:T(8,128)(2,1)} %get-tuple-element.292, s32[]{:T(128)S(6)} %select_n.38), kind=kOutput, calls=%fused_computation.4.clone.1 | convolution fusion | flops 538968064 | bytes 14680324 | tf_op jit(solution)/shard_map/while/body/kab,kbf->kaf/dot_general | solution.py:32
  143.0 19.2 %scatter_fusion = f32[32,128,256]{2,1,0:T(8,128)} fusion(f32[32,128,256]{2,1,0:T(8,128)} %get-tuple-element.277, s32[64]{0:T(128)S(1)} %get-tuple-element.252, f32[64,128,256]{2,1,0:T(8,128)} %broadcast_multiply_fusion.5), kind=kCustom, calls=%fused_computation.2.clone.1 | custom fusion | flops 2097152 | bytes 25166080 | tf_op jit(solution)/shard_map/while/body/scatter-add | solution.py:47
  162.2 3.9 convert_element_type.49
  166.2 95.0 %reduce-scatter.3.cloned.1.call-done = bf16[512,256]{1,0:T(8,128)(2,1)} async-done(((bf16[4096,256]{1,0:T(8,128)(2,1)}), bf16[512,256]{1,0:T(8,128)(2,1)}) %reduce-scatter.3.cloned.1.call-update) | async-done | bytes 262160 | tf_op jit(solution)/shard_map/reduce_scatter | solution.py:86
  261.1 2.3 fusion.5
  263.5 16.6 %copy.16 = bf16[1,1,384,128,128]{3,4,2,1,0:T(8,128)(2,1)} copy(bf16[1,1,384,128,128]{4,3,2,1,0:T(8,128)(2,1)} %bitcast.26) | data formatting | bytes 25165824 | tf_op args[2]
  280.2 11.2 %all-gather.5.cloned.1.call-done = bf16[4096,256]{1,0:T(8,128)(2,1)} async-done(((bf16[512,256]{1,0:T(8,128)(2,1)}), bf16[4096,256]{1,0:T(8,128)(2,1)}) %all-gather.5.cloned.1.call-update) | async-done | bytes 2097168 | tf_op jit(solution)/shard_map/all_gather | solution.py:90
  291.5 99.3 %while.21 = (s32[]{:T(128)}, f32[16,128,256]{2,1,0:T(8,128)S(1)}, s32[]{:T(128)}, s32[384]{0:T(512)S(1)}, bf16[384,128,128]{1,2,0:T(8,128)(2,1)}, /*index=5*/s32...) while((s32[]{:T(128)}, f32[16,128,256]{2,1,0:T(8,128)S(1)}, ...), condition=%wide.region_6.7_spmd, body=%wide.region_4.6_spmd.sunk | while | flops 541066816 | bytes 48241072 | solution.py:50
  291.6 0.7 compare_convert_fusion.5
  292.3 4.4 gather_fusion.1
  296.7 7.3 %broadcast_multiply_fusion.6 = f32[64,128,256]{2,1,0:T(8,128)} fusion(f32[64]{0:T(128)S(1)} %compare_convert_fusion.5, bf16[64,128,256]{2,1,0:T(8,128)(2,1)} %gather_fusion.1, bf16[384,128,128]{1,2,0:T(8,128)(2,1)} %get-tuple-element.328, s32[]{:T(128)S(6)} %select_n.40), kind=kOutput, calls=%fused_computation.11.clone.1 | convolution fusion | flops 538968064 | bytes 14680324 | tf_op jit(solution)/shard_map/while/body/kab,kaf->kbf/dot_general | solution.py:40
  303.9 12.4 %scatter_fusion.1 = f32[16,128,256]{2,1,0:T(8,128)S(1)} fusion(f32[16,128,256]{2,1,0:T(8,128)S(1)} %get-tuple-element.313, s32[64]{0:T(128)S(1)} %get-tuple-element.262, f32[64,128,256]{2,1,0:T(8,128)} %broadcast_multiply_fusion.6), kind=kCustom, calls=%fused_computation.3.clone.1 | custom fusion | flops 2097152 | bytes 25166080 | tf_op jit(solution)/shard_map/while/body/scatter-add | solution.py:47
  316.4 0.7 compare_convert_fusion.5
  317.1 4.4 gather_fusion.1
  321.5 7.3 %broadcast_multiply_fusion.6 = f32[64,128,256]{2,1,0:T(8,128)} fusion(f32[64]{0:T(128)S(1)} %compare_convert_fusion.5, bf16[64,128,256]{2,1,0:T(8,128)(2,1)} %gather_fusion.1, bf16[384,128,128]{1,2,0:T(8,128)(2,1)} %get-tuple-element.328, s32[]{:T(128)S(6)} %select_n.40), kind=kOutput, calls=%fused_computation.11.clone.1 | convolution fusion | flops 538968064 | bytes 14680324 | tf_op jit(solution)/shard_map/while/body/kab,kaf->kbf/dot_general | solution.py:40
  328.7 12.4 %scatter_fusion.1 = f32[16,128,256]{2,1,0:T(8,128)S(1)} fusion(f32[16,128,256]{2,1,0:T(8,128)S(1)} %get-tuple-element.313, s32[64]{0:T(128)S(1)} %get-tuple-element.262, f32[64,128,256]{2,1,0:T(8,128)} %broadcast_multiply_fusion.6), kind=kCustom, calls=%fused_computation.3.clone.1 | custom fusion | flops 2097152 | bytes 25166080 | tf_op jit(solution)/shard_map/while/body/scatter-add | solution.py:47
  341.9 4.4 gather_fusion.1
  346.3 7.3 %broadcast_multiply_fusion.6 = f32[64,128,256]{2,1,0:T(8,128)} fusion(f32[64]{0:T(128)S(1)} %compare_convert_fusion.5, bf16[64,128,256]{2,1,0:T(8,128)(2,1)} %gather_fusion.1, bf16[384,128,128]{1,2,0:T(8,128)(2,1)} %get-tuple-element.328, s32[]{:T(128)S(6)} %select_n.40), kind=kOutput, calls=%fused_computation.11.clone.1 | convolution fusion | flops 538968064 | bytes 14680324 | tf_op jit(solution)/shard_map/while/body/kab,kaf->kbf/dot_general | solution.py:40
  353.6 12.4 %scatter_fusion.1 = f32[16,128,256]{2,1,0:T(8,128)S(1)} fusion(f32[16,128,256]{2,1,0:T(8,128)S(1)} %get-tuple-element.313, s32[64]{0:T(128)S(1)} %get-tuple-element.262, f32[64,128,256]{2,1,0:T(8,128)} %broadcast_multiply_fusion.6), kind=kCustom, calls=%fused_computation.3.clone.1 | custom fusion | flops 2097152 | bytes 25166080 | tf_op jit(solution)/shard_map/while/body/scatter-add | solution.py:47
  366.0 0.7 compare_convert_fusion.5
  366.8 4.4 gather_fusion.1
  371.1 7.3 %broadcast_multiply_fusion.6 = f32[64,128,256]{2,1,0:T(8,128)} fusion(f32[64]{0:T(128)S(1)} %compare_convert_fusion.5, bf16[64,128,256]{2,1,0:T(8,128)(2,1)} %gather_fusion.1, bf16[384,128,128]{1,2,0:T(8,128)(2,1)} %get-tuple-element.328, s32[]{:T(128)S(6)} %select_n.40), kind=kOutput, calls=%fused_computation.11.clone.1 | convolution fusion | flops 538968064 | bytes 14680324 | tf_op jit(solution)/shard_map/while/body/kab,kaf->kbf/dot_general | solution.py:40
  378.4 12.4 %scatter_fusion.1 = f32[16,128,256]{2,1,0:T(8,128)S(1)} fusion(f32[16,128,256]{2,1,0:T(8,128)S(1)} %get-tuple-element.313, s32[64]{0:T(128)S(1)} %get-tuple-element.262, f32[64,128,256]{2,1,0:T(8,128)} %broadcast_multiply_fusion.6), kind=kCustom, calls=%fused_computation.3.clone.1 | custom fusion | flops 2097152 | bytes 25166080 | tf_op jit(solution)/shard_map/while/body/scatter-add | solution.py:47
  390.9 1.1 convert_element_type.55
  392.6 88.6 %all-reduce = (f32[16,256]{1,0:T(8,128)S(1)}, f32[16]{0:T(128)S(1)}) all-reduce(f32[16,256]{1,0:T(8,128)S(1)} %fusion.6, f32[16]{0:T(128)S(1)} %convert_reduce_fusion), channel_id=1, replica_groups=mesh['row'=4,'col'=8] {'row','col'}, use_global_device_ids=true, to_apply=%region_9.10 | all-reduce | flops 4112 | bytes 32896 | tf_op jit(solution)/shard_map/psum | solution.py:115
  481.2 0.7 broadcast_divide_fusion
  481.9 1.9 convolution_bitcast_fusion
  483.8 1.9 convolution_convert_fusion
  485.7 124.0 %all-reduce.3.cloned.1.call-done = f32[256,256]{0,1:T(8,128)} async-done(((f32[256,256]{0,1:T(8,128)}), f32[256,256]{0,1:T(8,128)}) %all-reduce.3.cloned.1.call-update) | async-done | bytes 262160 | tf_op jit(solution)/shard_map/psum | solution.py:115
  609.8 1.0 broadcast_multiply_fusion.2
  610.7 0.8 copy.18
  (49 shorter events, 5.0 us)
Async XLA Ops:
  7.2 1.0 copy-start
  7.2 32.6 %all-gather.3.cloned.1.call-start = ((), (), s32[]{:S(2)}) async-start(), calls=%async_computation.2 | async-start | bytes 1310720 | tf_op jit(solution)/shard_map/all_gather | solution.py:71
  10.0 251.1 %reduce-scatter.3.cloned.1.call-start = ((), (), s32[]{:S(2)}) async-start(), calls=%async_computation.3 | async-start | bytes 2359296 | tf_op jit(solution)/shard_map/reduce_scatter | solution.py:86
  39.8 2.4 copy-start.1
  162.2 98.9 %copy-start.3 = (s32[512]{0:T(512)S(1)}, s32[512]{0:T(512)}, u32[]{:S(2)}) copy-start(s32[512]{0:T(512)} %param.20) | copy-start | bytes 6148
  162.2 98.9 %copy-start.4 = (bf16[512,256]{1,0:T(8,128)(2,1)S(1)}, bf16[512,256]{1,0:T(8,128)(2,1)}, u32[]{:S(2)}) copy-start(bf16[512,256]{1,0:T(8,128)(2,1)} %param.21) | copy-start | bytes 786436
  162.2 98.9 %copy-start.6 = (f32[16,256]{1,0:T(8,128)S(1)}, f32[16,256]{1,0:T(8,128)}, u32[]{:S(2)}) copy-start(f32[16,256]{1,0:T(8,128)} %param.19) | copy-start | bytes 49156
  166.1 125.2 %all-gather.5.cloned.1.call-start = ((), (), s32[]{:S(2)}) async-start(), calls=%async_computation.4 | async-start | bytes 2359296 | tf_op jit(solution)/shard_map/all_gather | solution.py:90
  263.5 218.4 %reduce-scatter.5.cloned.1.call-start = ((), (), s32[]{:S(2)}) async-start(), calls=%async_computation.5 | async-start | bytes 1310720 | tf_op jit(solution)/shard_map/reduce_scatter | solution.py:102
  390.9 1.3 copy-start.5
  390.9 92.9 %copy-start.2 = (bf16[256,256]{1,0:T(8,128)(2,1)S(1)}, bf16[256,256]{1,0:T(8,128)(2,1)}, u32[]{:S(2)}) copy-start(bf16[256,256]{1,0:T(8,128)(2,1)} %param.14) | copy-start | bytes 393220
  392.0 217.7 %all-reduce.3.cloned.1.call-start = ((), (), s32[]{:S(2)}) async-start(), calls=%async_computation.6 | async-start | bytes 524288 | tf_op jit(solution)/shard_map/psum | solution.py:115
Sparse Core Ops, SparseCore 0:
  10.4 29.3 all-gather.2
  166.2 94.8 reduce-scatter.2
  263.6 27.7 all-gather.4
  392.1 76.0 reduce-scatter.4
  483.9 125.7 all-reduce.2
where the time goes:
time: 620 us; the launch traced here: 618 us
  waiting for transfers between devices  258 us (42%)
  other arithmetic  141 us (23%)
  blocking collectives  88.6 us (14%)
  matrix products  66.5 us (11%)
  local copies, waits for them, and re-layouts  49.6 us (8%)
  between operations  14.5 us (2%)
    scatter-add x8, other arithmetic, one_group(): return totals.at[targets].add(products * slot_mask[:, None, None])  127 us
    psum x1, waiting for transfers between devices, per_device(): lax.psum((weight_part, part_terms, part_sizes), ('row', 'col'))  124 us
    reduce_scatter x1, waiting for transfers between devices, per_device(): lax.psum_scatter(partial_rows.astype(jnp.bfloat16), 'col', scatter_dimens...  95 us
    psum x1, blocking collectives, per_device(): lax.psum((weight_part, part_terms, part_sizes), ('row', 'col'))  88.6 us
    dot_general x4, matrix products, one_group(): jnp.einsum('kab,kbf->kaf', values_here, panel_blocks[cols_here], preferre...  29.1 us
    dot_general x4, matrix products, one_group(): jnp.einsum('kab,kaf->kbf', values_here, panel_blocks[rows_here], preferre...  29 us
    all_gather x1, waiting for transfers between devices, per_device(): panels = lax.all_gather(hidden, 'row', axis=0, tiled=True)  27.7 us
    unnamed x16, local copies, waits for them, and re-layouts  18.4 us
  transfers between devices with their start and end apart: 5, of which 4 were waited for; matrix products, arithmetic and copies ran while one was open for 3% of the time, Pallas kernels for 0%

commit v1 on v0

v1 whole, which is shorter than its diff:
```python
import functools

import jax
import jax.numpy as jnp
from jax import lax
from jax.experimental import pallas as pl
from jax.experimental.pallas import tpu as pltpu
from jax.sharding import PartitionSpec as P

BLOCK = 128
GROUP = 16
BUFFERS = 8
HEAVY = 16
MIB = 1 << 20


def bits_of(count):
    return [1 << b for b in range(count.bit_length() - 1)]


def halving_order(count):
    if count == 1:
        return [0]
    evens = [2 * k for k in halving_order(count // 2)]
    return [k ^ 1 for k in evens] + evens


def build_kernel(
    live_ref, rows_ref, cols_ref, place_row_ref, place_col_ref, slots_ref, tile_ref, buf, total, counts, sems
):
    live = live_ref[0]
    groups = (live + GROUP - 1) // GROUP
    col_blocks = tile_ref.shape[1] // BLOCK

    def fetch(group, slot):
        return pltpu.make_async_copy(
            slots_ref.at[pl.ds(group * GROUP, GROUP)], buf.at[slot], sems.at[slot]
        )

    for b in range(BUFFERS):
        @pl.when(b < groups)
        def _():
            fetch(b, b).start()

    zeros = jnp.zeros((BLOCK, tile_ref.shape[1]), tile_ref.dtype)

    @pl.loop(0, tile_ref.shape[0] // BLOCK)
    def _(r):
        tile_ref[pl.ds(pl.multiple_of(r * BLOCK, BLOCK), BLOCK), :] = zeros

    def place(index):
        top = pl.multiple_of(rows_ref[index] * BLOCK, BLOCK)
        left = pl.multiple_of(cols_ref[index] * BLOCK, BLOCK)
        return pl.ds(top, BLOCK), pl.ds(left, BLOCK)

    @pl.loop(0, groups)
    def _(group):
        slot = lax.rem(group, BUFFERS)
        fetch(group, slot).wait()

        @pl.loop(0, jnp.minimum(GROUP, live - group * GROUP))
        def _(s):
            at = place(group * GROUP + s)
            tile_ref[at] += buf[slot, s]

        @pl.when(group + BUFFERS < groups)
        def _():
            fetch(group + BUFFERS, slot).start()

    slot_total = place_row_ref.shape[1]
    live_here = lax.broadcasted_iota(jnp.int32, (1, slot_total), 1) < live
    same = jnp.where(
        (place_row_ref[...] == place_col_ref[...]) & live_here, 1.0, 0.0
    )
    most = jnp.max(jnp.sum(same, axis=1, keepdims=True))

    @pl.when(most > HEAVY)
    def _():
        @pl.loop(0, counts.shape[0])
        def _(p):
            counts[p] = 0

        @pl.loop(0, live)
        def _(index):
            p = rows_ref[index] * col_blocks + cols_ref[index]
            counts[p] = counts[p] + 1

        @pl.loop(0, live)
        def _(index):
            p = rows_ref[index] * col_blocks + cols_ref[index]

            @pl.when(counts[p] > HEAVY)
            def _():
                counts[p] = 0
                total[...] = jnp.zeros_like(total)

                @pl.loop(index, live)
                def _(other):
                    @pl.when(rows_ref[other] * col_blocks + cols_ref[other] == p)
                    def _():
                        copy = pltpu.make_async_copy(
                            slots_ref.at[pl.ds(other, 1)], buf.at[0, pl.ds(0, 1)], sems.at[0]
                        )
                        copy.start()
                        copy.wait()
                        total[...] += buf[0, 0].astype(jnp.float32)

                tile_ref[place(index)] = total[...].astype(tile_ref.dtype)


def build_tile(slots, rows, cols, live, row_blocks, col_blocks):
    places = rows * col_blocks + cols
    smem = pl.BlockSpec(memory_space=pltpu.SMEM)
    vmem = pl.BlockSpec(memory_space=pltpu.VMEM)
    slot_total = slots.shape[0]
    return pl.pallas_call(
        build_kernel,
        out_shape=pltpu.VMEM((row_blocks * BLOCK, col_blocks * BLOCK), jnp.bfloat16),
        in_specs=[smem, smem, smem, vmem, vmem, pl.BlockSpec(memory_space=pl.ANY)],
        out_specs=vmem,
        scratch_shapes=[
            pltpu.VMEM((BUFFERS, GROUP, BLOCK, BLOCK), jnp.bfloat16),
            pltpu.VMEM((BLOCK, BLOCK), jnp.float32),
            pltpu.SMEM((row_blocks * col_blocks,), jnp.int32),
            pltpu.SemaphoreType.DMA((BUFFERS,)),
        ],
        compiler_params=pltpu.CompilerParams(vmem_limit_bytes=12 * MIB),
        cost_estimate=pl.CostEstimate(flops=0, bytes_accessed=20 * MIB, transcendentals=0),
        name="build_tile",
    )(live, rows, cols, places[None, :], places[:, None], slots)


def forward_kernel(order, *refs):
    at_ref, tile_ref, weight_ref = refs[:3]
    chunks = 2
    feature_refs = refs[3 : -1 - 2 * chunks]
    send_refs, rest_refs = refs[-1 - 2 * chunks : -1 - chunks], refs[-1 - chunks : -1]
    hidden = refs[-1]
    own_row, own_col = at_ref[0], at_ref[1]
    share = feature_refs[0].shape[0]
    for r, feature_ref in enumerate(feature_refs):
        at = pl.ds(pl.multiple_of((own_row ^ r) * share, share), share)
        hidden[at, :] = jnp.dot(
            feature_ref[...], weight_ref[...], preferred_element_type=jnp.float32
        ).astype(jnp.bfloat16)
    half = len(order) // 2
    width = hidden.shape[1] // chunks
    step = share // 2
    for t, k in enumerate(order):
        base = (own_col ^ k) * share
        into = send_refs if t < half else rest_refs
        for m in range(0, share, step):
            at = pl.ds(pl.multiple_of(base + m, step), step)
            product = jnp.dot(tile_ref[at, :], hidden[...], preferred_element_type=jnp.float32)
            product = product.astype(jnp.bfloat16)
            to = pl.ds((t % half) * share + m, step)
            for c in range(chunks):
                into[c][to, :] = product[:, c * width : (c + 1) * width]


def forward(at, tile, weight, features, order):
    share, width = features[0].shape
    half = len(order) // 2
    part = pltpu.VMEM((half * share, width // 2), jnp.bfloat16)
    vmem = pl.BlockSpec(memory_space=pltpu.VMEM)
    smem = pl.BlockSpec(memory_space=pltpu.SMEM)
    return pl.pallas_call(
        functools.partial(forward_kernel, order),
        out_shape=[part] * 4,
        in_specs=[smem] + [vmem] * (2 + len(features)),
        out_specs=[vmem] * 4,
        scratch_shapes=[pltpu.VMEM((len(features) * share, width), jnp.bfloat16)],
        compiler_params=pltpu.CompilerParams(vmem_limit_bytes=12 * MIB),
        cost_estimate=pl.CostEstimate(
            flops=2 * tile.shape[0] * tile.shape[1] * width, bytes_accessed=0, transcendentals=0
        ),
        name="forward",
    )(at, tile, weight, *features)


def backward_kernel(orders, row_count, *refs):
    at_ref, tile_ref = refs[:2]
    grad_refs = refs[2 : 2 + len(orders)]
    feature_refs = refs[2 + len(orders) : 2 + len(orders) + row_count]
    part_refs = refs[-2 - row_count : -2]
    weight_ref, turned = refs[-2:]
    own_row, own_col = at_ref[0], at_ref[1]
    share = feature_refs[0].shape[0]
    for order, grad_ref in zip(orders, grad_refs):
        for t, k in enumerate(order):
            at = pl.ds(pl.multiple_of((own_col ^ k) * share, share), share)
            turned[:, at] = grad_ref[t * share : (t + 1) * share, :].T
    total = None
    for r in range(row_count):
        at = pl.ds(pl.multiple_of((own_row ^ r) * share, share), share)
        product = jnp.dot(turned[...], tile_ref[:, at], preferred_element_type=jnp.float32)
        product = product.astype(jnp.bfloat16)
        part_refs[r][...] = product
        term = jnp.dot(product, feature_refs[r][...], preferred_element_type=jnp.float32)
        total = term if total is None else total + term
    weight_ref[...] = total


def backward(at, tile, grads, orders, features):
    share, width = features[0].shape
    chunk = grads[0].shape[1]
    rows = len(features)
    vmem = pl.BlockSpec(memory_space=pltpu.VMEM)
    smem = pl.BlockSpec(memory_space=pltpu.SMEM)
    return pl.pallas_call(
        functools.partial(backward_kernel, orders, rows),
        out_shape=[pltpu.VMEM((chunk, share), jnp.bfloat16)] * rows
        + [pltpu.VMEM((chunk, width), jnp.float32)],
        in_specs=[smem] + [vmem] * (1 + len(grads) + rows),
        out_specs=[vmem] * (rows + 1),
        scratch_shapes=[pltpu.VMEM((chunk, tile.shape[0]), jnp.bfloat16)],
        compiler_params=pltpu.CompilerParams(vmem_limit_bytes=12 * MIB),
        cost_estimate=pl.CostEstimate(
            flops=4 * tile.shape[0] * tile.shape[1] * chunk, bytes_accessed=0, transcendentals=0
        ),
        name="backward",
    )(at, tile, *grads, *features)


def silu_slope(values):
    sig = jax.nn.sigmoid(values)
    return sig * (1.0 + values * (1.0 - sig))


def swap(values, axis, mask, count):
    return lax.ppermute(values, axis, [(d, d ^ mask) for d in range(count)])


def dense_device(
    row_count,
    col_count,
    features,
    weight,
    adjacency,
    block_rows,
    block_cols,
    live_blocks,
    part_gains,
    partition,
    cotangent,
):
    share, width = features.shape
    chunk = width // 2
    at = jnp.stack([lax.axis_index("row"), lax.axis_index("col")]).astype(jnp.int32)
    gathered = [features] + [swap(features, "row", r, row_count) for r in range(1, row_count)]
    tile = build_tile(
        adjacency[0, 0],
        block_rows[0, 0],
        block_cols[0, 0],
        live_blocks[0],
        share * col_count // BLOCK,
        share * row_count // BLOCK,
    )
    member = (
        partition[:, None] == jnp.arange(part_gains.shape[0], dtype=jnp.int32)[None, :]
    ).astype(jnp.float32)
    row_gains = jnp.dot(member, part_gains, precision=lax.Precision.HIGHEST)
    upstream = cotangent.astype(jnp.float32) * row_gains

    order = halving_order(col_count)
    col_bits = bits_of(col_count)
    *parts, = forward(at, tile, weight, gathered, order)
    sends, rests = parts[:2], parts[2:]

    def wide(values):
        return values.astype(jnp.float32)

    summed, hidden_parts, weight_parts = [], [], []
    for c in range(2):
        arrived = [swap(sends[c], "col", col_bits[0], col_count)]
        rest = rests[c]
        for bit in col_bits[1:]:
            first = sum(wide(a[-rest.shape[0] :][: rest.shape[0] // 2]) for a in arrived)
            half = rest.shape[0] // 2
            out = (wide(rest[:half]) + first).astype(jnp.bfloat16)
            arrived.append(swap(out, "col", bit, col_count))
            rest = rest[half:]
        total = wide(rest)
        for a in arrived:
            total = total + wide(a[-share:])
        summed.append(total)
        grad = (upstream[:, c * chunk : (c + 1) * chunk] * silu_slope(total)).astype(jnp.bfloat16)
        held, orders = [grad], [[0]]
        for bit in reversed(col_bits[1:]):
            sent = held[0] if len(held) == 1 else jnp.concatenate(held[::-1], axis=0)
            held.append(swap(sent, "col", bit, col_count))
            orders.append([k ^ bit for o in orders[::-1] for k in o])
        bit = col_bits[0]
        for h, o in list(zip(held, orders)):
            held.append(swap(h, "col", bit, col_count))
            orders.append([k ^ bit for k in o])
        *hidden_part, weight_part = backward(at, tile, held, orders, gathered)
        for r in range(1, row_count):
            hidden_part[r] = swap(hidden_part[r], "row", r, row_count)
        hidden_parts.append(hidden_part)
        weight_parts.append(weight_part)

    summed = jnp.concatenate(summed, axis=1)
    activated = jax.nn.silu(summed)
    layer_out = (activated * row_gains).astype(jnp.bfloat16)

    hidden_grad = jnp.concatenate([sum(wide(p) for p in ps) for ps in hidden_parts], axis=0)
    feature_grad = lax.dot_general(
        hidden_grad.astype(jnp.bfloat16),
        weight,
        (((0,), (1,)), ((), ())),
        preferred_element_type=jnp.float32,
    ).astype(jnp.bfloat16)

    part_terms = jnp.dot(
        member.T, wide(cotangent) * activated, precision=lax.Precision.HIGHEST
    )
    part_sizes = jnp.broadcast_to(jnp.sum(member, axis=0)[:, None], (member.shape[1], width))
    totals = jnp.concatenate(weight_parts + [part_terms, part_sizes], axis=0)
    for bit in col_bits[1:] + col_bits[:1]:
        totals = totals + swap(totals, "col", bit, col_count)
    for bit in bits_of(row_count):
        totals = totals + swap(totals, "row", bit, row_count)
    total_nodes = share * row_count * col_count
    weight_grad = totals[:width].T / jnp.sqrt(jnp.float32(total_nodes))
    part_count = member.shape[1]
    gain_grad = totals[width : width + part_count] / jnp.sqrt(totals[width + part_count :])
    return (layer_out, feature_grad, weight_grad, gain_grad)


def slot_sum(tile_values, row_index, col_index, live_count, panels, out_blocks, forward_way):
    slot_count = tile_values.shape[0]
    feature_width = panels.shape[1]
    panel_blocks = panels.reshape(-1, BLOCK, feature_width)

    def one_slot(slot, totals):
        values = lax.dynamic_index_in_dim(tile_values, slot, 0, keepdims=False)
        source, target = col_index[slot], row_index[slot]
        if not forward_way:
            values, source, target = values.T, target, source
        panel = lax.dynamic_index_in_dim(panel_blocks, source, 0, keepdims=False)
        product = jnp.dot(values, panel, preferred_element_type=jnp.float32)
        return totals.at[target].add(product)

    start = jnp.zeros((out_blocks, BLOCK, feature_width), jnp.float32)
    totals = lax.fori_loop(0, jnp.minimum(live_count, slot_count), one_slot, start)
    return totals.reshape(out_blocks * BLOCK, feature_width)


def slot_device(
    features,
    weight,
    adjacency,
    block_rows,
    block_cols,
    live_blocks,
    part_gains,
    partition,
    cotangent,
):
    node_count = features.shape[0]
    row_total = node_count * lax.axis_size("col") // BLOCK
    col_total = node_count * lax.axis_size("row") // BLOCK
    slots = (adjacency[0, 0], block_rows[0, 0], block_cols[0, 0], live_blocks[0, 0])
    hidden = jnp.dot(features, weight, preferred_element_type=jnp.float32).astype(jnp.bfloat16)
    panels = lax.all_gather(hidden, "row", axis=0, tiled=True)
    member = (
        partition[:, None] == jnp.arange(part_gains.shape[0], dtype=jnp.int32)[None, :]
    ).astype(jnp.float32)
    row_gains = jnp.dot(member, part_gains, precision=lax.Precision.HIGHEST)
    upstream = cotangent.astype(jnp.float32) * row_gains
    partial_rows = slot_sum(*slots, panels, row_total, True)
    summed = lax.psum_scatter(
        partial_rows.astype(jnp.bfloat16), "col", scatter_dimension=0, tiled=True
    ).astype(jnp.float32)
    local_grad = (upstream * silu_slope(summed)).astype(jnp.bfloat16)
    agg_grad = lax.all_gather(local_grad, "col", axis=0, tiled=True)
    activated = jax.nn.silu(summed)
    layer_out = (activated * row_gains).astype(jnp.bfloat16)
    partial_cols = slot_sum(*slots, agg_grad, col_total, False)
    hidden_grad = lax.psum_scatter(
        partial_cols.astype(jnp.bfloat16), "row", scatter_dimension=0, tiled=True
    )
    feature_grad = lax.dot_general(
        hidden_grad, weight, (((1,), (1,)), ((), ())), preferred_element_type=jnp.float32
    ).astype(jnp.bfloat16)
    weight_part = lax.dot_general(
        features, hidden_grad, (((0,), (0,)), ((), ())), preferred_element_type=jnp.float32
    )
    part_terms = jnp.dot(
        member.T, cotangent.astype(jnp.float32) * activated, precision=lax.Precision.HIGHEST
    )
    part_sizes = jnp.sum(member, axis=0)
    weight_total, part_total, size_total = lax.psum(
        (weight_part, part_terms, part_sizes), ("row", "col")
    )
    total_nodes = node_count * lax.axis_size("row") * lax.axis_size("col")
    weight_grad = weight_total / jnp.sqrt(jnp.float32(total_nodes))
    gain_grad = part_total / jnp.sqrt(size_total)[:, None]
    return (layer_out, feature_grad, weight_grad, gain_grad)


def solution(mesh):
    row_count, col_count = mesh.shape["row"], mesh.shape["col"]

    def per_device(features, *others):
        tile_bytes = 2 * features.shape[0] ** 2 * row_count * col_count
        if tile_bytes <= 20 * MIB:
            return dense_device(row_count, col_count, features, *others)
        return slot_device(features, *others)

    in_specs = (
        P(("row", "col"), None),
        P(),
        P("row", "col", None, None, None),
        P("row", "col", None),
        P("row", "col", None),
        P("row", "col"),
        P(),
        P(("row", "col")),
        P(("row", "col"), None),
    )
    out_specs = (P(("row", "col"), None), P(("row", "col"), None), P(), P())
    return jax.shard_map(
        per_device, mesh=mesh, in_specs=in_specs, out_specs=out_specs, check_vma=False
    )
```

time: 620 us -> 141 us (0.23)
  waiting for transfers between devices: 258 us -> 69.3 us
  other arithmetic: 141 us -> 3.51 us
  blocking collectives: 88.6 us -> 0 us
  matrix products: 66.5 us -> 1.77 us
  local copies, waits for them, and re-layouts: 49.6 us -> 5.65 us
  starting transfers between devices: 0.21 us -> 38.8 us
  Pallas kernels: 0 us -> 19.8 us
  between operations: 14.5 us -> 1.54 us
    scatter-add x8 -> x0, other arithmetic: 127 us -> none  [one_group(): return totals.at[targets].add(products * slot_mask[:, None, None])]
    psum x1 -> x0, waiting for transfers between devices: 124 us -> none  [per_device(): lax.psum((weight_part, part_terms, part_sizes), ('row', 'col'))]
    reduce_scatter x2 -> x0, waiting for transfers between devices: 95 us -> none  [the longest x1 95 us: per_device(): lax.psum_scatter(partial_rows.astype(jnp.bfloat16), 'col', scatter_dimens...]
    psum x1 -> x0, blocking collectives: 88.6 us -> none  [per_device(): lax.psum((weight_part, part_terms, part_sizes), ('row', 'col'))]
    ppermute x0 -> x30, waiting for transfers between devices: none -> 69.3 us  [swap(): return lax.ppermute(values, axis, [(d, d ^ mask) for d in range(count)])]
    dot_general x13 -> x3, matrix products: 66.5 us -> 1.77 us  [the longest x1 0.97 us: dense_device(): lax.dot_general(hidden_grad.astype(jnp.bfloat16), weight, (((0,), (1,)),...]
    all_gather x2 -> x0, waiting for transfers between devices: 38.9 us -> none  [the longest x1 27.7 us: per_device(): panels = lax.all_gather(hidden, 'row', axis=0, tiled=True)]
    ppermute x0 -> x30, starting transfers between devices: none -> 38.8 us  [swap(): return lax.ppermute(values, axis, [(d, d ^ mask) for d in range(count)])]
  transfers between devices with their start and end apart: 5 -> 30, of which waited for: 4 -> 15; matrix products, arithmetic and copies ran while one was open for 3% -> 3% of each run, Pallas kernels for 0% -> 7%
where the time goes in v1:
time: 141 us; the launch traced here: 140 us
  waiting for transfers between devices  69.3 us (49%)
  starting transfers between devices  38.8 us (28%)
  Pallas kernels  19.8 us (14%)
  local copies, waits for them, and re-layouts  5.65 us (4%)
  other arithmetic  3.51 us (2%)
  matrix products  1.77 us (1%)
  between operations  1.54 us (1%)
    ppermute x30, waiting for transfers between devices, swap(): return lax.ppermute(values, axis, [(d, d ^ mask) for d in range(count)])  69.3 us
    ppermute x30, starting transfers between devices, swap(): return lax.ppermute(values, axis, [(d, d ^ mask) for d in range(count)])  38.8 us
    pallas_call x2, Pallas kernels, backward(): pl.pallas_call(functools.partial(backward_kernel, orders, rows), out_shap...  7.8 us
    pallas_call x1, Pallas kernels, build_tile(): pl.pallas_call(build_kernel, out_shape=pltpu.VMEM((row_blocks * BLOCK, co...  6.4 us
    pallas_call x1, Pallas kernels, forward(): pl.pallas_call(functools.partial(forward_kernel, order), out_shape=[part]...  5.58 us
    unnamed x13, local copies, waits for them, and re-layouts  5.44 us
  transfers between devices with their start and end apart: 30, of which 15 were waited for; matrix products, arithmetic and copies ran while one was open for 3% of the time, Pallas kernels for 7%

profile of v1, /device:TPU:0, one launch (start us, length us, event | category | flops | bytes accessed | tf_op | source)
XLA Modules:
  0.0 140.4 jit_solution(6544575880584625901)
XLA Ops:
  0.7 3.0 %collective-permute-start = (bf16[512,256]{1,0:T(8,128)(2,1)}, bf16[512,256]{1,0:T(8,128)(2,1)S(1)}, u32[]{:S(2)}, u32[]{:S(2)}) collective-permute-start(bf16[512,256]{1,0:T(8,128)(2,1)} %refs_8_.3), channel_id=1, source_target_pairs={{0,8},{8,0},{16,24},{24,16},{1,9},{9,1},{17,25},{25,17},{2,10},{10... | collective-permute-start | bytes 786440 | tf_op jit(solution)/shard_map/ppermute | solution.py:231
  3.7 1.5 %collective-permute-start.1 = (bf16[512,256]{1,0:T(8,128)(2,1)}, bf16[512,256]{1,0:T(8,128)(2,1)S(1)}, u32[]{:S(2)}, u32[]{:S(2)}) collective-permute-start(bf16[512,256]{1,0:T(8,128)(2,1)} %refs_8_.3), channel_id=1, source_target_pairs={{0,16},{8,24},{16,0},{24,8},{1,17},{9,25},{17,1},{25,9},{2,18},{10... | collective-permute-start | bytes 786440 | tf_op jit(solution)/shard_map/ppermute | solution.py:231
  5.9 0.7 fusion.12
  6.7 4.6 %copy-done.1 = bf16[1,1,384,128,128]{4,3,2,1,0:T(8,128)(2,1)S(1)} copy-done((bf16[1,1,384,128,128]{4,3,2,1,0:T(8,128)(2,1)S(1)}, bf16[1,1,384,128,128]{4,3,2,1,0:T(8,128)(2,1)}, u32[]{:S(2)}) %copy-start.1) | copy-done | bytes 12582936
  11.3 6.4 %build_tile.1.refs_1_ = bf16[4096,2048]{1,0:T(8,128)(2,1)S(1)} custom-call(s32[1]{0:T(128)} %bitcast.12.live_ref, s32[384]{0:T(512)S(1)} %get-tuple-element.52.rows_ref, s32[384]{0:T(512)S(1)} %get-tuple-element.53.cols_ref, s32[1,384]{1,0:T(1,128)S(1)} %get-tuple-element.51.place_row_ref, s32[384,1]{1,0:T(8,128)S(1)} %copy.16.place_col_ref, ...), custom_call_target="tpu_custom_call" | custom-call | bytes 20971520 | tf_op jit(solution)/shard_map/build_tile/pallas_call | solution.py:116
  17.9 5.6 %forward.1 = (bf16[2048,128]{1,0:T(8,128)(2,1)S(1)}, bf16[2048,128]{1,0:T(8,128)(2,1)S(1)}, bf16[2048,128]{1,0:T(8,128)(2,1)S(1)}, bf16[2048,128]{1,0:T(8,128)(2,1)S(1)}) custom-call(s32[2]{0:T(128)S(1)} %pad_add_fusion.refs_0_, bf16[4096,2048]{1,0:T(8,128)(2,1)S(1)} %build_tile.1.refs_1_, bf16[256,256]{1,0:T(8,128)(2,1)S(1)} %copy-done.3, ...), custom_call_target="tpu_custom_call" | custom-call | flops 4294967296 | tf_op jit(solution)/shard_map/forward/pallas_call | solution.py:167
  23.4 2.0 %collective-permute-start.3 = (bf16[2048,128]{1,0:T(8,128)(2,1)S(1)}, bf16[2048,128]{1,0:T(8,128)(2,1)S(1)}, u32[]{:S(2)}, u32[]{:S(2)}) collective-permute-start(bf16[2048,128]{1,0:T(8,128)(2,1)S(1)} %get-tuple-element.19), channel_id=1, source_target_pairs={{0,1},{1,0},{2,3},{3,2},{4,5},{5,4},{6,7},{7,6},{8,9},{9,8},{10,11... | collective-permute-start | bytes 1572872 | tf_op jit(solution)/shard_map/ppermute | solution.py:231
  25.5 1.5 %collective-permute-done.3 = bf16[2048,128]{1,0:T(8,128)(2,1)S(1)} collective-permute-done((bf16[2048,128]{1,0:T(8,128)(2,1)S(1)}, bf16[2048,128]{1,0:T(8,128)(2,1)S(1)}, u32[]{:S(2)}, u32[]{:S(2)}) %collective-permute-start.3) | collective-permute-done | bytes 524320 | tf_op jit(solution)/shard_map/ppermute | solution.py:231
  27.0 1.6 %collective-permute-start.4 = (bf16[1024,128]{1,0:T(8,128)(2,1)S(1)}, bf16[1024,128]{1,0:T(8,128)(2,1)S(1)}, u32[]{:S(2)}, u32[]{:S(2)}) collective-permute-start(bf16[1024,128]{1,0:T(8,128)(2,1)S(1)} %add_convert_fusion.1), channel_id=1, source_target_pairs={{0,2},{1,3},{2,0},{3,1},{4,6},{5,7},{6,4},{7,5},{8,10},{9,11},{10,... | collective-permute-start | bytes 786440 | tf_op jit(solution)/shard_map/ppermute | solution.py:231
  28.7 0.7 collective-permute-start.7
  29.4 6.9 %collective-permute-done.4 = bf16[1024,128]{1,0:T(8,128)(2,1)S(1)} collective-permute-done((bf16[1024,128]{1,0:T(8,128)(2,1)S(1)}, bf16[1024,128]{1,0:T(8,128)(2,1)S(1)}, u32[]{:S(2)}, u32[]{:S(2)}) %collective-permute-start.4) | collective-permute-done | bytes 262176 | tf_op jit(solution)/shard_map/ppermute | solution.py:231
  36.3 4.2 %collective-permute-start.5 = (bf16[512,128]{1,0:T(8,128)(2,1)S(1)}, bf16[512,128]{1,0:T(8,128)(2,1)S(1)}, u32[]{:S(2)}, u32[]{:S(2)}) collective-permute-start(bf16[512,128]{1,0:T(8,128)(2,1)S(1)} %add_convert_fusion.5), channel_id=1, source_target_pairs={{0,4},{1,5},{2,6},{3,7},{4,0},{5,1},{6,2},{7,3},{8,12},{9,13},{10,... | collective-permute-start | bytes 393224 | tf_op jit(solution)/shard_map/ppermute | solution.py:231
  40.5 3.6 %collective-permute-done.7 = bf16[1024,128]{1,0:T(8,128)(2,1)S(1)} collective-permute-done((bf16[1024,128]{1,0:T(8,128)(2,1)S(1)}, bf16[1024,128]{1,0:T(8,128)(2,1)S(1)}, u32[]{:S(2)}, u32[]{:S(2)}) %collective-permute-start.7) | collective-permute-done | bytes 262176 | tf_op jit(solution)/shard_map/ppermute | solution.py:231
  44.2 2.0 %collective-permute-start.8 = (bf16[512,128]{1,0:T(8,128)(2,1)S(1)}, bf16[512,128]{1,0:T(8,128)(2,1)S(1)}, u32[]{:S(2)}, u32[]{:S(2)}) collective-permute-start(bf16[512,128]{1,0:T(8,128)(2,1)S(1)} %add_convert_fusion.4), channel_id=1, source_target_pairs={{0,4},{1,5},{2,6},{3,7},{4,0},{5,1},{6,2},{7,3},{8,12},{9,13},{10,... | collective-permute-start | bytes 393224 | tf_op jit(solution)/shard_map/ppermute | solution.py:231
  46.2 0.4 convert_multiply_fusion.1
  46.6 6.5 %collective-permute-done.8 = bf16[512,128]{1,0:T(8,128)(2,1)S(1)} collective-permute-done((bf16[512,128]{1,0:T(8,128)(2,1)S(1)}, bf16[512,128]{1,0:T(8,128)(2,1)S(1)}, u32[]{:S(2)}, u32[]{:S(2)}) %collective-permute-start.8) | collective-permute-done | bytes 131104 | tf_op jit(solution)/shard_map/ppermute | solution.py:231
  53.1 0.3 fusion.3
  53.5 7.3 %collective-permute-done.17.refs_3_ = bf16[512,128]{1,0:T(8,128)(2,1)S(1)} collective-permute-done((bf16[512,128]{1,0:T(8,128)(2,1)S(1)}, bf16[512,128]{1,0:T(8,128)(2,1)S(1)}, u32[]{:S(2)}, u32[]{:S(2)}) %collective-permute-start.17) | collective-permute-done | bytes 131104 | tf_op jit(solution)/shard_map/ppermute | solution.py:231
  60.9 3.1 %collective-permute-start.9 = (bf16[512,128]{1,0:T(8,128)(2,1)S(1)}, bf16[512,128]{1,0:T(8,128)(2,1)S(1)}, u32[]{:S(2)}, u32[]{:S(2)}) collective-permute-start(bf16[512,128]{1,0:T(8,128)(2,1)S(1)} %get-tuple-element.44.refs_2_), channel_id=1, source_target_pairs={{0,4},{1,5},{2,6},{3,7},{4,0},{5,1},{6,2},{7,3},{8,12},{9,13},{10,... | collective-permute-start | bytes 393224 | tf_op jit(solution)/shard_map/ppermute | solution.py:231
  64.0 5.7 %collective-permute-done.9.refs_3_ = bf16[512,128]{1,0:T(8,128)(2,1)S(1)} collective-permute-done((bf16[512,128]{1,0:T(8,128)(2,1)S(1)}, bf16[512,128]{1,0:T(8,128)(2,1)S(1)}, u32[]{:S(2)}, u32[]{:S(2)}) %collective-permute-start.9) | collective-permute-done | bytes 131104 | tf_op jit(solution)/shard_map/ppermute | solution.py:231
  69.8 3.1 %collective-permute-start.10 = (bf16[1024,128]{1,0:T(8,128)(2,1)S(1)}, bf16[1024,128]{1,0:T(8,128)(2,1)S(1)}, u32[]{:S(2)}, u32[]{:S(2)}) collective-permute-start(bf16[1024,128]{1,0:T(8,128)(2,1)S(1)} %pad_maximum_fusion.1), channel_id=1, source_target_pairs={{0,2},{1,3},{2,0},{3,1},{4,6},{5,7},{6,4},{7,5},{8,10},{9,11},{10,... | collective-permute-start | bytes 786440 | tf_op jit(solution)/shard_map/ppermute | solution.py:231
  73.1 0.5 collective-permute-start.19
  73.6 0.4 collective-permute-start.20
  74.1 0.4 fusion
  74.6 0.3 collective-permute-start.12
  74.9 3.3 %collective-permute-done.10.refs_4_ = bf16[1024,128]{1,0:T(8,128)(2,1)S(1)} collective-permute-done((bf16[1024,128]{1,0:T(8,128)(2,1)S(1)}, bf16[1024,128]{1,0:T(8,128)(2,1)S(1)}, u32[]{:S(2)}, u32[]{:S(2)}) %collective-permute-start.10) | collective-permute-done | bytes 262176 | tf_op jit(solution)/shard_map/ppermute | solution.py:231
  78.3 3.9 %backward.3 = (bf16[128,512]{1,0:T(8,128)(2,1)S(1)}, bf16[128,512]{1,0:T(8,128)(2,1)S(1)}, bf16[128,512]{1,0:T(8,128)(2,1)S(1)}, bf16[128,512]{1,0:T(8,128)(2,1)S(1)}, f32[128,256]{1,0:T(8,128)S(1)}) custom-call(s32[2]{0:T(128)S(1)} %pad_add_fusion.refs_0_, bf16[4096,2048]{1,0:T(8,128)(2,1)S(1)} %build_tile.1.refs_1_, ...), custom_call_target="tpu_custom_call" | custom-call | flops 4294967296 | tf_op jit(solution)/shard_map/backward/pallas_call | solution.py:210
  82.2 3.9 %backward.2 = (bf16[128,512]{1,0:T(8,128)(2,1)S(1)}, bf16[128,512]{1,0:T(8,128)(2,1)S(1)}, bf16[128,512]{1,0:T(8,128)(2,1)S(1)}, bf16[128,512]{1,0:T(8,128)(2,1)S(1)}, f32[128,256]{1,0:T(8,128)S(1)}) custom-call(s32[2]{0:T(128)S(1)} %pad_add_fusion.refs_0_, bf16[4096,2048]{1,0:T(8,128)(2,1)S(1)} %build_tile.1.refs_1_, ...), custom_call_target="tpu_custom_call" | custom-call | flops 4294967296 | tf_op jit(solution)/shard_map/backward/pallas_call | solution.py:210
  86.2 1.8 %collective-permute-start.25 = (f32[288,256]{1,0:T(8,128)S(1)}, f32[288,256]{1,0:T(8,128)S(1)}, u32[]{:S(2)}, u32[]{:S(2)}) collective-permute-start(f32[288,256]{1,0:T(8,128)S(1)} %maximum_maximum_fusion), channel_id=1, source_target_pairs={{0,2},{1,3},{2,0},{3,1},{4,6},{5,7},{6,4},{7,5},{8,10},{9,11},{10,... | collective-permute-start | bytes 884744 | tf_op jit(solution)/shard_map/ppermute | solution.py:231
  88.0 7.7 %collective-permute-done.25 = f32[288,256]{1,0:T(8,128)S(1)} collective-permute-done((f32[288,256]{1,0:T(8,128)S(1)}, f32[288,256]{1,0:T(8,128)S(1)}, u32[]{:S(2)}, u32[]{:S(2)}) %collective-permute-start.25) | collective-permute-done | bytes 294944 | tf_op jit(solution)/shard_map/ppermute | solution.py:231
  95.8 2.7 %collective-permute-start.26 = (f32[288,256]{1,0:T(8,128)S(1)}, f32[288,256]{1,0:T(8,128)S(1)}, u32[]{:S(2)}, u32[]{:S(2)}) collective-permute-start(f32[288,256]{1,0:T(8,128)S(1)} %fusion.14), channel_id=1, source_target_pairs={{0,4},{1,5},{2,6},{3,7},{4,0},{5,1},{6,2},{7,3},{8,12},{9,13},{10,... | collective-permute-start | bytes 884744 | tf_op jit(solution)/shard_map/ppermute | solution.py:231
  98.5 13.2 %collective-permute-done.26 = f32[288,256]{1,0:T(8,128)S(1)} collective-permute-done((f32[288,256]{1,0:T(8,128)S(1)}, f32[288,256]{1,0:T(8,128)S(1)}, u32[]{:S(2)}, u32[]{:S(2)}) %collective-permute-start.26) | collective-permute-done | bytes 294944 | tf_op jit(solution)/shard_map/ppermute | solution.py:231
  111.9 4.6 %collective-permute-start.24 = (bf16[128,512]{1,0:T(8,128)(2,1)S(1)}, bf16[128,512]{1,0:T(8,128)(2,1)S(1)}, u32[]{:S(2)}, u32[]{:S(2)}) collective-permute-start(bf16[128,512]{1,0:T(8,128)(2,1)S(1)} %get-tuple-element.29), channel_id=1, source_target_pairs={{0,24},{8,16},{16,8},{24,0},{1,25},{9,17},{17,9},{25,1},{2,26},{10... | collective-permute-start | bytes 393224 | tf_op jit(solution)/shard_map/ppermute | solution.py:231
  116.5 0.6 collective-permute-start.22
  117.2 1.5 %collective-permute-start.28 = (f32[288,256]{1,0:T(8,128)S(1)}, f32[288,256]{1,0:T(8,128)S(1)}, u32[]{:S(2)}, u32[]{:S(2)}) collective-permute-start(f32[288,256]{1,0:T(8,128)S(1)} %add.136), channel_id=1, source_target_pairs={{0,8},{8,0},{16,24},{24,16},{1,9},{9,1},{17,25},{25,17},{2,10},{10... | collective-permute-start | bytes 884744 | tf_op jit(solution)/shard_map/ppermute | solution.py:231
  118.6 0.9 multiply_convert_fusion
  119.5 1.5 %collective-permute-start.16 = (bf16[128,512]{1,0:T(8,128)(2,1)S(1)}, bf16[128,512]{1,0:T(8,128)(2,1)S(1)}, u32[]{:S(2)}, u32[]{:S(2)}) collective-permute-start(bf16[128,512]{1,0:T(8,128)(2,1)S(1)} %get-tuple-element.25), channel_id=1, source_target_pairs={{0,24},{8,16},{16,8},{24,0},{1,25},{9,17},{17,9},{25,1},{2,26},{10... | collective-permute-start | bytes 393224 | tf_op jit(solution)/shard_map/ppermute | solution.py:231
  121.0 0.6 collective-permute-start.15
  121.6 1.9 %collective-permute-done.23 = bf16[128,512]{1,0:T(8,128)(2,1)S(1)} collective-permute-done((bf16[128,512]{1,0:T(8,128)(2,1)S(1)}, bf16[128,512]{1,0:T(8,128)(2,1)S(1)}, u32[]{:S(2)}, u32[]{:S(2)}) %collective-permute-start.23) | collective-permute-done | bytes 131104 | tf_op jit(solution)/shard_map/ppermute | solution.py:231
  123.5 0.8 collective-permute-start.14
  124.4 5.1 %collective-permute-done.28 = f32[288,256]{1,0:T(8,128)S(1)} collective-permute-done((f32[288,256]{1,0:T(8,128)S(1)}, f32[288,256]{1,0:T(8,128)S(1)}, u32[]{:S(2)}, u32[]{:S(2)}) %collective-permute-start.28) | collective-permute-done | bytes 294944 | tf_op jit(solution)/shard_map/ppermute | solution.py:231
  129.5 1.8 %collective-permute-start.29 = (f32[288,256]{1,0:T(8,128)S(1)}, f32[288,256]{1,0:T(8,128)S(1)}, u32[]{:S(2)}, u32[]{:S(2)}) collective-permute-start(f32[288,256]{1,0:T(8,128)S(1)} %add.137), channel_id=1, source_target_pairs={{0,16},{8,24},{16,0},{24,8},{1,17},{9,25},{17,1},{25,9},{2,18},{10... | collective-permute-start | bytes 884744 | tf_op jit(solution)/shard_map/ppermute | solution.py:231
  131.3 2.1 %collective-permute-done.16 = bf16[128,512]{1,0:T(8,128)(2,1)S(1)} collective-permute-done((bf16[128,512]{1,0:T(8,128)(2,1)S(1)}, bf16[128,512]{1,0:T(8,128)(2,1)S(1)}, u32[]{:S(2)}, u32[]{:S(2)}) %collective-permute-start.16) | collective-permute-done | bytes 131104 | tf_op jit(solution)/shard_map/ppermute | solution.py:231
  133.5 1.2 collective-permute-done.14
  134.7 1.0 convolution_convert_fusion
  135.7 3.1 %collective-permute-done.29 = f32[288,256]{1,0:T(8,128)S(1)} collective-permute-done((f32[288,256]{1,0:T(8,128)S(1)}, f32[288,256]{1,0:T(8,128)S(1)}, u32[]{:S(2)}, u32[]{:S(2)}) %collective-permute-start.29) | collective-permute-done | bytes 294944 | tf_op jit(solution)/shard_map/ppermute | solution.py:231
  138.9 0.6 fusion.8
  139.5 0.8 copy.17
  (55 shorter events, 1.8 us)
Async XLA Ops:
  0.6 45.5 %copy-start = (f32[16,256]{1,0:T(8,128)S(1)}, f32[16,256]{1,0:T(8,128)}, u32[]{:S(2)}) copy-start(f32[16,256]{1,0:T(8,128)} %param.15) | copy-start | bytes 49156
  0.6 17.2 %copy-start.3 = (bf16[256,256]{1,0:T(8,128)(2,1)S(1)}, bf16[256,256]{1,0:T(8,128)(2,1)}, u32[]{:S(2)}) copy-start(bf16[256,256]{1,0:T(8,128)(2,1)} %refs_2_.1) | copy-start | bytes 393220
  0.7 17.2 %collective-permute-start = (bf16[512,256]{1,0:T(8,128)(2,1)}, bf16[512,256]{1,0:T(8,128)(2,1)S(1)}, u32[]{:S(2)}, u32[]{:S(2)}) collective-permute-start(bf16[512,256]{1,0:T(8,128)(2,1)} %refs_8_.3), channel_id=1, source_target_pairs={{0,8},{8,0},{16,24},{24,16},{1,9},{9,1},{17,25},{25,17},{2,10},{10... | collective-permute-start | bytes 786440 | tf_op jit(solution)/shard_map/ppermute | solution.py:231
  3.7 14.2 %collective-permute-start.1 = (bf16[512,256]{1,0:T(8,128)(2,1)}, bf16[512,256]{1,0:T(8,128)(2,1)S(1)}, u32[]{:S(2)}, u32[]{:S(2)}) collective-permute-start(bf16[512,256]{1,0:T(8,128)(2,1)} %refs_8_.3), channel_id=1, source_target_pairs={{0,16},{8,24},{16,0},{24,8},{1,17},{9,25},{17,1},{25,9},{2,18},{10... | collective-permute-start | bytes 786440 | tf_op jit(solution)/shard_map/ppermute | solution.py:231
  5.2 12.6 %collective-permute-start.2 = (bf16[512,256]{1,0:T(8,128)(2,1)}, bf16[512,256]{1,0:T(8,128)(2,1)S(1)}, u32[]{:S(2)}, u32[]{:S(2)}) collective-permute-start(bf16[512,256]{1,0:T(8,128)(2,1)} %refs_8_.3), channel_id=1, source_target_pairs={{0,24},{8,16},{16,8},{24,0},{1,25},{9,17},{17,9},{25,1},{2,26},{10... | collective-permute-start | bytes 786440 | tf_op jit(solution)/shard_map/ppermute | solution.py:231
  6.7 4.6 %copy-start.1 = (bf16[1,1,384,128,128]{4,3,2,1,0:T(8,128)(2,1)S(1)}, bf16[1,1,384,128,128]{4,3,2,1,0:T(8,128)(2,1)}, u32[]{:S(2)}) copy-start(bf16[1,1,384,128,128]{4,3,2,1,0:T(8,128)(2,1)} %param.11) | copy-start | bytes 37748740
  11.3 6.5 %copy-start.2 = (bf16[512,256]{1,0:T(8,128)(2,1)S(1)}, bf16[512,256]{1,0:T(8,128)(2,1)}, u32[]{:S(2)}) copy-start(bf16[512,256]{1,0:T(8,128)(2,1)} %refs_8_.3) | copy-start | bytes 786436
  17.7 28.4 %copy-start.4 = (bf16[512,256]{1,0:T(8,128)(2,1)S(1)}, bf16[512,256]{1,0:T(8,128)(2,1)}, u32[]{:S(2)}) copy-start(bf16[512,256]{1,0:T(8,128)(2,1)} %param.17) | copy-start | bytes 786436
  17.7 28.4 %copy-start.5 = (s32[512]{0:T(512)S(1)}, s32[512]{0:T(512)}, u32[]{:S(2)}) copy-start(s32[512]{0:T(512)} %param.16) | copy-start | bytes 6148
  23.4 3.5 %collective-permute-start.3 = (bf16[2048,128]{1,0:T(8,128)(2,1)S(1)}, bf16[2048,128]{1,0:T(8,128)(2,1)S(1)}, u32[]{:S(2)}, u32[]{:S(2)}) collective-permute-start(bf16[2048,128]{1,0:T(8,128)(2,1)S(1)} %get-tuple-element.19), channel_id=1, source_target_pairs={{0,1},{1,0},{2,3},{3,2},{4,5},{5,4},{6,7},{7,6},{8,9},{9,8},{10,11... | collective-permute-start | bytes 1572872 | tf_op jit(solution)/shard_map/ppermute | solution.py:231
  25.4 3.2 %collective-permute-start.6 = (bf16[2048,128]{1,0:T(8,128)(2,1)S(1)}, bf16[2048,128]{1,0:T(8,128)(2,1)S(1)}, u32[]{:S(2)}, u32[]{:S(2)}) collective-permute-start(bf16[2048,128]{1,0:T(8,128)(2,1)S(1)} %get-tuple-element.21), channel_id=1, source_target_pairs={{0,1},{1,0},{2,3},{3,2},{4,5},{5,4},{6,7},{7,6},{8,9},{9,8},{10,11... | collective-permute-start | bytes 1572872 | tf_op jit(solution)/shard_map/ppermute | solution.py:231
  27.0 9.2 %collective-permute-start.4 = (bf16[1024,128]{1,0:T(8,128)(2,1)S(1)}, bf16[1024,128]{1,0:T(8,128)(2,1)S(1)}, u32[]{:S(2)}, u32[]{:S(2)}) collective-permute-start(bf16[1024,128]{1,0:T(8,128)(2,1)S(1)} %add_convert_fusion.1), channel_id=1, source_target_pairs={{0,2},{1,3},{2,0},{3,1},{4,6},{5,7},{6,4},{7,5},{8,10},{9,11},{10,... | collective-permute-start | bytes 786440 | tf_op jit(solution)/shard_map/ppermute | solution.py:231
  28.7 15.4 %collective-permute-start.7 = (bf16[1024,128]{1,0:T(8,128)(2,1)S(1)}, bf16[1024,128]{1,0:T(8,128)(2,1)S(1)}, u32[]{:S(2)}, u32[]{:S(2)}) collective-permute-start(bf16[1024,128]{1,0:T(8,128)(2,1)S(1)} %add_convert_fusion), channel_id=1, source_target_pairs={{0,2},{1,3},{2,0},{3,1},{4,6},{5,7},{6,4},{7,5},{8,10},{9,11},{10,... | collective-permute-start | bytes 786440 | tf_op jit(solution)/shard_map/ppermute | solution.py:231
  36.3 10.3 %collective-permute-start.5 = (bf16[512,128]{1,0:T(8,128)(2,1)S(1)}, bf16[512,128]{1,0:T(8,128)(2,1)S(1)}, u32[]{:S(2)}, u32[]{:S(2)}) collective-permute-start(bf16[512,128]{1,0:T(8,128)(2,1)S(1)} %add_convert_fusion.5), channel_id=1, source_target_pairs={{0,4},{1,5},{2,6},{3,7},{4,0},{5,1},{6,2},{7,3},{8,12},{9,13},{10,... | collective-permute-start | bytes 393224 | tf_op jit(solution)/shard_map/ppermute | solution.py:231
  44.2 8.9 %collective-permute-start.8 = (bf16[512,128]{1,0:T(8,128)(2,1)S(1)}, bf16[512,128]{1,0:T(8,128)(2,1)S(1)}, u32[]{:S(2)}, u32[]{:S(2)}) collective-permute-start(bf16[512,128]{1,0:T(8,128)(2,1)S(1)} %add_convert_fusion.4), channel_id=1, source_target_pairs={{0,4},{1,5},{2,6},{3,7},{4,0},{5,1},{6,2},{7,3},{8,12},{9,13},{10,... | collective-permute-start | bytes 393224 | tf_op jit(solution)/shard_map/ppermute | solution.py:231
  53.4 7.4 %collective-permute-start.17 = (bf16[512,128]{1,0:T(8,128)(2,1)S(1)}, bf16[512,128]{1,0:T(8,128)(2,1)S(1)}, u32[]{:S(2)}, u32[]{:S(2)}) collective-permute-start(bf16[512,128]{1,0:T(8,128)(2,1)S(1)} %get-tuple-element.48.refs_2_), channel_id=1, source_target_pairs={{0,4},{1,5},{2,6},{3,7},{4,0},{5,1},{6,2},{7,3},{8,12},{9,13},{10,... | collective-permute-start | bytes 393224 | tf_op jit(solution)/shard_map/ppermute | solution.py:231
  60.8 12.0 %collective-permute-start.18 = (bf16[1024,128]{1,0:T(8,128)(2,1)S(1)}, bf16[1024,128]{1,0:T(8,128)(2,1)S(1)}, u32[]{:S(2)}, u32[]{:S(2)}) collective-permute-start(bf16[1024,128]{1,0:T(8,128)(2,1)S(1)} %pad_maximum_fusion.2), channel_id=1, source_target_pairs={{0,2},{1,3},{2,0},{3,1},{4,6},{5,7},{6,4},{7,5},{8,10},{9,11},{10,... | collective-permute-start | bytes 786440 | tf_op jit(solution)/shard_map/ppermute | solution.py:231
  60.9 8.8 %collective-permute-start.9 = (bf16[512,128]{1,0:T(8,128)(2,1)S(1)}, bf16[512,128]{1,0:T(8,128)(2,1)S(1)}, u32[]{:S(2)}, u32[]{:S(2)}) collective-permute-start(bf16[512,128]{1,0:T(8,128)(2,1)S(1)} %get-tuple-element.44.refs_2_), channel_id=1, source_target_pairs={{0,4},{1,5},{2,6},{3,7},{4,0},{5,1},{6,2},{7,3},{8,12},{9,13},{10,... | collective-permute-start | bytes 393224 | tf_op jit(solution)/shard_map/ppermute | solution.py:231
  69.8 8.5 %collective-permute-start.10 = (bf16[1024,128]{1,0:T(8,128)(2,1)S(1)}, bf16[1024,128]{1,0:T(8,128)(2,1)S(1)}, u32[]{:S(2)}, u32[]{:S(2)}) collective-permute-start(bf16[1024,128]{1,0:T(8,128)(2,1)S(1)} %pad_maximum_fusion.1), channel_id=1, source_target_pairs={{0,2},{1,3},{2,0},{3,1},{4,6},{5,7},{6,4},{7,5},{8,10},{9,11},{10,... | collective-permute-start | bytes 786440 | tf_op jit(solution)/shard_map/ppermute | solution.py:231
  72.9 5.4 %collective-permute-start.21 = (bf16[1024,128]{1,0:T(8,128)(2,1)S(1)}, bf16[1024,128]{1,0:T(8,128)(2,1)S(1)}, u32[]{:S(2)}, u32[]{:S(2)}) collective-permute-start(bf16[1024,128]{1,0:T(8,128)(2,1)S(1)} %collective-permute-done.18.refs_4_), channel_id=1, source_target_pairs={{0,1},{1,0},{2,3},{3,2},{4,5},{5,4},{6,7},{7,6},{8,9},{9,8},{10,11... | collective-permute-start | bytes 786440 | tf_op jit(solution)/shard_map/ppermute | solution.py:231
  73.1 1.5 %collective-permute-start.19 = (bf16[512,128]{1,0:T(8,128)(2,1)S(1)}, bf16[512,128]{1,0:T(8,128)(2,1)S(1)}, u32[]{:S(2)}, u32[]{:S(2)}) collective-permute-start(bf16[512,128]{1,0:T(8,128)(2,1)S(1)} %get-tuple-element.48.refs_2_), channel_id=1, source_target_pairs={{0,1},{1,0},{2,3},{3,2},{4,5},{5,4},{6,7},{7,6},{8,9},{9,8},{10,11... | collective-permute-start | bytes 393224 | tf_op jit(solution)/shard_map/ppermute | solution.py:231
  73.6 8.6 %collective-permute-start.11 = (bf16[512,128]{1,0:T(8,128)(2,1)S(1)}, bf16[512,128]{1,0:T(8,128)(2,1)S(1)}, u32[]{:S(2)}, u32[]{:S(2)}) collective-permute-start(bf16[512,128]{1,0:T(8,128)(2,1)S(1)} %get-tuple-element.44.refs_2_), channel_id=1, source_target_pairs={{0,1},{1,0},{2,3},{3,2},{4,5},{5,4},{6,7},{7,6},{8,9},{9,8},{10,11... | collective-permute-start | bytes 393224 | tf_op jit(solution)/shard_map/ppermute | solution.py:231
  73.6 4.6 %collective-permute-start.20 = (bf16[512,128]{1,0:T(8,128)(2,1)S(1)}, bf16[512,128]{1,0:T(8,128)(2,1)S(1)}, u32[]{:S(2)}, u32[]{:S(2)}) collective-permute-start(bf16[512,128]{1,0:T(8,128)(2,1)S(1)} %collective-permute-done.17.refs_3_), channel_id=1, source_target_pairs={{0,1},{1,0},{2,3},{3,2},{4,5},{5,4},{6,7},{7,6},{8,9},{9,8},{10,11... | collective-permute-start | bytes 393224 | tf_op jit(solution)/shard_map/ppermute | solution.py:231
  74.6 7.6 %collective-permute-start.12 = (bf16[512,128]{1,0:T(8,128)(2,1)S(1)}, bf16[512,128]{1,0:T(8,128)(2,1)S(1)}, u32[]{:S(2)}, u32[]{:S(2)}) collective-permute-start(bf16[512,128]{1,0:T(8,128)(2,1)S(1)} %collective-permute-done.9.refs_3_), channel_id=1, source_target_pairs={{0,1},{1,0},{2,3},{3,2},{4,5},{5,4},{6,7},{7,6},{8,9},{9,8},{10,11... | collective-permute-start | bytes 393224 | tf_op jit(solution)/shard_map/ppermute | solution.py:231
  78.2 3.9 %collective-permute-start.13 = (bf16[1024,128]{1,0:T(8,128)(2,1)S(1)}, bf16[1024,128]{1,0:T(8,128)(2,1)S(1)}, u32[]{:S(2)}, u32[]{:S(2)}) collective-permute-start(bf16[1024,128]{1,0:T(8,128)(2,1)S(1)} %collective-permute-done.10.refs_4_), channel_id=1, source_target_pairs={{0,1},{1,0},{2,3},{3,2},{4,5},{5,4},{6,7},{7,6},{8,9},{9,8},{10,11... | collective-permute-start | bytes 786440 | tf_op jit(solution)/shard_map/ppermute | solution.py:231
  86.2 9.5 %collective-permute-start.25 = (f32[288,256]{1,0:T(8,128)S(1)}, f32[288,256]{1,0:T(8,128)S(1)}, u32[]{:S(2)}, u32[]{:S(2)}) collective-permute-start(f32[288,256]{1,0:T(8,128)S(1)} %maximum_maximum_fusion), channel_id=1, source_target_pairs={{0,2},{1,3},{2,0},{3,1},{4,6},{5,7},{6,4},{7,5},{8,10},{9,11},{10,... | collective-permute-start | bytes 884744 | tf_op jit(solution)/shard_map/ppermute | solution.py:231
  95.8 16.0 %collective-permute-start.26 = (f32[288,256]{1,0:T(8,128)S(1)}, f32[288,256]{1,0:T(8,128)S(1)}, u32[]{:S(2)}, u32[]{:S(2)}) collective-permute-start(f32[288,256]{1,0:T(8,128)S(1)} %fusion.14), channel_id=1, source_target_pairs={{0,4},{1,5},{2,6},{3,7},{4,0},{5,1},{6,2},{7,3},{8,12},{9,13},{10,... | collective-permute-start | bytes 884744 | tf_op jit(solution)/shard_map/ppermute | solution.py:231
  111.8 5.3 %collective-permute-start.27 = (f32[288,256]{1,0:T(8,128)S(1)}, f32[288,256]{1,0:T(8,128)S(1)}, u32[]{:S(2)}, u32[]{:S(2)}) collective-permute-start(f32[288,256]{1,0:T(8,128)S(1)} %add.135), channel_id=1, source_target_pairs={{0,1},{1,0},{2,3},{3,2},{4,5},{5,4},{6,7},{7,6},{8,9},{9,8},{10,11... | collective-permute-start | bytes 884744 | tf_op jit(solution)/shard_map/ppermute | solution.py:231
  111.9 9.1 %collective-permute-start.24 = (bf16[128,512]{1,0:T(8,128)(2,1)S(1)}, bf16[128,512]{1,0:T(8,128)(2,1)S(1)}, u32[]{:S(2)}, u32[]{:S(2)}) collective-permute-start(bf16[128,512]{1,0:T(8,128)(2,1)S(1)} %get-tuple-element.29), channel_id=1, source_target_pairs={{0,24},{8,16},{16,8},{24,0},{1,25},{9,17},{17,9},{25,1},{2,26},{10... | collective-permute-start | bytes 393224 | tf_op jit(solution)/shard_map/ppermute | solution.py:231
  116.5 7.0 %collective-permute-start.23 = (bf16[128,512]{1,0:T(8,128)(2,1)S(1)}, bf16[128,512]{1,0:T(8,128)(2,1)S(1)}, u32[]{:S(2)}, u32[]{:S(2)}) collective-permute-start(bf16[128,512]{1,0:T(8,128)(2,1)S(1)} %get-tuple-element.28), channel_id=1, source_target_pairs={{0,16},{8,24},{16,0},{24,8},{1,17},{9,25},{17,1},{25,9},{2,18},{10... | collective-permute-start | bytes 393224 | tf_op jit(solution)/shard_map/ppermute | solution.py:231
  116.5 7.8 %collective-permute-start.22 = (bf16[128,512]{1,0:T(8,128)(2,1)S(1)}, bf16[128,512]{1,0:T(8,128)(2,1)S(1)}, u32[]{:S(2)}, u32[]{:S(2)}) collective-permute-start(bf16[128,512]{1,0:T(8,128)(2,1)S(1)} %get-tuple-element.27), channel_id=1, source_target_pairs={{0,8},{8,0},{16,24},{24,16},{1,9},{9,1},{17,25},{25,17},{2,10},{10... | collective-permute-start | bytes 393224 | tf_op jit(solution)/shard_map/ppermute | solution.py:231
  117.2 12.3 %collective-permute-start.28 = (f32[288,256]{1,0:T(8,128)S(1)}, f32[288,256]{1,0:T(8,128)S(1)}, u32[]{:S(2)}, u32[]{:S(2)}) collective-permute-start(f32[288,256]{1,0:T(8,128)S(1)} %add.136), channel_id=1, source_target_pairs={{0,8},{8,0},{16,24},{24,16},{1,9},{9,1},{17,25},{25,17},{2,10},{10... | collective-permute-start | bytes 884744 | tf_op jit(solution)/shard_map/ppermute | solution.py:231
  119.5 14.0 %collective-permute-start.16 = (bf16[128,512]{1,0:T(8,128)(2,1)S(1)}, bf16[128,512]{1,0:T(8,128)(2,1)S(1)}, u32[]{:S(2)}, u32[]{:S(2)}) collective-permute-start(bf16[128,512]{1,0:T(8,128)(2,1)S(1)} %get-tuple-element.25), channel_id=1, source_target_pairs={{0,24},{8,16},{16,8},{24,0},{1,25},{9,17},{17,9},{25,1},{2,26},{10... | collective-permute-start | bytes 393224 | tf_op jit(solution)/shard_map/ppermute | solution.py:231
  121.0 12.5 %collective-permute-start.15 = (bf16[128,512]{1,0:T(8,128)(2,1)S(1)}, bf16[128,512]{1,0:T(8,128)(2,1)S(1)}, u32[]{:S(2)}, u32[]{:S(2)}) collective-permute-start(bf16[128,512]{1,0:T(8,128)(2,1)S(1)} %get-tuple-element.24), channel_id=1, source_target_pairs={{0,16},{8,24},{16,0},{24,8},{1,17},{9,25},{17,1},{25,9},{2,18},{10... | collective-permute-start | bytes 393224 | tf_op jit(solution)/shard_map/ppermute | solution.py:231
  123.5 11.2 %collective-permute-start.14 = (bf16[128,512]{1,0:T(8,128)(2,1)S(1)}, bf16[128,512]{1,0:T(8,128)(2,1)S(1)}, u32[]{:S(2)}, u32[]{:S(2)}) collective-permute-start(bf16[128,512]{1,0:T(8,128)(2,1)S(1)} %get-tuple-element.23), channel_id=1, source_target_pairs={{0,8},{8,0},{16,24},{24,16},{1,9},{9,1},{17,25},{25,17},{2,10},{10... | collective-permute-start | bytes 393224 | tf_op jit(solution)/shard_map/ppermute | solution.py:231
  129.5 9.3 %collective-permute-start.29 = (f32[288,256]{1,0:T(8,128)S(1)}, f32[288,256]{1,0:T(8,128)S(1)}, u32[]{:S(2)}, u32[]{:S(2)}) collective-permute-start(f32[288,256]{1,0:T(8,128)S(1)} %add.137), channel_id=1, source_target_pairs={{0,16},{8,24},{16,0},{24,8},{1,17},{9,25},{17,1},{25,9},{2,18},{10... | collective-permute-start | bytes 884744 | tf_op jit(solution)/shard_map/ppermute | solution.py:231

commit v2 on v1

--- a/solution.py
+++ b/solution.py
@@ -1,4 +1,5 @@
 import functools
+import math
 
 import jax
 import jax.numpy as jnp
@@ -11,6 +12,7 @@
 GROUP = 16
 BUFFERS = 8
 HEAVY = 16
+CHUNKS = 2
 MIB = 1 << 20
 
 
@@ -112,7 +114,6 @@
     places = rows * col_blocks + cols
     smem = pl.BlockSpec(memory_space=pltpu.SMEM)
     vmem = pl.BlockSpec(memory_space=pltpu.VMEM)
-    slot_total = slots.shape[0]
     return pl.pallas_call(
         build_kernel,
         out_shape=pltpu.VMEM((row_blocks * BLOCK, col_blocks * BLOCK), jnp.bfloat16),
@@ -124,102 +125,46 @@
             pltpu.SMEM((row_blocks * col_blocks,), jnp.int32),
             pltpu.SemaphoreType.DMA((BUFFERS,)),
         ],
-        compiler_params=pltpu.CompilerParams(vmem_limit_bytes=12 * MIB),
+        compiler_params=pltpu.CompilerParams(vmem_limit_bytes=36 * MIB),
         cost_estimate=pl.CostEstimate(flops=0, bytes_accessed=20 * MIB, transcendentals=0),
         name="build_tile",
     )(live, rows, cols, places[None, :], places[:, None], slots)
 
 
-def forward_kernel(order, *refs):
-    at_ref, tile_ref, weight_ref = refs[:3]
-    chunks = 2
-    feature_refs = refs[3 : -1 - 2 * chunks]
-    send_refs, rest_refs = refs[-1 - 2 * chunks : -1 - chunks], refs[-1 - chunks : -1]
-    hidden = refs[-1]
+def forward_kernel(order, chunk, at_ref, tile_ref, *refs):
+    *feature_refs, send_ref, rest_ref, panel = refs
     own_row, own_col = at_ref[0], at_ref[1]
     share = feature_refs[0].shape[0]
     for r, feature_ref in enumerate(feature_refs):
         at = pl.ds(pl.multiple_of((own_row ^ r) * share, share), share)
-        hidden[at, :] = jnp.dot(
-            feature_ref[...], weight_ref[...], preferred_element_type=jnp.float32
-        ).astype(jnp.bfloat16)
+        panel[at, :] = feature_ref[...]
+    step = share // CHUNKS
     half = len(order) // 2
-    width = hidden.shape[1] // chunks
-    step = share // 2
+    first = chunk * len(order) * step
     for t, k in enumerate(order):
-        base = (own_col ^ k) * share
-        into = send_refs if t < half else rest_refs
-        for m in range(0, share, step):
-            at = pl.ds(pl.multiple_of(base + m, step), step)
-            product = jnp.dot(tile_ref[at, :], hidden[...], preferred_element_type=jnp.float32)
-            product = product.astype(jnp.bfloat16)
-            to = pl.ds((t % half) * share + m, step)
-            for c in range(chunks):
-                into[c][to, :] = product[:, c * width : (c + 1) * width]
-
-
-def forward(at, tile, weight, features, order):
+        at = pl.ds(pl.multiple_of(first + (own_col ^ k) * step, step), step)
+        product = jnp.dot(tile_ref[at, :], panel[...], preferred_element_type=jnp.float32)
+        into = send_ref if t < half else rest_ref
+        into[pl.ds((t % half) * step, step), :] = product.astype(jnp.bfloat16)
+
+
+def forward(chunk, at, tile, features, order):
     share, width = features[0].shape
-    half = len(order) // 2
-    part = pltpu.VMEM((half * share, width // 2), jnp.bfloat16)
+    part = pltpu.VMEM((len(order) // 2 * share // CHUNKS, width), jnp.bfloat16)
     vmem = pl.BlockSpec(memory_space=pltpu.VMEM)
     smem = pl.BlockSpec(memory_space=pltpu.SMEM)
     return pl.pallas_call(
-        functools.partial(forward_kernel, order),
-        out_shape=[part] * 4,
-        in_specs=[smem] + [vmem] * (2 + len(features)),
-        out_specs=[vmem] * 4,
+        functools.partial(forward_kernel, order, chunk),
+        out_shape=[part] * 2,
+        in_specs=[smem] + [vmem] * (1 + len(features)),
+        out_specs=[vmem] * 2,
         scratch_shapes=[pltpu.VMEM((len(features) * share, width), jnp.bfloat16)],
-        compiler_params=pltpu.CompilerParams(vmem_limit_bytes=12 * MIB),
+        compiler_params=pltpu.CompilerParams(vmem_limit_bytes=8 * MIB),
         cost_estimate=pl.CostEstimate(
-            flops=2 * tile.shape[0] * tile.shape[1] * width, bytes_accessed=0, transcendentals=0
+            flops=2 * tile.shape[0] // CHUNKS * tile.shape[1] * width, bytes_accessed=0, transcendentals=0
         ),
         name="forward",
-    )(at, tile, weight, *features)
-
-
-def backward_kernel(orders, row_count, *refs):
-    at_ref, tile_ref = refs[:2]
-    grad_refs = refs[2 : 2 + len(orders)]
-    feature_refs = refs[2 + len(orders) : 2 + len(orders) + row_count]
-    part_refs = refs[-2 - row_count : -2]
-    weight_ref, turned = refs[-2:]
-    own_row, own_col = at_ref[0], at_ref[1]
-    share = feature_refs[0].shape[0]
-    for order, grad_ref in zip(orders, grad_refs):
-        for t, k in enumerate(order):
-            at = pl.ds(pl.multiple_of((own_col ^ k) * share, share), share)
-            turned[:, at] = grad_ref[t * share : (t + 1) * share, :].T
-    total = None
-    for r in range(row_count):
-        at = pl.ds(pl.multiple_of((own_row ^ r) * share, share), share)
-        product = jnp.dot(turned[...], tile_ref[:, at], preferred_element_type=jnp.float32)
-        product = product.astype(jnp.bfloat16)
-        part_refs[r][...] = product
-        term = jnp.dot(product, feature_refs[r][...], preferred_element_type=jnp.float32)
-        total = term if total is None else total + term
-    weight_ref[...] = total
-
-
-def backward(at, tile, grads, orders, features):
-    share, width = features[0].shape
-    chunk = grads[0].shape[1]
-    rows = len(features)
-    vmem = pl.BlockSpec(memory_space=pltpu.VMEM)
-    smem = pl.BlockSpec(memory_space=pltpu.SMEM)
-    return pl.pallas_call(
-        functools.partial(backward_kernel, orders, rows),
-        out_shape=[pltpu.VMEM((chunk, share), jnp.bfloat16)] * rows
-        + [pltpu.VMEM((chunk, width), jnp.float32)],
-        in_specs=[smem] + [vmem] * (1 + len(grads) + rows),
-        out_specs=[vmem] * (rows + 1),
-        scratch_shapes=[pltpu.VMEM((chunk, tile.shape[0]), jnp.bfloat16)],
-        compiler_params=pltpu.CompilerParams(vmem_limit_bytes=12 * MIB),
-        cost_estimate=pl.CostEstimate(
-            flops=4 * tile.shape[0] * tile.shape[1] * chunk, bytes_accessed=0, transcendentals=0
-        ),
-        name="backward",
-    )(at, tile, *grads, *features)
+    )(at, tile, *features)
 
 
 def silu_slope(values):
@@ -227,8 +172,240 @@
     return sig * (1.0 + values * (1.0 - sig))
 
 
+def wide(values):
+    return values.astype(jnp.float32)
+
+
+def dot_last(left, right):
+    return lax.dot_general(left, right, (((1,), (1,)), ((), ())), preferred_element_type=jnp.float32)
+
+
+def gate_kernel(chunk, upstream_ref, weight_ref, *refs):
+    *term_refs, turned_ref, grad_ref, rows_ref, summed_ref = refs
+    step = grad_ref.shape[0]
+    rows = None
+    for term_ref in term_refs:
+        term = wide(term_ref[term_ref.shape[0] - step :, :])
+        rows = term if rows is None else rows + term
+    high = rows.astype(jnp.bfloat16)
+    low = (rows - wide(high)).astype(jnp.bfloat16)
+    weight = weight_ref[...]
+    summed = jnp.dot(high, weight, preferred_element_type=jnp.float32) + jnp.dot(
+        low, weight, preferred_element_type=jnp.float32
+    )
+    upstream = upstream_ref[chunk * step : (chunk + 1) * step, :]
+    grad = (upstream * silu_slope(summed)).astype(jnp.bfloat16)
+    turned_ref[...] = dot_last(grad, weight).astype(jnp.bfloat16)
+    grad_ref[...] = grad
+    rows_ref[...] = high
+    summed_ref[...] = summed
+
+
+def gate(chunk, upstream, weight, terms):
+    shape = (upstream.shape[0] // CHUNKS, upstream.shape[1])
+    vmem = pl.BlockSpec(memory_space=pltpu.VMEM)
+    return pl.pallas_call(
+        functools.partial(gate_kernel, chunk),
+        out_shape=[pltpu.VMEM(shape, jnp.bfloat16)] * 3 + [pltpu.VMEM(shape, jnp.float32)],
+        in_specs=[vmem] * (2 + len(terms)),
+        out_specs=[vmem] * 4,
+        compiler_params=pltpu.CompilerParams(vmem_limit_bytes=8 * MIB),
+        cost_estimate=pl.CostEstimate(flops=1 << 27, bytes_accessed=0, transcendentals=1 << 16),
+        name="gate",
+    )(upstream, weight, *terms)
+
+
+def pack(values, exact_rows):
+    exact = values[values.shape[0] - exact_rows :]
+    high = exact.astype(jnp.bfloat16)
+    low = (exact - wide(high)).astype(jnp.bfloat16)
+    return jnp.concatenate([values[: -exact_rows].astype(jnp.bfloat16), high, low], axis=0)
+
+
+def unpack(message, exact_rows):
+    values = wide(message)
+    rows = message.shape[0] - 2 * exact_rows
+    exact = values[rows : rows + exact_rows] + values[rows + exact_rows :]
+    return jnp.concatenate([values[:rows], exact], axis=0)
+
+
+def local_kernel(at_ref, members_ref, gains_ref, cotangent_ref, *refs):
+    *given, out_ref, keep_ref, send_ref, weights, exact = refs
+    step = given[0].shape[0]
+    weight_part, part_terms = None, None
+    for n in range(CHUNKS):
+        rows_ref, grad_ref, summed_ref = given[3 * n : 3 * n + 3]
+        at = slice(n * step, (n + 1) * step)
+        summed = summed_ref[...]
+        activated = summed * jax.nn.sigmoid(summed)
+        out_ref[at, :] = (activated * gains_ref[at, :]).astype(out_ref.dtype)
+        term = lax.dot_general(
+            rows_ref[...], grad_ref[...], (((0,), (0,)), ((), ())), preferred_element_type=jnp.float32
+        )
+        weight_part = term if weight_part is None else weight_part + term
+        term = jnp.dot(
+            members_ref[:, at],
+            wide(cotangent_ref[at, :]) * activated,
+            precision=lax.Precision.HIGHEST,
+            preferred_element_type=jnp.float32,
+        )
+        part_terms = term if part_terms is None else part_terms + term
+    weights[...] = weight_part
+    count = part_terms.shape[0]
+    exact[:count, :] = part_terms
+    sizes = jnp.sum(members_ref[...], axis=1, keepdims=True)
+    exact[count:, :] = jnp.broadcast_to(sizes, part_terms.shape)
+    core = at_ref[1] & 1
+    for half, message_ref in ((core, keep_ref), (1 - core, send_ref)):
+        rows = weights.shape[0] // 2
+        top = weights[pl.ds(pl.multiple_of(half * rows, rows), rows), :]
+        bottom = exact[pl.ds(pl.multiple_of(half * count, count), count), :]
+        message_ref[...] = pack(jnp.concatenate([top, bottom], axis=0), count)
+
+
+def local_terms(at, members, gains, cotangent, chunks):
+    share, width = cotangent.shape
+    count = members.shape[0]
+    vmem = pl.BlockSpec(memory_space=pltpu.VMEM)
+    smem = pl.BlockSpec(memory_space=pltpu.SMEM)
+    given = [x for rows, grad, summed in chunks for x in (rows, grad, summed)]
+    return pl.pallas_call(
+        local_kernel,
+        out_shape=[
+            jax.ShapeDtypeStruct((share, width), jnp.bfloat16),
+            pltpu.VMEM((width // 2 + 2 * count, width), jnp.bfloat16),
+            pltpu.VMEM((width // 2 + 2 * count, width), jnp.bfloat16),
+        ],
+        in_specs=[smem] + [vmem] * (3 + len(given)),
+        out_specs=[vmem] * 3,
+        scratch_shapes=[
+            pltpu.VMEM((width, width), jnp.float32),
+            pltpu.VMEM((2 * count, width), jnp.float32),
+        ],
+        compiler_params=pltpu.CompilerParams(vmem_limit_bytes=8 * MIB),
+        cost_estimate=pl.CostEstimate(flops=1 << 28, bytes_accessed=1 << 19, transcendentals=1 << 17),
+        name="local_terms",
+    )(at, members, gains, cotangent, *given)
+
+
+def add_kernel(exact_rows, own_ref, other_ref, out_ref):
+    out_ref[...] = pack(
+        unpack(own_ref[...], exact_rows) + unpack(other_ref[...], exact_rows), exact_rows
+    )
+
+
+def add_messages(exact_rows, own, other):
+    vmem = pl.BlockSpec(memory_space=pltpu.VMEM)
+    return pl.pallas_call(
+        functools.partial(add_kernel, exact_rows),
+        out_shape=pltpu.VMEM(own.shape, jnp.bfloat16),
+        in_specs=[vmem] * 2,
+        out_specs=vmem,
+        compiler_params=pltpu.CompilerParams(vmem_limit_bytes=4 * MIB),
+        name="add_messages",
+    )(own, other)
+
+
+def totals_kernel(exact_rows, scale, at_ref, own_ref, other_ref, weight_ref, gain_ref, exact):
+    core = at_ref[1] & 1
+    rows = weight_ref.shape[0] // 2
+    for half, message_ref in ((core, own_ref), (1 - core, other_ref)):
+        values = unpack(message_ref[...], exact_rows)
+        weight_ref[pl.ds(pl.multiple_of(half * rows, rows), rows), :] = values[:rows] * scale
+        exact[pl.ds(pl.multiple_of(half * exact_rows, exact_rows), exact_rows), :] = values[rows:]
+    gain_ref[...] = exact[:exact_rows, :] / jnp.sqrt(exact[exact_rows:, :])
+
+
+def totals(exact_rows, scale, at, own, other):
+    width = own.shape[1]
+    vmem = pl.BlockSpec(memory_space=pltpu.VMEM)
+    smem = pl.BlockSpec(memory_space=pltpu.SMEM)
+    return pl.pallas_call(
+        functools.partial(totals_kernel, exact_rows, scale),
+        out_shape=[
+            jax.ShapeDtypeStruct((width, width), jnp.float32),
+            jax.ShapeDtypeStruct((exact_rows, width), jnp.float32),
+        ],
+        in_specs=[smem] + [vmem] * 2,
+        out_specs=[vmem] * 2,
+        scratch_shapes=[pltpu.VMEM((2 * exact_rows, width), jnp.float32)],
+        compiler_params=pltpu.CompilerParams(vmem_limit_bytes=4 * MIB),
+        name="totals",
+    )(at, own, other)
+
+
+def backward_kernel(orders, row_count, chunk, at_ref, tile_ref, *refs):
+    grad_refs, refs = refs[: len(orders)], refs[len(orders) :]
+    before_refs, refs = refs[: row_count * (chunk > 0)], refs[row_count * (chunk > 0) :]
+    *part_refs, turned = refs
+    own_row, own_col = at_ref[0], at_ref[1]
+    step = turned.shape[1] // sum(len(o) for o in orders)
+    for order, grad_ref in zip(orders, grad_refs):
+        for t, k in enumerate(order):
+            at = pl.ds(pl.multiple_of((own_col ^ k) * step, step), step)
+            turned[:, at] = grad_ref[t * step : (t + 1) * step, :].T
+    share = part_refs[0].shape[1]
+    depth = turned.shape[1]
+    for r in reversed(range(row_count)):
+        at = pl.ds(pl.multiple_of((own_row ^ r) * share, share), share)
+        product = jnp.dot(
+            turned[...],
+            tile_ref[chunk * depth : (chunk + 1) * depth, at],
+            preferred_element_type=jnp.float32,
+        )
+        if chunk:
+            product = product + before_refs[r][...]
+        part_refs[r][...] = product.astype(part_refs[r].dtype)
+
+
+def backward(chunk, at, tile, grads, orders, before, share, row_count):
+    width = grads[0].shape[1]
+    last = chunk == CHUNKS - 1
+    vmem = pl.BlockSpec(memory_space=pltpu.VMEM)
+    smem = pl.BlockSpec(memory_space=pltpu.SMEM)
+    kinds = [jnp.bfloat16 if last and r else jnp.float32 for r in range(row_count)]
+    return pl.pallas_call(
+        functools.partial(backward_kernel, orders, row_count, chunk),
+        out_shape=[pltpu.VMEM((width, share), kind) for kind in kinds],
+        in_specs=[smem] + [vmem] * (1 + len(grads) + len(before)),
+        out_specs=[vmem] * row_count,
+        scratch_shapes=[pltpu.VMEM((width, tile.shape[0] // CHUNKS), jnp.bfloat16)],
+        compiler_params=pltpu.CompilerParams(vmem_limit_bytes=8 * MIB),
+        cost_estimate=pl.CostEstimate(
+            flops=2 * tile.shape[0] // CHUNKS * tile.shape[1] * width, bytes_accessed=0, transcendentals=0
+        ),
+        name="backward",
+    )(at, tile, *grads, *before)
+
+
+def finish_kernel(*refs):
+    *part_refs, out_ref = refs
+    total = None
+    for part_ref in part_refs:
+        term = wide(part_ref[...])
+        total = term if total is None else total + term
+    out_ref[...] = total.T.astype(out_ref.dtype)
+
+
+def finish(parts):
+    width, share = parts[0].shape
+    vmem = pl.BlockSpec(memory_space=pltpu.VMEM)
+    return pl.pallas_call(
+        finish_kernel,
+        out_shape=jax.ShapeDtypeStruct((share, width), jnp.bfloat16),
+        in_specs=[vmem] * len(parts),
+        out_specs=vmem,
+        compiler_params=pltpu.CompilerParams(vmem_limit_bytes=8 * MIB),
+        name="finish",
+    )(*parts)
+
+
 def swap(values, axis, mask, count):
     return lax.ppermute(values, axis, [(d, d ^ mask) for d in range(count)])
+
+
+def after(values, *others):
+    return lax.optimization_barrier((values, *others))[0]
 
 
 def dense_device(
@@ -245,86 +422,82 @@
     cotangent,
 ):
     share, width = features.shape
-    chunk = width // 2
+    step = share // CHUNKS
+    row_blocks = share * col_count // BLOCK
     at = jnp.stack([lax.axis_index("row"), lax.axis_index("col")]).astype(jnp.int32)
     gathered = [features] + [swap(features, "row", r, row_count) for r in range(1, row_count)]
+    per_device, per_chunk = share // BLOCK, step // BLOCK
+    rows, cols = block_rows[0, 0], block_cols[0, 0]
+    owner, inner = rows // per_device, rows % per_device
+    rows = (inner // per_chunk * col_count + owner) * per_chunk + inner % per_chunk
     tile = build_tile(
-        adjacency[0, 0],
-        block_rows[0, 0],
-        block_cols[0, 0],
-        live_blocks[0],
-        share * col_count // BLOCK,
-        share * row_count // BLOCK,
-    )
-    member = (
-        partition[:, None] == jnp.arange(part_gains.shape[0], dtype=jnp.int32)[None, :]
+        adjacency[0, 0], rows, cols, live_blocks[0], row_blocks, share * row_count // BLOCK
+    )
+    part_count = part_gains.shape[0]
+    members = (
+        partition[None, :] == jnp.arange(part_count, dtype=jnp.int32)[:, None]
     ).astype(jnp.float32)
-    row_gains = jnp.dot(member, part_gains, precision=lax.Precision.HIGHEST)
-    upstream = cotangent.astype(jnp.float32) * row_gains
+    row_gains = lax.dot_general(
+        members, part_gains, (((0,), (0,)), ((), ())), precision=lax.Precision.HIGHEST
+    )
+    upstream = wide(cotangent) * row_gains
 
     order = halving_order(col_count)
     col_bits = bits_of(col_count)
-    *parts, = forward(at, tile, weight, gathered, order)
-    sends, rests = parts[:2], parts[2:]
-
-    def wide(values):
-        return values.astype(jnp.float32)
-
-    summed, hidden_parts, weight_parts = [], [], []
-    for c in range(2):
-        arrived = [swap(sends[c], "col", col_bits[0], col_count)]
-        rest = rests[c]
-        for bit in col_bits[1:]:
-            first = sum(wide(a[-rest.shape[0] :][: rest.shape[0] // 2]) for a in arrived)
+    chunks = range(CHUNKS)
+    sends, rests = zip(*(forward(n, at, tile, gathered, order) for n in chunks))
+    sends, rests = list(sends), list(rests)
+
+    arrived = [[swap(send, "col", col_bits[0], col_count)] for send in sends]
+    for bit in col_bits[1:]:
+        last = None
+        for n in chunks:
+            rest = rests[n]
             half = rest.shape[0] // 2
+            first = sum(wide(a[-2 * half :][:half]) for a in arrived[n])
             out = (wide(rest[:half]) + first).astype(jnp.bfloat16)
-            arrived.append(swap(out, "col", bit, col_count))
-            rest = rest[half:]
-        total = wide(rest)
-        for a in arrived:
-            total = total + wide(a[-share:])
-        summed.append(total)
-        grad = (upstream[:, c * chunk : (c + 1) * chunk] * silu_slope(total)).astype(jnp.bfloat16)
-        held, orders = [grad], [[0]]
-        for bit in reversed(col_bits[1:]):
-            sent = held[0] if len(held) == 1 else jnp.concatenate(held[::-1], axis=0)
-            held.append(swap(sent, "col", bit, col_count))
-            orders.append([k ^ bit for o in orders[::-1] for k in o])
-        bit = col_bits[0]
-        for h, o in list(zip(held, orders)):
-            held.append(swap(h, "col", bit, col_count))
-            orders.append([k ^ bit for k in o])
-        *hidden_part, weight_part = backward(at, tile, held, orders, gathered)
-        for r in range(1, row_count):
-            hidden_part[r] = swap(hidden_part[r], "row", r, row_count)
-        hidden_parts.append(hidden_part)
-        weight_parts.append(weight_part)
-
-    summed = jnp.concatenate(summed, axis=1)
-    activated = jax.nn.silu(summed)
-    layer_out = (activated * row_gains).astype(jnp.bfloat16)
-
-    hidden_grad = jnp.concatenate([sum(wide(p) for p in ps) for ps in hidden_parts], axis=0)
-    feature_grad = lax.dot_general(
-        hidden_grad.astype(jnp.bfloat16),
-        weight,
-        (((0,), (1,)), ((), ())),
-        preferred_element_type=jnp.float32,
-    ).astype(jnp.bfloat16)
-
-    part_terms = jnp.dot(
-        member.T, wide(cotangent) * activated, precision=lax.Precision.HIGHEST
-    )
-    part_sizes = jnp.broadcast_to(jnp.sum(member, axis=0)[:, None], (member.shape[1], width))
-    totals = jnp.concatenate(weight_parts + [part_terms, part_sizes], axis=0)
-    for bit in col_bits[1:] + col_bits[:1]:
-        totals = totals + swap(totals, "col", bit, col_count)
-    for bit in bits_of(row_count):
-        totals = totals + swap(totals, "row", bit, row_count)
-    total_nodes = share * row_count * col_count
-    weight_grad = totals[:width].T / jnp.sqrt(jnp.float32(total_nodes))
-    part_count = member.shape[1]
-    gain_grad = totals[width : width + part_count] / jnp.sqrt(totals[width + part_count :])
+            if last is not None:
+                out = after(out, last)
+            last = out
+            arrived[n].append(swap(out, "col", bit, col_count))
+            rests[n] = rest[half:]
+    gated = []
+    for n in chunks:
+        up = after(upstream, gated[-1][0]) if n else upstream
+        gated.append(gate(n, up, weight, [rests[n]] + arrived[n]))
+    held, orders = [[g[0]] for g in gated], [[0]]
+    for bit in reversed(col_bits[1:]):
+        last = None
+        for n in chunks:
+            sent = held[n][0] if len(orders) == 1 else jnp.concatenate(held[n][::-1], axis=0)
+            if last is not None:
+                sent = after(sent, last)
+            last = sent
+            held[n].append(swap(sent, "col", bit, col_count))
+        orders.append([k ^ bit for o in orders[::-1] for k in o])
+
+    layer_out, message, out = local_terms(
+        at, members, row_gains, cotangent, [(rows, grad, summed) for _, grad, rows, summed in gated]
+    )
+    stages = [("col", col_bits[0], col_count)]
+    stages += [("row", bit, row_count) for bit in bits_of(row_count)]
+    stages += [("col", bit, col_count) for bit in col_bits[1:]]
+    for stage in stages:
+        message = add_messages(part_count, message, swap(out, *stage))
+        out = message
+    other = swap(message, "col", col_bits[0], col_count)
+    scale = 1.0 / math.sqrt(share * row_count * col_count)
+    weight_grad, gain_grad = totals(part_count, scale, at, message, other)
+
+    parts = []
+    bit = col_bits[0]
+    piece_orders = orders + [[k ^ bit for k in o] for o in orders]
+    for n in chunks:
+        pieces = held[n] + [swap(h, "col", bit, col_count) for h in held[n]]
+        parts = backward(n, at, tile, pieces, piece_orders, parts, share, row_count)
+    parts = [p if r == 0 else swap(p, "row", r, row_count) for r, p in enumerate(parts)]
+    feature_grad = finish(parts)
+
     return (layer_out, feature_grad, weight_grad, gain_grad)
 
 

time: 141 us -> 99.3 us (0.70)
  waiting for transfers between devices: 69.3 us -> 34.1 us
  local copies, waits for them, and re-layouts: 5.65 us -> 1.69 us
    ppermute x30 -> x28, waiting for transfers between devices: 69.3 us -> 34.1 us  [swap(): return lax.ppermute(values, axis, [(d, d ^ mask) for d in range(count)])]
    unnamed x13 -> x11, local copies, waits for them, and re-layouts: 5.44 us -> 0.03 us
    pallas_call x3 -> x14, Pallas kernels: 13.4 us -> 17.1 us  [the longest x2 6.54 us: backward(): pl.pallas_call(functools.partial(backward_kernel, orders, row_count, chun...]
    pallas_call x1, Pallas kernels: 6.4 us -> 3.91 us  [build_tile(): pl.pallas_call(build_kernel, out_shape=pltpu.VMEM((row_blocks * BLOCK, co...]
    squeeze x0 -> x2, local copies, waits for them, and re-layouts: none -> 1.63 us  [dense_device(): rows, cols = (block_rows[0, 0], block_cols[0, 0])]
    ppermute x30 -> x28, starting transfers between devices: 38.8 us -> 38.3 us  [swap(): return lax.ppermute(values, axis, [(d, d ^ mask) for d in range(count)])]
  transfers between devices with their start and end apart: 30 -> 28, of which waited for: 15 -> 12; matrix products, arithmetic and copies ran while one was open for 3% -> 5% of each run, Pallas kernels for 7% -> 17%
where the time goes in v2:
time: 99.3 us; the launch traced here: 99.9 us
  starting transfers between devices  38.3 us (39%)
  waiting for transfers between devices  34.1 us (34%)
  Pallas kernels  21 us (21%)
  other arithmetic  2.87 us (3%)
  local copies, waits for them, and re-layouts  1.69 us (2%)
  between operations  1.53 us (2%)
    ppermute x28, starting transfers between devices, swap(): return lax.ppermute(values, axis, [(d, d ^ mask) for d in range(count)])  38.3 us
    ppermute x28, waiting for transfers between devices, swap(): return lax.ppermute(values, axis, [(d, d ^ mask) for d in range(count)])  34.1 us
    pallas_call x2, Pallas kernels, backward(): pl.pallas_call(functools.partial(backward_kernel, orders, row_count, chun...  6.54 us
    pallas_call x2, Pallas kernels, forward(): pl.pallas_call(functools.partial(forward_kernel, order, chunk), out_shape...  5.95 us
    pallas_call x1, Pallas kernels, build_tile(): pl.pallas_call(build_kernel, out_shape=pltpu.VMEM((row_blocks * BLOCK, co...  3.91 us
  transfers between devices with their start and end apart: 28, of which 12 were waited for; matrix products, arithmetic and copies ran while one was open for 5% of the time, Pallas kernels for 17%

profile of v2, /device:TPU:0, one launch (start us, length us, event | category | flops | bytes accessed | tf_op | source)
XLA Modules:
  0.0 99.9 jit_solution(3379305614281616246)
XLA Ops:
  0.7 3.0 %collective-permute-start = (bf16[512,256]{1,0:T(8,128)(2,1)}, bf16[512,256]{1,0:T(8,128)(2,1)S(1)}, u32[]{:S(2)}, u32[]{:S(2)}) collective-permute-start(bf16[512,256]{1,0:T(8,128)(2,1)} %refs_0_.3), channel_id=1, source_target_pairs={{0,8},{8,0},{16,24},{24,16},{1,9},{9,1},{17,25},{25,17},{2,10},{10... | collective-permute-start | bytes 786440 | tf_op jit(solution)/shard_map/ppermute | solution.py:404
  3.7 1.5 %collective-permute-start.1 = (bf16[512,256]{1,0:T(8,128)(2,1)}, bf16[512,256]{1,0:T(8,128)(2,1)S(1)}, u32[]{:S(2)}, u32[]{:S(2)}) collective-permute-start(bf16[512,256]{1,0:T(8,128)(2,1)} %refs_0_.3), channel_id=1, source_target_pairs={{0,16},{8,24},{16,0},{24,8},{1,17},{9,25},{17,1},{25,9},{2,18},{10... | collective-permute-start | bytes 786440 | tf_op jit(solution)/shard_map/ppermute | solution.py:404
  5.2 0.7 reduce
  5.9 0.7 reduce.1.cols_ref
  6.6 0.7 bitcast_add_fusion.place_row_ref
  8.0 0.8 copy.23
  8.8 0.8 copy.18
  10.0 3.9 %build_tile.1.tile_ref = bf16[4096,2048]{1,0:T(8,128)(2,1)S(1)} custom-call(s32[1]{0:T(128)} %bitcast.22.live_ref, s32[384]{0:T(512)S(1)} %fusion.18.rows_ref, s32[384]{0:T(512)S(1)} %reduce.1.cols_ref, s32[1,384]{1,0:T(1,128)S(1)} %bitcast_add_fusion.place_row_ref, s32[384,1]{1,0:T(8,128)S(1)} %fusion.5.place_col_ref, bf16[384,128,128]{2,1,0:T(8,128)(2,1)} %bitcast.23), custom_call_target="tpu_custom_call" | custom-call | bytes 20971520 | tf_op jit(solution)/shard_map/build_tile/pallas_call | solution.py:117
  14.0 3.2 %collective-permute-done.1.refs_2_ = bf16[512,256]{1,0:T(8,128)(2,1)S(1)} collective-permute-done((bf16[512,256]{1,0:T(8,128)(2,1)}, bf16[512,256]{1,0:T(8,128)(2,1)S(1)}, u32[]{:S(2)}, u32[]{:S(2)}) %collective-permute-start.1) | collective-permute-done | bytes 262176 | tf_op jit(solution)/shard_map/ppermute | solution.py:404
  17.3 3.0 %forward.2 = (bf16[1024,256]{1,0:T(8,128)(2,1)S(1)}, bf16[1024,256]{1,0:T(8,128)(2,1)S(1)}) custom-call(s32[2]{0:T(128)S(1)} %pad_add_fusion.at_ref, bf16[4096,2048]{1,0:T(8,128)(2,1)S(1)} %build_tile.1.tile_ref, bf16[512,256]{1,0:T(8,128)(2,1)S(1)} %copy-done.1, bf16[512,256]{1,0:T(8,128)(2,1)S(1)} %collective-permute-done.refs_1_, ...), custom_call_target="tpu_custom_call" | custom-call | flops 2147483648 | tf_op jit(solution)/shard_map/forward/pallas_call | solution.py:156
  20.2 0.4 collective-permute-start.3
  20.7 3.0 %forward.3 = (bf16[1024,256]{1,0:T(8,128)(2,1)S(1)}, bf16[1024,256]{1,0:T(8,128)(2,1)S(1)}) custom-call(s32[2]{0:T(128)S(1)} %pad_add_fusion.at_ref, bf16[4096,2048]{1,0:T(8,128)(2,1)S(1)} %build_tile.1.tile_ref, bf16[512,256]{1,0:T(8,128)(2,1)S(1)} %copy-done.1, bf16[512,256]{1,0:T(8,128)(2,1)S(1)} %collective-permute-done.refs_1_, ...), custom_call_target="tpu_custom_call" | custom-call | flops 2147483648 | tf_op jit(solution)/shard_map/forward/pallas_call | solution.py:156
  23.9 2.0 %collective-permute-start.4 = (bf16[512,256]{1,0:T(8,128)(2,1)S(1)}, bf16[512,256]{1,0:T(8,128)(2,1)S(1)}, u32[]{:S(2)}, u32[]{:S(2)}) collective-permute-start(bf16[512,256]{1,0:T(8,128)(2,1)S(1)} %add_convert_fusion.1), channel_id=1, source_target_pairs={{0,2},{1,3},{2,0},{3,1},{4,6},{5,7},{6,4},{7,5},{8,10},{9,11},{10,... | collective-permute-start | bytes 786440 | tf_op jit(solution)/shard_map/ppermute | solution.py:404
  26.1 1.8 %collective-permute-start.7 = (bf16[512,256]{1,0:T(8,128)(2,1)S(1)}, bf16[512,256]{1,0:T(8,128)(2,1)S(1)}, u32[]{:S(2)}, u32[]{:S(2)}) collective-permute-start(bf16[512,256]{1,0:T(8,128)(2,1)S(1)} %add_convert_fusion), channel_id=1, source_target_pairs={{0,2},{1,3},{2,0},{3,1},{4,6},{5,7},{6,4},{7,5},{8,10},{9,11},{10,... | collective-permute-start | bytes 786440 | tf_op jit(solution)/shard_map/ppermute | solution.py:404
  27.9 5.3 %collective-permute-done.4.refs_2_ = bf16[512,256]{1,0:T(8,128)(2,1)S(1)} collective-permute-done((bf16[512,256]{1,0:T(8,128)(2,1)S(1)}, bf16[512,256]{1,0:T(8,128)(2,1)S(1)}, u32[]{:S(2)}, u32[]{:S(2)}) %collective-permute-start.4) | collective-permute-done | bytes 262176 | tf_op jit(solution)/shard_map/ppermute | solution.py:404
  33.2 4.3 %collective-permute-start.5 = (bf16[256,256]{1,0:T(8,128)(2,1)S(1)}, bf16[256,256]{1,0:T(8,128)(2,1)S(1)}, u32[]{:S(2)}, u32[]{:S(2)}) collective-permute-start(bf16[256,256]{1,0:T(8,128)(2,1)S(1)} %add_convert_fusion.3), channel_id=1, source_target_pairs={{0,4},{1,5},{2,6},{3,7},{4,0},{5,1},{6,2},{7,3},{8,12},{9,13},{10,... | collective-permute-start | bytes 393224 | tf_op jit(solution)/shard_map/ppermute | solution.py:404
  37.6 0.4 convert_multiply_fusion
  38.1 2.6 %collective-permute-done.5.refs_3_ = bf16[256,256]{1,0:T(8,128)(2,1)S(1)} collective-permute-done((bf16[256,256]{1,0:T(8,128)(2,1)S(1)}, bf16[256,256]{1,0:T(8,128)(2,1)S(1)}, u32[]{:S(2)}, u32[]{:S(2)}) %collective-permute-start.5) | collective-permute-done | bytes 131104 | tf_op jit(solution)/shard_map/ppermute | solution.py:404
  40.7 0.4 gate.2
  41.1 3.5 %collective-permute-start.10 = (bf16[256,256]{1,0:T(8,128)(2,1)S(1)}, bf16[256,256]{1,0:T(8,128)(2,1)S(1)}, u32[]{:S(2)}, u32[]{:S(2)}) collective-permute-start(bf16[256,256]{1,0:T(8,128)(2,1)S(1)} %get-tuple-element.39.refs_0_), channel_id=1, source_target_pairs={{0,4},{1,5},{2,6},{3,7},{4,0},{5,1},{6,2},{7,3},{8,12},{9,13},{10,... | collective-permute-start | bytes 393224 | tf_op jit(solution)/shard_map/ppermute | solution.py:404
  44.8 3.4 %collective-permute-done.10.refs_1_ = bf16[256,256]{1,0:T(8,128)(2,1)S(1)} collective-permute-done((bf16[256,256]{1,0:T(8,128)(2,1)S(1)}, bf16[256,256]{1,0:T(8,128)(2,1)S(1)}, u32[]{:S(2)}, u32[]{:S(2)}) %collective-permute-start.10) | collective-permute-done | bytes 131104 | tf_op jit(solution)/shard_map/ppermute | solution.py:404
  48.1 5.8 %collective-permute-start.15 = (bf16[512,256]{1,0:T(8,128)(2,1)S(1)}, bf16[512,256]{1,0:T(8,128)(2,1)S(1)}, u32[]{:S(2)}, u32[]{:S(2)}) collective-permute-start(bf16[512,256]{1,0:T(8,128)(2,1)S(1)} %constant_dynamic-update-slice_fusion), channel_id=1, source_target_pairs={{0,2},{1,3},{2,0},{3,1},{4,6},{5,7},{6,4},{7,5},{8,10},{9,11},{10,... | collective-permute-start | bytes 786440 | tf_op jit(solution)/shard_map/ppermute | solution.py:404
  53.9 2.1 %collective-permute-done.8.refs_3_ = bf16[256,256]{1,0:T(8,128)(2,1)S(1)} collective-permute-done((bf16[256,256]{1,0:T(8,128)(2,1)S(1)}, bf16[256,256]{1,0:T(8,128)(2,1)S(1)}, u32[]{:S(2)}, u32[]{:S(2)}) %collective-permute-start.8) | collective-permute-done | bytes 131104 | tf_op jit(solution)/shard_map/ppermute | solution.py:404
  56.1 0.4 gate.3
  56.5 1.3 %collective-permute-start.9 = (bf16[256,256]{1,0:T(8,128)(2,1)S(1)}, bf16[256,256]{1,0:T(8,128)(2,1)S(1)}, u32[]{:S(2)}, u32[]{:S(2)}) collective-permute-start(bf16[256,256]{1,0:T(8,128)(2,1)S(1)} %get-tuple-element.50.refs_0_), channel_id=1, source_target_pairs={{0,4},{1,5},{2,6},{3,7},{4,0},{5,1},{6,2},{7,3},{8,12},{9,13},{10,... | collective-permute-start | bytes 393224 | tf_op jit(solution)/shard_map/ppermute | solution.py:404
  57.8 4.7 %collective-permute-done.9.refs_1_ = bf16[256,256]{1,0:T(8,128)(2,1)S(1)} collective-permute-done((bf16[256,256]{1,0:T(8,128)(2,1)S(1)}, bf16[256,256]{1,0:T(8,128)(2,1)S(1)}, u32[]{:S(2)}, u32[]{:S(2)}) %collective-permute-start.9) | collective-permute-done | bytes 131104 | tf_op jit(solution)/shard_map/ppermute | solution.py:404
  62.5 4.1 %collective-permute-start.11 = (bf16[512,256]{1,0:T(8,128)(2,1)S(1)}, bf16[512,256]{1,0:T(8,128)(2,1)S(1)}, u32[]{:S(2)}, u32[]{:S(2)}) collective-permute-start(bf16[512,256]{1,0:T(8,128)(2,1)S(1)} %pad_maximum_fusion), channel_id=1, source_target_pairs={{0,2},{1,3},{2,0},{3,1},{4,6},{5,7},{6,4},{7,5},{8,10},{9,11},{10,... | collective-permute-start | bytes 786440 | tf_op jit(solution)/shard_map/ppermute | solution.py:404
  66.6 1.5 %local_terms.1 = (bf16[512,256]{1,0:T(8,128)(2,1)}, bf16[160,256]{1,0:T(8,128)(2,1)S(1)}, bf16[160,256]{1,0:T(8,128)(2,1)S(1)}) custom-call(s32[2]{0:T(128)S(1)} %pad_add_fusion.at_ref, f32[16,512]{1,0:T(8,128)S(1)} %fusion.13.members_ref, f32[512,256]{1,0:T(8,128)S(1)} %get-tuple-element.65.gains_ref, bf16[512,256]{1,0:T(8,128)(2,1)S(1)} %copy-done.2, ...), custom_call_target="tpu_custom_call" | custom-call | flops 268435456 | bytes 524288 | tf_op jit(solution)/shard_map/local_terms/pallas_call | solution.py:272
  68.1 0.5 collective-permute-start.22
  68.6 0.5 collective-permute-start.17
  69.1 0.4 collective-permute-done.22.other_ref
  69.6 0.8 collective-permute-start.23
  70.3 2.1 %collective-permute-done.11.refs_2_ = bf16[512,256]{1,0:T(8,128)(2,1)S(1)} collective-permute-done((bf16[512,256]{1,0:T(8,128)(2,1)S(1)}, bf16[512,256]{1,0:T(8,128)(2,1)S(1)}, u32[]{:S(2)}, u32[]{:S(2)}) %collective-permute-start.11) | collective-permute-done | bytes 262176 | tf_op jit(solution)/shard_map/ppermute | solution.py:404
  72.5 1.9 %collective-permute-done.23.other_ref = bf16[160,256]{1,0:T(8,128)(2,1)S(1)} collective-permute-done((bf16[160,256]{1,0:T(8,128)(2,1)S(1)}, bf16[160,256]{1,0:T(8,128)(2,1)S(1)}, u32[]{:S(2)}, u32[]{:S(2)}) %collective-permute-start.23) | collective-permute-done | bytes 81952 | tf_op jit(solution)/shard_map/ppermute | solution.py:404
  74.4 0.6 collective-permute-start.13
  75.0 0.4 collective-permute-start.24
  75.4 3.3 %backward.2 = (f32[256,512]{1,0:T(8,128)S(1)}, f32[256,512]{1,0:T(8,128)S(1)}, f32[256,512]{1,0:T(8,128)S(1)}, f32[256,512]{1,0:T(8,128)S(1)}) custom-call(s32[2]{0:T(128)S(1)} %pad_add_fusion.at_ref, bf16[4096,2048]{1,0:T(8,128)(2,1)S(1)} %build_tile.1.tile_ref, bf16[256,256]{1,0:T(8,128)(2,1)S(1)} %get-tuple-element.39.refs_0_, ...), custom_call_target="tpu_custom_call" | custom-call | flops 2147483648 | tf_op jit(solution)/shard_map/backward/pallas_call | solution.py:367
  78.7 3.3 %backward.3 = (f32[256,512]{1,0:T(8,128)S(1)}, bf16[256,512]{1,0:T(8,128)(2,1)S(1)}, bf16[256,512]{1,0:T(8,128)(2,1)S(1)}, bf16[256,512]{1,0:T(8,128)(2,1)S(1)}) custom-call(s32[2]{0:T(128)S(1)} %pad_add_fusion.at_ref, bf16[4096,2048]{1,0:T(8,128)(2,1)S(1)} %build_tile.1.tile_ref, bf16[256,256]{1,0:T(8,128)(2,1)S(1)} %get-tuple-element.50.refs_0_, ...), custom_call_target="tpu_custom_call" | custom-call | flops 2147483648 | tf_op jit(solution)/shard_map/backward/pallas_call | solution.py:367
  82.0 1.8 %collective-permute-start.19 = (bf16[256,512]{1,0:T(8,128)(2,1)S(1)}, bf16[256,512]{1,0:T(8,128)(2,1)S(1)}, u32[]{:S(2)}, u32[]{:S(2)}) collective-permute-start(bf16[256,512]{1,0:T(8,128)(2,1)S(1)} %get-tuple-element.57), channel_id=1, source_target_pairs={{0,8},{8,0},{16,24},{24,16},{1,9},{9,1},{17,25},{25,17},{2,10},{10... | collective-permute-start | bytes 786440 | tf_op jit(solution)/shard_map/ppermute | solution.py:404
  83.8 0.5 collective-permute-start.20
  84.3 1.2 %collective-permute-start.21 = (bf16[256,512]{1,0:T(8,128)(2,1)S(1)}, bf16[256,512]{1,0:T(8,128)(2,1)S(1)}, u32[]{:S(2)}, u32[]{:S(2)}) collective-permute-start(bf16[256,512]{1,0:T(8,128)(2,1)S(1)} %get-tuple-element.59), channel_id=1, source_target_pairs={{0,24},{8,16},{16,8},{24,0},{1,25},{9,17},{17,9},{25,1},{2,26},{10... | collective-permute-start | bytes 786440 | tf_op jit(solution)/shard_map/ppermute | solution.py:404
  85.6 1.1 %collective-permute-start.25 = (bf16[160,256]{1,0:T(8,128)(2,1)S(1)}, bf16[160,256]{1,0:T(8,128)(2,1)S(1)}, u32[]{:S(2)}, u32[]{:S(2)}) collective-permute-start(bf16[160,256]{1,0:T(8,128)(2,1)S(1)} %add_messages.7.own_ref), channel_id=1, source_target_pairs={{0,2},{1,3},{2,0},{3,1},{4,6},{5,7},{6,4},{7,5},{8,10},{9,11},{10,... | collective-permute-start | bytes 245768 | tf_op jit(solution)/shard_map/ppermute | solution.py:404
  86.7 3.4 %collective-permute-done.25.other_ref = bf16[160,256]{1,0:T(8,128)(2,1)S(1)} collective-permute-done((bf16[160,256]{1,0:T(8,128)(2,1)S(1)}, bf16[160,256]{1,0:T(8,128)(2,1)S(1)}, u32[]{:S(2)}, u32[]{:S(2)}) %collective-permute-start.25) | collective-permute-done | bytes 81952 | tf_op jit(solution)/shard_map/ppermute | solution.py:404
  90.1 2.7 %collective-permute-start.26 = (bf16[160,256]{1,0:T(8,128)(2,1)S(1)}, bf16[160,256]{1,0:T(8,128)(2,1)S(1)}, u32[]{:S(2)}, u32[]{:S(2)}) collective-permute-start(bf16[160,256]{1,0:T(8,128)(2,1)S(1)} %add_messages.8.own_ref), channel_id=1, source_target_pairs={{0,4},{1,5},{2,6},{3,7},{4,0},{5,1},{6,2},{7,3},{8,12},{9,13},{10,... | collective-permute-start | bytes 245768 | tf_op jit(solution)/shard_map/ppermute | solution.py:404
  92.8 3.6 %collective-permute-done.26.other_ref = bf16[160,256]{1,0:T(8,128)(2,1)S(1)} collective-permute-done((bf16[160,256]{1,0:T(8,128)(2,1)S(1)}, bf16[160,256]{1,0:T(8,128)(2,1)S(1)}, u32[]{:S(2)}, u32[]{:S(2)}) %collective-permute-start.26) | collective-permute-done | bytes 81952 | tf_op jit(solution)/shard_map/ppermute | solution.py:404
  96.5 1.3 %collective-permute-done.27.other_ref = bf16[160,256]{1,0:T(8,128)(2,1)S(1)} collective-permute-done((bf16[160,256]{1,0:T(8,128)(2,1)S(1)}, bf16[160,256]{1,0:T(8,128)(2,1)S(1)}, u32[]{:S(2)}, u32[]{:S(2)}) %collective-permute-start.27) | collective-permute-done | bytes 81952 | tf_op jit(solution)/shard_map/ppermute | solution.py:404
  97.8 1.3 %totals.1 = (f32[256,256]{1,0:T(8,128)}, f32[16,256]{1,0:T(8,128)}) custom-call(s32[2]{0:T(128)S(1)} %pad_add_fusion.at_ref, bf16[160,256]{1,0:T(8,128)(2,1)S(1)} %add_messages.9.own_ref, bf16[160,256]{1,0:T(8,128)(2,1)S(1)} %collective-permute-done.27.other_ref), custom_call_target="tpu_custom_call" | custom-call | tf_op jit(solution)/shard_map/totals/pallas_call | solution.py:323
  99.1 0.9 finish.1
  (52 shorter events, 1.4 us)
Async XLA Ops:
  0.6 37.0 %copy-start = (f32[16,256]{1,0:T(8,128)S(1)}, f32[16,256]{1,0:T(8,128)}, u32[]{:S(2)}) copy-start(f32[16,256]{1,0:T(8,128)} %param.15) | copy-start | bytes 49156
  0.6 16.6 %copy-start.1 = (bf16[512,256]{1,0:T(8,128)(2,1)S(1)}, bf16[512,256]{1,0:T(8,128)(2,1)}, u32[]{:S(2)}) copy-start(bf16[512,256]{1,0:T(8,128)(2,1)} %refs_0_.3) | copy-start | bytes 786436
  0.7 13.4 %collective-permute-start = (bf16[512,256]{1,0:T(8,128)(2,1)}, bf16[512,256]{1,0:T(8,128)(2,1)S(1)}, u32[]{:S(2)}, u32[]{:S(2)}) collective-permute-start(bf16[512,256]{1,0:T(8,128)(2,1)} %refs_0_.3), channel_id=1, source_target_pairs={{0,8},{8,0},{16,24},{24,16},{1,9},{9,1},{17,25},{25,17},{2,10},{10... | collective-permute-start | bytes 786440 | tf_op jit(solution)/shard_map/ppermute | solution.py:404
  3.7 13.6 %collective-permute-start.1 = (bf16[512,256]{1,0:T(8,128)(2,1)}, bf16[512,256]{1,0:T(8,128)(2,1)S(1)}, u32[]{:S(2)}, u32[]{:S(2)}) collective-permute-start(bf16[512,256]{1,0:T(8,128)(2,1)} %refs_0_.3), channel_id=1, source_target_pairs={{0,16},{8,24},{16,0},{24,8},{1,17},{9,25},{17,1},{25,9},{2,18},{10... | collective-permute-start | bytes 786440 | tf_op jit(solution)/shard_map/ppermute | solution.py:404
  5.2 12.1 %collective-permute-start.2 = (bf16[512,256]{1,0:T(8,128)(2,1)}, bf16[512,256]{1,0:T(8,128)(2,1)S(1)}, u32[]{:S(2)}, u32[]{:S(2)}) collective-permute-start(bf16[512,256]{1,0:T(8,128)(2,1)} %refs_0_.3), channel_id=1, source_target_pairs={{0,24},{8,16},{16,8},{24,0},{1,25},{9,17},{17,9},{25,1},{2,26},{10... | collective-permute-start | bytes 786440 | tf_op jit(solution)/shard_map/ppermute | solution.py:404
  14.0 23.6 %copy-start.2 = (bf16[512,256]{1,0:T(8,128)(2,1)S(1)}, bf16[512,256]{1,0:T(8,128)(2,1)}, u32[]{:S(2)}) copy-start(bf16[512,256]{1,0:T(8,128)(2,1)} %cotangent_ref.1) | copy-start | bytes 786436
  14.0 23.6 %copy-start.4 = (s32[512]{0:T(512)S(1)}, s32[512]{0:T(512)}, u32[]{:S(2)}) copy-start(s32[512]{0:T(512)} %param.16) | copy-start | bytes 6148
  14.0 26.6 %copy-start.3 = (bf16[256,256]{1,0:T(8,128)(2,1)S(1)}, bf16[256,256]{1,0:T(8,128)(2,1)}, u32[]{:S(2)}) copy-start(bf16[256,256]{1,0:T(8,128)(2,1)} %weight_ref.3) | copy-start | bytes 393220
  20.2 3.6 %collective-permute-start.3 = (bf16[1024,256]{1,0:T(8,128)(2,1)S(1)}, bf16[1024,256]{1,0:T(8,128)(2,1)S(1)}, u32[]{:S(2)}, u32[]{:S(2)}) collective-permute-start(bf16[1024,256]{1,0:T(8,128)(2,1)S(1)} %get-tuple-element.35), channel_id=1, source_target_pairs={{0,1},{1,0},{2,3},{3,2},{4,5},{5,4},{6,7},{7,6},{8,9},{9,8},{10,11... | collective-permute-start | bytes 1572872 | tf_op jit(solution)/shard_map/ppermute | solution.py:404
  23.6 2.4 %collective-permute-start.6 = (bf16[1024,256]{1,0:T(8,128)(2,1)S(1)}, bf16[1024,256]{1,0:T(8,128)(2,1)S(1)}, u32[]{:S(2)}, u32[]{:S(2)}) collective-permute-start(bf16[1024,256]{1,0:T(8,128)(2,1)S(1)} %get-tuple-element.42), channel_id=1, source_target_pairs={{0,1},{1,0},{2,3},{3,2},{4,5},{5,4},{6,7},{7,6},{8,9},{9,8},{10,11... | collective-permute-start | bytes 1572872 | tf_op jit(solution)/shard_map/ppermute | solution.py:404
  23.9 9.2 %collective-permute-start.4 = (bf16[512,256]{1,0:T(8,128)(2,1)S(1)}, bf16[512,256]{1,0:T(8,128)(2,1)S(1)}, u32[]{:S(2)}, u32[]{:S(2)}) collective-permute-start(bf16[512,256]{1,0:T(8,128)(2,1)S(1)} %add_convert_fusion.1), channel_id=1, source_target_pairs={{0,2},{1,3},{2,0},{3,1},{4,6},{5,7},{6,4},{7,5},{8,10},{9,11},{10,... | collective-permute-start | bytes 786440 | tf_op jit(solution)/shard_map/ppermute | solution.py:404
  26.1 18.5 %collective-permute-start.7 = (bf16[512,256]{1,0:T(8,128)(2,1)S(1)}, bf16[512,256]{1,0:T(8,128)(2,1)S(1)}, u32[]{:S(2)}, u32[]{:S(2)}) collective-permute-start(bf16[512,256]{1,0:T(8,128)(2,1)S(1)} %add_convert_fusion), channel_id=1, source_target_pairs={{0,2},{1,3},{2,0},{3,1},{4,6},{5,7},{6,4},{7,5},{8,10},{9,11},{10,... | collective-permute-start | bytes 786440 | tf_op jit(solution)/shard_map/ppermute | solution.py:404
  33.2 7.4 %collective-permute-start.5 = (bf16[256,256]{1,0:T(8,128)(2,1)S(1)}, bf16[256,256]{1,0:T(8,128)(2,1)S(1)}, u32[]{:S(2)}, u32[]{:S(2)}) collective-permute-start(bf16[256,256]{1,0:T(8,128)(2,1)S(1)} %add_convert_fusion.3), channel_id=1, source_target_pairs={{0,4},{1,5},{2,6},{3,7},{4,0},{5,1},{6,2},{7,3},{8,12},{9,13},{10,... | collective-permute-start | bytes 393224 | tf_op jit(solution)/shard_map/ppermute | solution.py:404
  41.1 7.0 %collective-permute-start.10 = (bf16[256,256]{1,0:T(8,128)(2,1)S(1)}, bf16[256,256]{1,0:T(8,128)(2,1)S(1)}, u32[]{:S(2)}, u32[]{:S(2)}) collective-permute-start(bf16[256,256]{1,0:T(8,128)(2,1)S(1)} %get-tuple-element.39.refs_0_), channel_id=1, source_target_pairs={{0,4},{1,5},{2,6},{3,7},{4,0},{5,1},{6,2},{7,3},{8,12},{9,13},{10,... | collective-permute-start | bytes 393224 | tf_op jit(solution)/shard_map/ppermute | solution.py:404
  44.7 11.4 %collective-permute-start.8 = (bf16[256,256]{1,0:T(8,128)(2,1)S(1)}, bf16[256,256]{1,0:T(8,128)(2,1)S(1)}, u32[]{:S(2)}, u32[]{:S(2)}) collective-permute-start(bf16[256,256]{1,0:T(8,128)(2,1)S(1)} %add_convert_fusion.2), channel_id=1, source_target_pairs={{0,4},{1,5},{2,6},{3,7},{4,0},{5,1},{6,2},{7,3},{8,12},{9,13},{10,... | collective-permute-start | bytes 393224 | tf_op jit(solution)/shard_map/ppermute | solution.py:404
  48.1 18.5 %collective-permute-start.15 = (bf16[512,256]{1,0:T(8,128)(2,1)S(1)}, bf16[512,256]{1,0:T(8,128)(2,1)S(1)}, u32[]{:S(2)}, u32[]{:S(2)}) collective-permute-start(bf16[512,256]{1,0:T(8,128)(2,1)S(1)} %constant_dynamic-update-slice_fusion), channel_id=1, source_target_pairs={{0,2},{1,3},{2,0},{3,1},{4,6},{5,7},{6,4},{7,5},{8,10},{9,11},{10,... | collective-permute-start | bytes 786440 | tf_op jit(solution)/shard_map/ppermute | solution.py:404
  56.5 6.0 %collective-permute-start.9 = (bf16[256,256]{1,0:T(8,128)(2,1)S(1)}, bf16[256,256]{1,0:T(8,128)(2,1)S(1)}, u32[]{:S(2)}, u32[]{:S(2)}) collective-permute-start(bf16[256,256]{1,0:T(8,128)(2,1)S(1)} %get-tuple-element.50.refs_0_), channel_id=1, source_target_pairs={{0,4},{1,5},{2,6},{3,7},{4,0},{5,1},{6,2},{7,3},{8,12},{9,13},{10,... | collective-permute-start | bytes 393224 | tf_op jit(solution)/shard_map/ppermute | solution.py:404
  62.5 9.9 %collective-permute-start.11 = (bf16[512,256]{1,0:T(8,128)(2,1)S(1)}, bf16[512,256]{1,0:T(8,128)(2,1)S(1)}, u32[]{:S(2)}, u32[]{:S(2)}) collective-permute-start(bf16[512,256]{1,0:T(8,128)(2,1)S(1)} %pad_maximum_fusion), channel_id=1, source_target_pairs={{0,2},{1,3},{2,0},{3,1},{4,6},{5,7},{6,4},{7,5},{8,10},{9,11},{10,... | collective-permute-start | bytes 786440 | tf_op jit(solution)/shard_map/ppermute | solution.py:404
  66.6 8.8 %collective-permute-start.18 = (bf16[512,256]{1,0:T(8,128)(2,1)S(1)}, bf16[512,256]{1,0:T(8,128)(2,1)S(1)}, u32[]{:S(2)}, u32[]{:S(2)}) collective-permute-start(bf16[512,256]{1,0:T(8,128)(2,1)S(1)} %collective-permute-done.15.refs_2_), channel_id=1, source_target_pairs={{0,1},{1,0},{2,3},{3,2},{4,5},{5,4},{6,7},{7,6},{8,9},{9,8},{10,11... | collective-permute-start | bytes 786440 | tf_op jit(solution)/shard_map/ppermute | solution.py:404
  68.1 1.4 %collective-permute-start.22 = (bf16[160,256]{1,0:T(8,128)(2,1)S(1)}, bf16[160,256]{1,0:T(8,128)(2,1)S(1)}, u32[]{:S(2)}, u32[]{:S(2)}) collective-permute-start(bf16[160,256]{1,0:T(8,128)(2,1)S(1)} %get-tuple-element.61), channel_id=1, source_target_pairs={{0,1},{1,0},{2,3},{3,2},{4,5},{5,4},{6,7},{7,6},{8,9},{9,8},{10,11... | collective-permute-start | bytes 245768 | tf_op jit(solution)/shard_map/ppermute | solution.py:404
  68.6 5.8 %collective-permute-start.16 = (bf16[256,256]{1,0:T(8,128)(2,1)S(1)}, bf16[256,256]{1,0:T(8,128)(2,1)S(1)}, u32[]{:S(2)}, u32[]{:S(2)}) collective-permute-start(bf16[256,256]{1,0:T(8,128)(2,1)S(1)} %get-tuple-element.39.refs_0_), channel_id=1, source_target_pairs={{0,1},{1,0},{2,3},{3,2},{4,5},{5,4},{6,7},{7,6},{8,9},{9,8},{10,11... | collective-permute-start | bytes 393224 | tf_op jit(solution)/shard_map/ppermute | solution.py:404
  68.6 6.3 %collective-permute-start.17 = (bf16[256,256]{1,0:T(8,128)(2,1)S(1)}, bf16[256,256]{1,0:T(8,128)(2,1)S(1)}, u32[]{:S(2)}, u32[]{:S(2)}) collective-permute-start(bf16[256,256]{1,0:T(8,128)(2,1)S(1)} %collective-permute-done.10.refs_1_), channel_id=1, source_target_pairs={{0,1},{1,0},{2,3},{3,2},{4,5},{5,4},{6,7},{7,6},{8,9},{9,8},{10,11... | collective-permute-start | bytes 393224 | tf_op jit(solution)/shard_map/ppermute | solution.py:404
  69.6 4.8 %collective-permute-start.23 = (bf16[160,256]{1,0:T(8,128)(2,1)S(1)}, bf16[160,256]{1,0:T(8,128)(2,1)S(1)}, u32[]{:S(2)}, u32[]{:S(2)}) collective-permute-start(bf16[160,256]{1,0:T(8,128)(2,1)S(1)} %add_messages.5.own_ref), channel_id=1, source_target_pairs={{0,8},{8,0},{16,24},{24,16},{1,9},{9,1},{17,25},{25,17},{2,10},{10... | collective-permute-start | bytes 245768 | tf_op jit(solution)/shard_map/ppermute | solution.py:404
  72.5 6.2 %collective-permute-start.14 = (bf16[512,256]{1,0:T(8,128)(2,1)S(1)}, bf16[512,256]{1,0:T(8,128)(2,1)S(1)}, u32[]{:S(2)}, u32[]{:S(2)}) collective-permute-start(bf16[512,256]{1,0:T(8,128)(2,1)S(1)} %collective-permute-done.11.refs_2_), channel_id=1, source_target_pairs={{0,1},{1,0},{2,3},{3,2},{4,5},{5,4},{6,7},{7,6},{8,9},{9,8},{10,11... | collective-permute-start | bytes 786440 | tf_op jit(solution)/shard_map/ppermute | solution.py:404
  74.3 4.3 %collective-permute-start.12 = (bf16[256,256]{1,0:T(8,128)(2,1)S(1)}, bf16[256,256]{1,0:T(8,128)(2,1)S(1)}, u32[]{:S(2)}, u32[]{:S(2)}) collective-permute-start(bf16[256,256]{1,0:T(8,128)(2,1)S(1)} %get-tuple-element.50.refs_0_), channel_id=1, source_target_pairs={{0,1},{1,0},{2,3},{3,2},{4,5},{5,4},{6,7},{7,6},{8,9},{9,8},{10,11... | collective-permute-start | bytes 393224 | tf_op jit(solution)/shard_map/ppermute | solution.py:404
  74.4 4.3 %collective-permute-start.13 = (bf16[256,256]{1,0:T(8,128)(2,1)S(1)}, bf16[256,256]{1,0:T(8,128)(2,1)S(1)}, u32[]{:S(2)}, u32[]{:S(2)}) collective-permute-start(bf16[256,256]{1,0:T(8,128)(2,1)S(1)} %collective-permute-done.9.refs_1_), channel_id=1, source_target_pairs={{0,1},{1,0},{2,3},{3,2},{4,5},{5,4},{6,7},{7,6},{8,9},{9,8},{10,11... | collective-permute-start | bytes 393224 | tf_op jit(solution)/shard_map/ppermute | solution.py:404
  75.0 10.6 %collective-permute-start.24 = (bf16[160,256]{1,0:T(8,128)(2,1)S(1)}, bf16[160,256]{1,0:T(8,128)(2,1)S(1)}, u32[]{:S(2)}, u32[]{:S(2)}) collective-permute-start(bf16[160,256]{1,0:T(8,128)(2,1)S(1)} %add_messages.6.own_ref), channel_id=1, source_target_pairs={{0,16},{8,24},{16,0},{24,8},{1,17},{9,25},{17,1},{25,9},{2,18},{10... | collective-permute-start | bytes 245768 | tf_op jit(solution)/shard_map/ppermute | solution.py:404
  82.0 17.0 %collective-permute-start.19 = (bf16[256,512]{1,0:T(8,128)(2,1)S(1)}, bf16[256,512]{1,0:T(8,128)(2,1)S(1)}, u32[]{:S(2)}, u32[]{:S(2)}) collective-permute-start(bf16[256,512]{1,0:T(8,128)(2,1)S(1)} %get-tuple-element.57), channel_id=1, source_target_pairs={{0,8},{8,0},{16,24},{24,16},{1,9},{9,1},{17,25},{25,17},{2,10},{10... | collective-permute-start | bytes 786440 | tf_op jit(solution)/shard_map/ppermute | solution.py:404
  83.8 15.3 %collective-permute-start.20 = (bf16[256,512]{1,0:T(8,128)(2,1)S(1)}, bf16[256,512]{1,0:T(8,128)(2,1)S(1)}, u32[]{:S(2)}, u32[]{:S(2)}) collective-permute-start(bf16[256,512]{1,0:T(8,128)(2,1)S(1)} %get-tuple-element.58), channel_id=1, source_target_pairs={{0,16},{8,24},{16,0},{24,8},{1,17},{9,25},{17,1},{25,9},{2,18},{10... | collective-permute-start | bytes 786440 | tf_op jit(solution)/shard_map/ppermute | solution.py:404
  84.3 14.7 %collective-permute-start.21 = (bf16[256,512]{1,0:T(8,128)(2,1)S(1)}, bf16[256,512]{1,0:T(8,128)(2,1)S(1)}, u32[]{:S(2)}, u32[]{:S(2)}) collective-permute-start(bf16[256,512]{1,0:T(8,128)(2,1)S(1)} %get-tuple-element.59), channel_id=1, source_target_pairs={{0,24},{8,16},{16,8},{24,0},{1,25},{9,17},{17,9},{25,1},{2,26},{10... | collective-permute-start | bytes 786440 | tf_op jit(solution)/shard_map/ppermute | solution.py:404
  85.6 4.5 %collective-permute-start.25 = (bf16[160,256]{1,0:T(8,128)(2,1)S(1)}, bf16[160,256]{1,0:T(8,128)(2,1)S(1)}, u32[]{:S(2)}, u32[]{:S(2)}) collective-permute-start(bf16[160,256]{1,0:T(8,128)(2,1)S(1)} %add_messages.7.own_ref), channel_id=1, source_target_pairs={{0,2},{1,3},{2,0},{3,1},{4,6},{5,7},{6,4},{7,5},{8,10},{9,11},{10,... | collective-permute-start | bytes 245768 | tf_op jit(solution)/shard_map/ppermute | solution.py:404
  90.1 6.3 %collective-permute-start.26 = (bf16[160,256]{1,0:T(8,128)(2,1)S(1)}, bf16[160,256]{1,0:T(8,128)(2,1)S(1)}, u32[]{:S(2)}, u32[]{:S(2)}) collective-permute-start(bf16[160,256]{1,0:T(8,128)(2,1)S(1)} %add_messages.8.own_ref), channel_id=1, source_target_pairs={{0,4},{1,5},{2,6},{3,7},{4,0},{5,1},{6,2},{7,3},{8,12},{9,13},{10,... | collective-permute-start | bytes 245768 | tf_op jit(solution)/shard_map/ppermute | solution.py:404
  96.4 1.3 %collective-permute-start.27 = (bf16[160,256]{1,0:T(8,128)(2,1)S(1)}, bf16[160,256]{1,0:T(8,128)(2,1)S(1)}, u32[]{:S(2)}, u32[]{:S(2)}) collective-permute-start(bf16[160,256]{1,0:T(8,128)(2,1)S(1)} %add_messages.9.own_ref), channel_id=1, source_target_pairs={{0,1},{1,0},{2,3},{3,2},{4,5},{5,4},{6,7},{7,6},{8,9},{9,8},{10,11... | collective-permute-start | bytes 245768 | tf_op jit(solution)/shard_map/ppermute | solution.py:404

commit v3 on v2

--- a/solution.py
+++ b/solution.py
@@ -14,6 +14,7 @@
 HEAVY = 16
 CHUNKS = 2
 MIB = 1 << 20
+LIGHT = pl.CostEstimate(flops=1, bytes_accessed=1, transcendentals=0)
 
 
 def bits_of(count):
@@ -27,16 +28,21 @@
     return [k ^ 1 for k in evens] + evens
 
 
+def shift_of(count):
+    return count.bit_length() - 1
+
+
 def build_kernel(
-    live_ref, rows_ref, cols_ref, place_row_ref, place_col_ref, slots_ref, tile_ref, buf, total, counts, sems
+    layout, live_ref, rows_ref, cols_ref, row_lane_ref, col_lane_ref, slots_ref, tile_ref, buf, total, counts, sems
 ):
-    live = live_ref[0]
+    owners, per_owner, per_chunk = layout
+    live = live_ref[0, 0]
     groups = (live + GROUP - 1) // GROUP
     col_blocks = tile_ref.shape[1] // BLOCK
 
     def fetch(group, slot):
         return pltpu.make_async_copy(
-            slots_ref.at[pl.ds(group * GROUP, GROUP)], buf.at[slot], sems.at[slot]
+            slots_ref.at[0, 0, pl.ds(group * GROUP, GROUP)], buf.at[slot], sems.at[slot]
         )
 
     for b in range(BUFFERS):
@@ -50,9 +56,20 @@
     def _(r):
         tile_ref[pl.ds(pl.multiple_of(r * BLOCK, BLOCK), BLOCK), :] = zeros
 
+    lane_places = row_lane_ref[0] * col_blocks + col_lane_ref[0]
+    slot_total = lane_places.shape[1]
+    places = jnp.broadcast_to(lane_places.astype(jnp.float32), (BLOCK, slot_total))
+    live_lanes = lax.broadcasted_iota(jnp.int32, (1, slot_total), 1) < live
+    same = jnp.where((places.T[:, :1] == places[:1, :]) & live_lanes, 1.0, 0.0)
+    most = jnp.max(jnp.sum(same, axis=1, keepdims=True))
+
     def place(index):
-        top = pl.multiple_of(rows_ref[index] * BLOCK, BLOCK)
-        left = pl.multiple_of(cols_ref[index] * BLOCK, BLOCK)
+        row = rows_ref[0, 0, index]
+        owner, inner = row >> shift_of(per_owner), row & (per_owner - 1)
+        chunk, inner = inner >> shift_of(per_chunk), inner & (per_chunk - 1)
+        row = (chunk * owners + owner) * per_chunk + inner
+        top = pl.multiple_of(row * BLOCK, BLOCK)
+        left = pl.multiple_of(cols_ref[0, 0, index] * BLOCK, BLOCK)
         return pl.ds(top, BLOCK), pl.ds(left, BLOCK)
 
     @pl.loop(0, groups)
@@ -60,21 +77,24 @@
         slot = lax.rem(group, BUFFERS)
         fetch(group, slot).wait()
 
-        @pl.loop(0, jnp.minimum(GROUP, live - group * GROUP))
-        def _(s):
+        def add(s):
             at = place(group * GROUP + s)
             tile_ref[at] += buf[slot, s]
+
+        here = live - group * GROUP
+
+        @pl.when(here >= GROUP)
+        def _():
+            for s in range(GROUP):
+                add(s)
+
+        @pl.when(here < GROUP)
+        def _():
+            pl.loop(0, here)(add)
 
         @pl.when(group + BUFFERS < groups)
         def _():
             fetch(group + BUFFERS, slot).start()
-
-    slot_total = place_row_ref.shape[1]
-    live_here = lax.broadcasted_iota(jnp.int32, (1, slot_total), 1) < live
-    same = jnp.where(
-        (place_row_ref[...] == place_col_ref[...]) & live_here, 1.0, 0.0
-    )
-    most = jnp.max(jnp.sum(same, axis=1, keepdims=True))
 
     @pl.when(most > HEAVY)
     def _():
@@ -84,12 +104,12 @@
 
         @pl.loop(0, live)
         def _(index):
-            p = rows_ref[index] * col_blocks + cols_ref[index]
+            p = rows_ref[0, 0, index] * col_blocks + cols_ref[0, 0, index]
             counts[p] = counts[p] + 1
 
         @pl.loop(0, live)
         def _(index):
-            p = rows_ref[index] * col_blocks + cols_ref[index]
+            p = rows_ref[0, 0, index] * col_blocks + cols_ref[0, 0, index]
 
             @pl.when(counts[p] > HEAVY)
             def _():
@@ -98,10 +118,10 @@
 
                 @pl.loop(index, live)
                 def _(other):
-                    @pl.when(rows_ref[other] * col_blocks + cols_ref[other] == p)
+                    @pl.when(rows_ref[0, 0, other] * col_blocks + cols_ref[0, 0, other] == p)
                     def _():
                         copy = pltpu.make_async_copy(
-                            slots_ref.at[pl.ds(other, 1)], buf.at[0, pl.ds(0, 1)], sems.at[0]
+                            slots_ref.at[0, 0, pl.ds(other, 1)], buf.at[0, pl.ds(0, 1)], sems.at[0]
                         )
                         copy.start()
                         copy.wait()
@@ -110,12 +130,11 @@
                 tile_ref[place(index)] = total[...].astype(tile_ref.dtype)
 
 
-def build_tile(slots, rows, cols, live, row_blocks, col_blocks):
-    places = rows * col_blocks + cols
+def build_tile(slots, rows, cols, live, row_blocks, col_blocks, layout):
     smem = pl.BlockSpec(memory_space=pltpu.SMEM)
     vmem = pl.BlockSpec(memory_space=pltpu.VMEM)
     return pl.pallas_call(
-        build_kernel,
+        functools.partial(build_kernel, layout),
         out_shape=pltpu.VMEM((row_blocks * BLOCK, col_blocks * BLOCK), jnp.bfloat16),
         in_specs=[smem, smem, smem, vmem, vmem, pl.BlockSpec(memory_space=pl.ANY)],
         out_specs=vmem,
@@ -128,7 +147,7 @@
         compiler_params=pltpu.CompilerParams(vmem_limit_bytes=36 * MIB),
         cost_estimate=pl.CostEstimate(flops=0, bytes_accessed=20 * MIB, transcendentals=0),
         name="build_tile",
-    )(live, rows, cols, places[None, :], places[:, None], slots)
+    )(live, rows, cols, rows, cols, slots)
 
 
 def forward_kernel(order, chunk, at_ref, tile_ref, *refs):
@@ -180,12 +199,38 @@
     return lax.dot_general(left, right, (((1,), (1,)), ((), ())), preferred_element_type=jnp.float32)
 
 
-def gate_kernel(chunk, upstream_ref, weight_ref, *refs):
+def combine_kernel(specs, *refs):
+    out_refs = refs[-len(specs) :]
+    for spec, out_ref in zip(specs, out_refs):
+        total = None
+        for source, start in spec:
+            term = wide(refs[source][start : start + out_ref.shape[0], :])
+            total = term if total is None else total + term
+        out_ref[...] = total.astype(out_ref.dtype)
+
+
+def combine(step, sums):
+    sources = list({id(x): x for terms in sums for x, _ in terms}.values())
+    at = {id(x): i for i, x in enumerate(sources)}
+    specs = [[(at[id(x)], start) for x, start in terms] for terms in sums]
+    vmem = pl.BlockSpec(memory_space=pltpu.VMEM)
+    return pl.pallas_call(
+        functools.partial(combine_kernel, specs),
+        out_shape=[pltpu.VMEM((step, sources[0].shape[1]), jnp.bfloat16)] * len(sums),
+        in_specs=[vmem] * len(sources),
+        out_specs=[vmem] * len(sums),
+        compiler_params=pltpu.CompilerParams(vmem_limit_bytes=4 * MIB),
+        cost_estimate=LIGHT,
+        name="combine",
+    )(*sources)
+
+
+def gate_kernel(chunk, starts, upstream_ref, weight_ref, *refs):
     *term_refs, turned_ref, grad_ref, rows_ref, summed_ref = refs
     step = grad_ref.shape[0]
     rows = None
-    for term_ref in term_refs:
-        term = wide(term_ref[term_ref.shape[0] - step :, :])
+    for term_ref, start in zip(term_refs, starts):
+        term = wide(term_ref[start : start + step, :])
         rows = term if rows is None else rows + term
     high = rows.astype(jnp.bfloat16)
     low = (rows - wide(high)).astype(jnp.bfloat16)
@@ -205,14 +250,14 @@
     shape = (upstream.shape[0] // CHUNKS, upstream.shape[1])
     vmem = pl.BlockSpec(memory_space=pltpu.VMEM)
     return pl.pallas_call(
-        functools.partial(gate_kernel, chunk),
+        functools.partial(gate_kernel, chunk, [start for _, start in terms]),
         out_shape=[pltpu.VMEM(shape, jnp.bfloat16)] * 3 + [pltpu.VMEM(shape, jnp.float32)],
         in_specs=[vmem] * (2 + len(terms)),
         out_specs=[vmem] * 4,
         compiler_params=pltpu.CompilerParams(vmem_limit_bytes=8 * MIB),
-        cost_estimate=pl.CostEstimate(flops=1 << 27, bytes_accessed=0, transcendentals=1 << 16),
+        cost_estimate=LIGHT,
         name="gate",
-    )(upstream, weight, *terms)
+    )(upstream, weight, *(x for x, _ in terms))
 
 
 def pack(values, exact_rows):
@@ -283,7 +328,7 @@
             pltpu.VMEM((2 * count, width), jnp.float32),
         ],
         compiler_params=pltpu.CompilerParams(vmem_limit_bytes=8 * MIB),
-        cost_estimate=pl.CostEstimate(flops=1 << 28, bytes_accessed=1 << 19, transcendentals=1 << 17),
+        cost_estimate=LIGHT,
         name="local_terms",
     )(at, members, gains, cotangent, *given)
 
@@ -302,6 +347,7 @@
         in_specs=[vmem] * 2,
         out_specs=vmem,
         compiler_params=pltpu.CompilerParams(vmem_limit_bytes=4 * MIB),
+        cost_estimate=LIGHT,
         name="add_messages",
     )(own, other)
 
@@ -330,6 +376,7 @@
         out_specs=[vmem] * 2,
         scratch_shapes=[pltpu.VMEM((2 * exact_rows, width), jnp.float32)],
         compiler_params=pltpu.CompilerParams(vmem_limit_bytes=4 * MIB),
+        cost_estimate=LIGHT,
         name="totals",
     )(at, own, other)
 
@@ -339,7 +386,7 @@
     before_refs, refs = refs[: row_count * (chunk > 0)], refs[row_count * (chunk > 0) :]
     *part_refs, turned = refs
     own_row, own_col = at_ref[0], at_ref[1]
-    step = turned.shape[1] // sum(len(o) for o in orders)
+    step = grad_refs[0].shape[0]
     for order, grad_ref in zip(orders, grad_refs):
         for t, k in enumerate(order):
             at = pl.ds(pl.multiple_of((own_col ^ k) * step, step), step)
@@ -372,7 +419,7 @@
         scratch_shapes=[pltpu.VMEM((width, tile.shape[0] // CHUNKS), jnp.bfloat16)],
         compiler_params=pltpu.CompilerParams(vmem_limit_bytes=8 * MIB),
         cost_estimate=pl.CostEstimate(
-            flops=2 * tile.shape[0] // CHUNKS * tile.shape[1] * width, bytes_accessed=0, transcendentals=0
+            flops=tile.shape[0] // CHUNKS * tile.shape[1] * width, bytes_accessed=0, transcendentals=0
         ),
         name="backward",
     )(at, tile, *grads, *before)
@@ -396,6 +443,7 @@
         in_specs=[vmem] * len(parts),
         out_specs=vmem,
         compiler_params=pltpu.CompilerParams(vmem_limit_bytes=8 * MIB),
+        cost_estimate=LIGHT,
         name="finish",
     )(*parts)
 
@@ -426,12 +474,9 @@
     row_blocks = share * col_count // BLOCK
     at = jnp.stack([lax.axis_index("row"), lax.axis_index("col")]).astype(jnp.int32)
     gathered = [features] + [swap(features, "row", r, row_count) for r in range(1, row_count)]
-    per_device, per_chunk = share // BLOCK, step // BLOCK
-    rows, cols = block_rows[0, 0], block_cols[0, 0]
-    owner, inner = rows // per_device, rows % per_device
-    rows = (inner // per_chunk * col_count + owner) * per_chunk + inner % per_chunk
+    layout = (col_count, share // BLOCK, step // BLOCK)
     tile = build_tile(
-        adjacency[0, 0], rows, cols, live_blocks[0], row_blocks, share * row_count // BLOCK
+        adjacency, block_rows, block_cols, live_blocks, row_blocks, share * row_count // BLOCK, layout
     )
     part_count = part_gains.shape[0]
     members = (
@@ -448,52 +493,65 @@
     sends, rests = zip(*(forward(n, at, tile, gathered, order) for n in chunks))
     sends, rests = list(sends), list(rests)
 
-    arrived = [[swap(send, "col", col_bits[0], col_count)] for send in sends]
+    pending = []
+    for n in chunks:
+        other = swap(sends[n], "col", col_bits[0], col_count)
+        kept = enumerate(order[len(order) // 2 :])
+        pending.append({k: [(rests[n], t * step), (other, t * step)] for t, k in kept})
+    last = None
     for bit in col_bits[1:]:
-        last = None
+        for terms in pending:
+            blocks = sorted((k for k in terms if k & bit), reverse=True)
+            sums = [terms.pop(k) for k in blocks]
+            if last is not None:
+                x, start = sums[0][-1]
+                sums[0][-1] = (after(x, last), start)
+            outs = combine(step, sums)
+            last = outs[0]
+            for k, out in zip(blocks, outs):
+                terms[k ^ bit].append((swap(out, "col", bit, col_count), 0))
+    gated, held = [], []
+    for n in chunks:
+        gated.append(gate(n, after(upstream, last), weight, pending[n][0]))
+        last = gated[-1][0]
+        held.append({0: last})
+    scale = 1.0 / math.sqrt(share * row_count * col_count)
+    messages = []
+    for bit in reversed(col_bits[1:]):
         for n in chunks:
-            rest = rests[n]
-            half = rest.shape[0] // 2
-            first = sum(wide(a[-2 * half :][:half]) for a in arrived[n])
-            out = (wide(rest[:half]) + first).astype(jnp.bfloat16)
-            if last is not None:
-                out = after(out, last)
-            last = out
-            arrived[n].append(swap(out, "col", bit, col_count))
-            rests[n] = rest[half:]
-    gated = []
-    for n in chunks:
-        up = after(upstream, gated[-1][0]) if n else upstream
-        gated.append(gate(n, up, weight, [rests[n]] + arrived[n]))
-    held, orders = [[g[0]] for g in gated], [[0]]
-    for bit in reversed(col_bits[1:]):
-        last = None
-        for n in chunks:
-            sent = held[n][0] if len(orders) == 1 else jnp.concatenate(held[n][::-1], axis=0)
-            if last is not None:
-                sent = after(sent, last)
-            last = sent
-            held[n].append(swap(sent, "col", bit, col_count))
-        orders.append([k ^ bit for o in orders[::-1] for k in o])
-
-    layer_out, message, out = local_terms(
-        at, members, row_gains, cotangent, [(rows, grad, summed) for _, grad, rows, summed in gated]
-    )
-    stages = [("col", col_bits[0], col_count)]
-    stages += [("row", bit, row_count) for bit in bits_of(row_count)]
+            for k in list(held[n]):
+                sent = held[n][k]
+                if k and n == 0:
+                    sent = last = after(sent, last)
+                if k and n:
+                    if not messages:
+                        ready = after(at, last)
+                        local = [(rows, grad, summed) for _, grad, rows, summed in gated]
+                        layer_out, message, out = local_terms(
+                            ready, members, row_gains, cotangent, local
+                        )
+                        message = add_messages(
+                            part_count, message, swap(out, "col", col_bits[0], col_count)
+                        )
+                        messages.append(message)
+                    sent = after(sent, messages[0], *held[n].values())
+                held[n][k ^ bit] = swap(sent, "col", bit, col_count)
+    stages = [("row", bit, row_count) for bit in bits_of(row_count)]
     stages += [("col", bit, col_count) for bit in col_bits[1:]]
     for stage in stages:
-        message = add_messages(part_count, message, swap(out, *stage))
-        out = message
+        message = add_messages(part_count, message, swap(message, *stage))
+        messages.append(message)
     other = swap(message, "col", col_bits[0], col_count)
-    scale = 1.0 / math.sqrt(share * row_count * col_count)
     weight_grad, gain_grad = totals(part_count, scale, at, message, other)
 
     parts = []
     bit = col_bits[0]
-    piece_orders = orders + [[k ^ bit for k in o] for o in orders]
     for n in chunks:
-        pieces = held[n] + [swap(h, "col", bit, col_count) for h in held[n]]
+        sent = jnp.concatenate(list(held[n].values()), axis=0)
+        if n:
+            sent = after(sent, messages[1])
+        pieces = list(held[n].values()) + [swap(sent, "col", bit, col_count)]
+        piece_orders = [[k] for k in held[n]] + [[k ^ bit for k in held[n]]]
         parts = backward(n, at, tile, pieces, piece_orders, parts, share, row_count)
     parts = [p if r == 0 else swap(p, "row", r, row_count) for r, p in enumerate(parts)]
     feature_grad = finish(parts)
@@ -577,8 +635,10 @@
     row_count, col_count = mesh.shape["row"], mesh.shape["col"]
 
     def per_device(features, *others):
-        tile_bytes = 2 * features.shape[0] ** 2 * row_count * col_count
-        if tile_bytes <= 20 * MIB:
+        share = features.shape[0]
+        tile_bytes = 2 * share**2 * row_count * col_count
+        sizes = (row_count, col_count, share // (BLOCK * CHUNKS))
+        if tile_bytes <= 20 * MIB and all(n & (n - 1) == 0 < n for n in sizes):
             return dense_device(row_count, col_count, features, *others)
         return slot_device(features, *others)
 

time: 99.3 us -> 91.5 us (0.921)
  waiting for transfers between devices: 34.1 us -> 29.2 us
  starting transfers between devices: 38.3 us -> 33.5 us
  Pallas kernels: 21 us -> 25.1 us
  other arithmetic: 2.87 us -> 0.15 us
    ppermute x28, waiting for transfers between devices: 34.1 us -> 29.2 us  [swap(): return lax.ppermute(values, axis, [(d, d ^ mask) for d in range(count)])]
    ppermute x28, starting transfers between devices: 38.3 us -> 33.5 us  [swap(): return lax.ppermute(values, axis, [(d, d ^ mask) for d in range(count)])]
    pallas_call x3 -> x7, Pallas kernels: 4.76 us -> 8.85 us  [the longest x1 7.78 us: build_tile(): pl.pallas_call(functools.partial(build_kernel, layout), out_shape=pltpu.V...]
    squeeze x2 -> x0, local copies, waits for them, and re-layouts: 1.63 us -> none  [dense_device(): rows, cols = (block_rows[0, 0], block_cols[0, 0])]
    unnamed x2 -> x0, other arithmetic: 1.4 us -> none
    unnamed x11 -> x14, local copies, waits for them, and re-layouts: 0.03 us -> 1.38 us
    add x3 -> x0, other arithmetic: 1.13 us -> none  [the longest x2 1.1 us: build_tile(): places = rows * col_blocks + cols]
  transfers between devices with their start and end apart: 28 -> 28, of which waited for: 12 -> 12; matrix products, arithmetic and copies ran while one was open for 5% -> 1% of each run, Pallas kernels for 17% -> 23%
where the time goes in v3:
time: 91.5 us; the launch traced here: 91.3 us
  starting transfers between devices  33.5 us (37%)
  waiting for transfers between devices  29.2 us (32%)
  Pallas kernels  25.1 us (27%)
  between operations  1.51 us (2%)
  local copies, waits for them, and re-layouts  1.38 us (2%)
    ppermute x28, starting transfers between devices, swap(): return lax.ppermute(values, axis, [(d, d ^ mask) for d in range(count)])  33.5 us
    ppermute x28, waiting for transfers between devices, swap(): return lax.ppermute(values, axis, [(d, d ^ mask) for d in range(count)])  29.2 us
    pallas_call x1, Pallas kernels, build_tile(): pl.pallas_call(functools.partial(build_kernel, layout), out_shape=pltpu.V...  7.78 us
    pallas_call x2, Pallas kernels, backward(): pl.pallas_call(functools.partial(backward_kernel, orders, row_count, chun...  6.48 us
    pallas_call x2, Pallas kernels, forward(): pl.pallas_call(functools.partial(forward_kernel, order, chunk), out_shape...  6.02 us
  transfers between devices with their start and end apart: 28, of which 12 were waited for; matrix products, arithmetic and copies ran while one was open for 1% of the time, Pallas kernels for 23%

profile of v3, /device:TPU:0, one launch (start us, length us, event | category | flops | bytes accessed | tf_op | source)
XLA Modules:
  0.0 91.3 jit_solution(433640779098467164)
XLA Ops:
  0.7 3.0 %collective-permute-start = (bf16[512,256]{1,0:T(8,128)(2,1)}, bf16[512,256]{1,0:T(8,128)(2,1)S(1)}, u32[]{:S(2)}, u32[]{:S(2)}) collective-permute-start(bf16[512,256]{1,0:T(8,128)(2,1)} %refs_0_.3), channel_id=1, source_target_pairs={{0,8},{8,0},{16,24},{24,16},{1,9},{9,1},{17,25},{25,17},{2,10},{10... | collective-permute-start | bytes 786440 | tf_op jit(solution)/shard_map/ppermute | solution.py:452
  3.7 1.5 %collective-permute-start.1 = (bf16[512,256]{1,0:T(8,128)(2,1)}, bf16[512,256]{1,0:T(8,128)(2,1)S(1)}, u32[]{:S(2)}, u32[]{:S(2)}) collective-permute-start(bf16[512,256]{1,0:T(8,128)(2,1)} %refs_0_.3), channel_id=1, source_target_pairs={{0,16},{8,24},{16,0},{24,8},{1,17},{9,25},{17,1},{25,9},{2,18},{10... | collective-permute-start | bytes 786440 | tf_op jit(solution)/shard_map/ppermute | solution.py:452
  5.9 0.7 copy-done.4
  6.5 0.7 copy-done.5
  7.2 7.8 %build_tile.1.tile_ref = bf16[4096,2048]{1,0:T(8,128)(2,1)S(1)} custom-call(s32[1,1]{1,0:T(1,128)S(6)} %copy.13.live_ref, s32[1,1,384]{2,1,0:T(1,128)S(1)} %copy-done.4, s32[1,1,384]{2,1,0:T(1,128)S(1)} %copy-done.5, s32[1,1,384]{2,1,0:T(1,128)S(1)} %copy-done.4, s32[1,1,384]{2,1,0:T(1,128)S(1)} %copy-done.5, bf16[1,1,384,128,128]{4,3,2,1,0:T(8,128)(2,1)} %slots_ref.1), custom_call_target="tpu_custom_call" | custom-call | bytes 20971520 | tf_op jit(solution)/shard_map/build_tile/pallas_call | solution.py:136
  15.0 0.1 pad_add_fusion.at_ref
  15.1 2.2 %collective-permute-done.1.refs_2_ = bf16[512,256]{1,0:T(8,128)(2,1)S(1)} collective-permute-done((bf16[512,256]{1,0:T(8,128)(2,1)}, bf16[512,256]{1,0:T(8,128)(2,1)S(1)}, u32[]{:S(2)}, u32[]{:S(2)}) %collective-permute-start.1) | collective-permute-done | bytes 262176 | tf_op jit(solution)/shard_map/ppermute | solution.py:452
  17.3 3.0 %forward.3 = (bf16[1024,256]{1,0:T(8,128)(2,1)S(1)}, bf16[1024,256]{1,0:T(8,128)(2,1)S(1)}) custom-call(s32[2]{0:T(128)S(1)} %pad_add_fusion.at_ref, bf16[4096,2048]{1,0:T(8,128)(2,1)S(1)} %build_tile.1.tile_ref, bf16[512,256]{1,0:T(8,128)(2,1)S(1)} %copy-done.1, bf16[512,256]{1,0:T(8,128)(2,1)S(1)} %collective-permute-done.refs_1_, ...), custom_call_target="tpu_custom_call" | custom-call | flops 2147483648 | tf_op jit(solution)/shard_map/forward/pallas_call | solution.py:175
  20.3 0.1 collective-permute-start.4
  20.4 3.0 %forward.2 = (bf16[1024,256]{1,0:T(8,128)(2,1)S(1)}, bf16[1024,256]{1,0:T(8,128)(2,1)S(1)}) custom-call(s32[2]{0:T(128)S(1)} %pad_add_fusion.at_ref, bf16[4096,2048]{1,0:T(8,128)(2,1)S(1)} %build_tile.1.tile_ref, bf16[512,256]{1,0:T(8,128)(2,1)S(1)} %copy-done.1, bf16[512,256]{1,0:T(8,128)(2,1)S(1)} %collective-permute-done.refs_1_, ...), custom_call_target="tpu_custom_call" | custom-call | flops 2147483648 | tf_op jit(solution)/shard_map/forward/pallas_call | solution.py:175
  23.4 0.6 collective-permute-start.3
  24.0 1.6 %collective-permute-start.6 = (bf16[256,256]{1,0:T(8,128)(2,1)S(1)}, bf16[256,256]{1,0:T(8,128)(2,1)S(1)}, u32[]{:S(2)}, u32[]{:S(2)}) collective-permute-start(bf16[256,256]{1,0:T(8,128)(2,1)S(1)} %get-tuple-element.46), channel_id=1, source_target_pairs={{0,2},{1,3},{2,0},{3,1},{4,6},{5,7},{6,4},{7,5},{8,10},{9,11},{10,... | collective-permute-start | bytes 393224 | tf_op jit(solution)/shard_map/ppermute | solution.py:452
  25.7 1.5 %collective-permute-start.5 = (bf16[256,256]{1,0:T(8,128)(2,1)S(1)}, bf16[256,256]{1,0:T(8,128)(2,1)S(1)}, u32[]{:S(2)}, u32[]{:S(2)}) collective-permute-start(bf16[256,256]{1,0:T(8,128)(2,1)S(1)} %get-tuple-element.48), channel_id=1, source_target_pairs={{0,2},{1,3},{2,0},{3,1},{4,6},{5,7},{6,4},{7,5},{8,10},{9,11},{10,... | collective-permute-start | bytes 393224 | tf_op jit(solution)/shard_map/ppermute | solution.py:452
  27.2 0.6 collective-permute-start.7
  27.8 2.6 %collective-permute-done.6.refs_2_ = bf16[256,256]{1,0:T(8,128)(2,1)S(1)} collective-permute-done((bf16[256,256]{1,0:T(8,128)(2,1)S(1)}, bf16[256,256]{1,0:T(8,128)(2,1)S(1)}, u32[]{:S(2)}, u32[]{:S(2)}) %collective-permute-start.6) | collective-permute-done | bytes 131104 | tf_op jit(solution)/shard_map/ppermute | solution.py:452
  30.5 2.7 %collective-permute-start.8 = (bf16[256,256]{1,0:T(8,128)(2,1)S(1)}, bf16[256,256]{1,0:T(8,128)(2,1)S(1)}, u32[]{:S(2)}, u32[]{:S(2)}) collective-permute-start(bf16[256,256]{1,0:T(8,128)(2,1)S(1)} %combine.6), channel_id=1, source_target_pairs={{0,4},{1,5},{2,6},{3,7},{4,0},{5,1},{6,2},{7,3},{8,12},{9,13},{10,... | collective-permute-start | bytes 393224 | tf_op jit(solution)/shard_map/ppermute | solution.py:452
  33.2 0.4 convert_multiply_fusion
  33.6 1.6 %collective-permute-start.10 = (bf16[256,256]{1,0:T(8,128)(2,1)S(1)}, bf16[256,256]{1,0:T(8,128)(2,1)S(1)}, u32[]{:S(2)}, u32[]{:S(2)}) collective-permute-start(bf16[256,256]{1,0:T(8,128)(2,1)S(1)} %get-tuple-element.55), channel_id=1, source_target_pairs={{0,2},{1,3},{2,0},{3,1},{4,6},{5,7},{6,4},{7,5},{8,10},{9,11},{10,... | collective-permute-start | bytes 393224 | tf_op jit(solution)/shard_map/ppermute | solution.py:452
  35.3 1.2 %collective-permute-start.11 = (bf16[256,256]{1,0:T(8,128)(2,1)S(1)}, bf16[256,256]{1,0:T(8,128)(2,1)S(1)}, u32[]{:S(2)}, u32[]{:S(2)}) collective-permute-start(bf16[256,256]{1,0:T(8,128)(2,1)S(1)} %combine.7), channel_id=1, source_target_pairs={{0,4},{1,5},{2,6},{3,7},{4,0},{5,1},{6,2},{7,3},{8,12},{9,13},{10,... | collective-permute-start | bytes 393224 | tf_op jit(solution)/shard_map/ppermute | solution.py:452
  36.5 3.6 %collective-permute-done.7.refs_2_ = bf16[256,256]{1,0:T(8,128)(2,1)S(1)} collective-permute-done((bf16[256,256]{1,0:T(8,128)(2,1)S(1)}, bf16[256,256]{1,0:T(8,128)(2,1)S(1)}, u32[]{:S(2)}, u32[]{:S(2)}) %collective-permute-start.7) | collective-permute-done | bytes 131104 | tf_op jit(solution)/shard_map/ppermute | solution.py:452
  40.1 0.4 gate.2
  40.5 1.3 %collective-permute-start.9 = (bf16[256,256]{1,0:T(8,128)(2,1)S(1)}, bf16[256,256]{1,0:T(8,128)(2,1)S(1)}, u32[]{:S(2)}, u32[]{:S(2)}) collective-permute-start(bf16[256,256]{1,0:T(8,128)(2,1)S(1)} %get-tuple-element.53.refs_0_), channel_id=1, source_target_pairs={{0,4},{1,5},{2,6},{3,7},{4,0},{5,1},{6,2},{7,3},{8,12},{9,13},{10,... | collective-permute-start | bytes 393224 | tf_op jit(solution)/shard_map/ppermute | solution.py:452
  41.8 2.4 %collective-permute-done.10.refs_2_ = bf16[256,256]{1,0:T(8,128)(2,1)S(1)} collective-permute-done((bf16[256,256]{1,0:T(8,128)(2,1)S(1)}, bf16[256,256]{1,0:T(8,128)(2,1)S(1)}, u32[]{:S(2)}, u32[]{:S(2)}) %collective-permute-start.10) | collective-permute-done | bytes 131104 | tf_op jit(solution)/shard_map/ppermute | solution.py:452
  44.2 4.2 %collective-permute-done.11.refs_3_ = bf16[256,256]{1,0:T(8,128)(2,1)S(1)} collective-permute-done((bf16[256,256]{1,0:T(8,128)(2,1)S(1)}, bf16[256,256]{1,0:T(8,128)(2,1)S(1)}, u32[]{:S(2)}, u32[]{:S(2)}) %collective-permute-start.11) | collective-permute-done | bytes 131104 | tf_op jit(solution)/shard_map/ppermute | solution.py:452
  48.4 0.4 gate.3
  48.8 0.1 collective-permute-start.12
  48.9 5.8 %collective-permute-start.13 = (bf16[256,256]{1,0:T(8,128)(2,1)S(1)}, bf16[256,256]{1,0:T(8,128)(2,1)S(1)}, u32[]{:S(2)}, u32[]{:S(2)}) collective-permute-start(bf16[256,256]{1,0:T(8,128)(2,1)S(1)} %get-tuple-element.56.refs_0_), channel_id=1, source_target_pairs={{0,2},{1,3},{2,0},{3,1},{4,6},{5,7},{6,4},{7,5},{8,10},{9,11},{10,... | collective-permute-start | bytes 393224 | tf_op jit(solution)/shard_map/ppermute | solution.py:452
  54.7 2.0 %collective-permute-start.19 = (bf16[256,256]{1,0:T(8,128)(2,1)S(1)}, bf16[256,256]{1,0:T(8,128)(2,1)S(1)}, u32[]{:S(2)}, u32[]{:S(2)}) collective-permute-start(bf16[256,256]{1,0:T(8,128)(2,1)S(1)} %collective-permute-done.9.refs_1_), channel_id=1, source_target_pairs={{0,2},{1,3},{2,0},{3,1},{4,6},{5,7},{6,4},{7,5},{8,10},{9,11},{10,... | collective-permute-start | bytes 393224 | tf_op jit(solution)/shard_map/ppermute | solution.py:452
  56.7 1.5 %local_terms.1 = (bf16[512,256]{1,0:T(8,128)(2,1)}, bf16[160,256]{1,0:T(8,128)(2,1)S(1)}, bf16[160,256]{1,0:T(8,128)(2,1)S(1)}) custom-call(s32[2]{0:T(128)S(1)} %pad_add_fusion.at_ref, f32[16,512]{1,0:T(8,128)S(1)} %fusion.members_ref, f32[512,256]{1,0:T(8,128)S(1)} %get-tuple-element.81.gains_ref, bf16[512,256]{1,0:T(8,128)(2,1)S(1)} %copy-done.2, ...), custom_call_target="tpu_custom_call" | custom-call | flops 1 | bytes 1 | tf_op jit(solution)/shard_map/local_terms/pallas_call | solution.py:317
  58.2 1.3 %collective-permute-done.14.other_ref = bf16[160,256]{1,0:T(8,128)(2,1)S(1)} collective-permute-done((bf16[160,256]{1,0:T(8,128)(2,1)S(1)}, bf16[160,256]{1,0:T(8,128)(2,1)S(1)}, u32[]{:S(2)}, u32[]{:S(2)}) %collective-permute-start.14) | collective-permute-done | bytes 81952 | tf_op jit(solution)/shard_map/ppermute | solution.py:452
  59.5 0.1 collective-permute-start.15
  59.6 1.2 %collective-permute-start.16 = (bf16[160,256]{1,0:T(8,128)(2,1)S(1)}, bf16[160,256]{1,0:T(8,128)(2,1)S(1)}, u32[]{:S(2)}, u32[]{:S(2)}) collective-permute-start(bf16[160,256]{1,0:T(8,128)(2,1)S(1)} %add_messages.5.own_ref), channel_id=1, source_target_pairs={{0,8},{8,0},{16,24},{24,16},{1,9},{9,1},{17,25},{25,17},{2,10},{10... | collective-permute-start | bytes 245768 | tf_op jit(solution)/shard_map/ppermute | solution.py:452
  60.9 0.5 collective-permute-done.19.refs_3_
  61.5 2.7 %collective-permute-done.16.other_ref = bf16[160,256]{1,0:T(8,128)(2,1)S(1)} collective-permute-done((bf16[160,256]{1,0:T(8,128)(2,1)S(1)}, bf16[160,256]{1,0:T(8,128)(2,1)S(1)}, u32[]{:S(2)}, u32[]{:S(2)}) %collective-permute-start.16) | collective-permute-done | bytes 81952 | tf_op jit(solution)/shard_map/ppermute | solution.py:452
  64.2 0.9 %collective-permute-done.15.refs_3_ = bf16[256,256]{1,0:T(8,128)(2,1)S(1)} collective-permute-done((bf16[256,256]{1,0:T(8,128)(2,1)S(1)}, bf16[256,256]{1,0:T(8,128)(2,1)S(1)}, u32[]{:S(2)}, u32[]{:S(2)}) %collective-permute-start.15) | collective-permute-done | bytes 131104 | tf_op jit(solution)/shard_map/ppermute | solution.py:452
  65.2 1.6 %collective-permute-start.24 = (bf16[160,256]{1,0:T(8,128)(2,1)S(1)}, bf16[160,256]{1,0:T(8,128)(2,1)S(1)}, u32[]{:S(2)}, u32[]{:S(2)}) collective-permute-start(bf16[160,256]{1,0:T(8,128)(2,1)S(1)} %add_messages.6.own_ref), channel_id=1, source_target_pairs={{0,16},{8,24},{16,0},{24,8},{1,17},{9,25},{17,1},{25,9},{2,18},{10... | collective-permute-start | bytes 245768 | tf_op jit(solution)/shard_map/ppermute | solution.py:452
  66.8 3.2 %backward.2 = (f32[256,512]{1,0:T(8,128)S(1)}, f32[256,512]{1,0:T(8,128)S(1)}, f32[256,512]{1,0:T(8,128)S(1)}, f32[256,512]{1,0:T(8,128)S(1)}) custom-call(s32[2]{0:T(128)S(1)} %pad_add_fusion.at_ref, bf16[4096,2048]{1,0:T(8,128)(2,1)S(1)} %build_tile.1.tile_ref, bf16[256,256]{1,0:T(8,128)(2,1)S(1)} %get-tuple-element.53.refs_0_, ...), custom_call_target="tpu_custom_call" | custom-call | flops 1073741824 | tf_op jit(solution)/shard_map/backward/pallas_call | solution.py:414
  70.1 3.3 %backward.3 = (f32[256,512]{1,0:T(8,128)S(1)}, bf16[256,512]{1,0:T(8,128)(2,1)S(1)}, bf16[256,512]{1,0:T(8,128)(2,1)S(1)}, bf16[256,512]{1,0:T(8,128)(2,1)S(1)}) custom-call(s32[2]{0:T(128)S(1)} %pad_add_fusion.at_ref, bf16[4096,2048]{1,0:T(8,128)(2,1)S(1)} %build_tile.1.tile_ref, bf16[256,256]{1,0:T(8,128)(2,1)S(1)} %get-tuple-element.56.refs_0_, ...), custom_call_target="tpu_custom_call" | custom-call | flops 1073741824 | tf_op jit(solution)/shard_map/backward/pallas_call | solution.py:414
  73.3 0.6 collective-permute-start.21
  73.9 1.2 %collective-permute-start.22 = (bf16[256,512]{1,0:T(8,128)(2,1)S(1)}, bf16[256,512]{1,0:T(8,128)(2,1)S(1)}, u32[]{:S(2)}, u32[]{:S(2)}) collective-permute-start(bf16[256,512]{1,0:T(8,128)(2,1)S(1)} %get-tuple-element.76), channel_id=1, source_target_pairs={{0,16},{8,24},{16,0},{24,8},{1,17},{9,25},{17,1},{25,9},{2,18},{10... | collective-permute-start | bytes 786440 | tf_op jit(solution)/shard_map/ppermute | solution.py:452
  75.1 1.8 %collective-permute-start.23 = (bf16[256,512]{1,0:T(8,128)(2,1)S(1)}, bf16[256,512]{1,0:T(8,128)(2,1)S(1)}, u32[]{:S(2)}, u32[]{:S(2)}) collective-permute-start(bf16[256,512]{1,0:T(8,128)(2,1)S(1)} %get-tuple-element.77), channel_id=1, source_target_pairs={{0,24},{8,16},{16,8},{24,0},{1,25},{9,17},{17,9},{25,1},{2,26},{10... | collective-permute-start | bytes 786440 | tf_op jit(solution)/shard_map/ppermute | solution.py:452
  76.9 1.0 %collective-permute-start.25 = (bf16[160,256]{1,0:T(8,128)(2,1)S(1)}, bf16[160,256]{1,0:T(8,128)(2,1)S(1)}, u32[]{:S(2)}, u32[]{:S(2)}) collective-permute-start(bf16[160,256]{1,0:T(8,128)(2,1)S(1)} %add_messages.7.own_ref), channel_id=1, source_target_pairs={{0,2},{1,3},{2,0},{3,1},{4,6},{5,7},{6,4},{7,5},{8,10},{9,11},{10,... | collective-permute-start | bytes 245768 | tf_op jit(solution)/shard_map/ppermute | solution.py:452
  77.9 3.5 %collective-permute-done.25.other_ref = bf16[160,256]{1,0:T(8,128)(2,1)S(1)} collective-permute-done((bf16[160,256]{1,0:T(8,128)(2,1)S(1)}, bf16[160,256]{1,0:T(8,128)(2,1)S(1)}, u32[]{:S(2)}, u32[]{:S(2)}) %collective-permute-start.25) | collective-permute-done | bytes 81952 | tf_op jit(solution)/shard_map/ppermute | solution.py:452
  81.4 2.2 %collective-permute-start.26 = (bf16[160,256]{1,0:T(8,128)(2,1)S(1)}, bf16[160,256]{1,0:T(8,128)(2,1)S(1)}, u32[]{:S(2)}, u32[]{:S(2)}) collective-permute-start(bf16[160,256]{1,0:T(8,128)(2,1)S(1)} %add_messages.8.own_ref), channel_id=1, source_target_pairs={{0,4},{1,5},{2,6},{3,7},{4,0},{5,1},{6,2},{7,3},{8,12},{9,13},{10,... | collective-permute-start | bytes 245768 | tf_op jit(solution)/shard_map/ppermute | solution.py:452
  83.6 4.1 %collective-permute-done.26.other_ref = bf16[160,256]{1,0:T(8,128)(2,1)S(1)} collective-permute-done((bf16[160,256]{1,0:T(8,128)(2,1)S(1)}, bf16[160,256]{1,0:T(8,128)(2,1)S(1)}, u32[]{:S(2)}, u32[]{:S(2)}) %collective-permute-start.26) | collective-permute-done | bytes 81952 | tf_op jit(solution)/shard_map/ppermute | solution.py:452
  87.8 1.3 %collective-permute-done.27.other_ref = bf16[160,256]{1,0:T(8,128)(2,1)S(1)} collective-permute-done((bf16[160,256]{1,0:T(8,128)(2,1)S(1)}, bf16[160,256]{1,0:T(8,128)(2,1)S(1)}, u32[]{:S(2)}, u32[]{:S(2)}) %collective-permute-start.27) | collective-permute-done | bytes 81952 | tf_op jit(solution)/shard_map/ppermute | solution.py:452
  89.1 1.3 %totals.1 = (f32[256,256]{1,0:T(8,128)}, f32[16,256]{1,0:T(8,128)}) custom-call(s32[2]{0:T(128)S(1)} %pad_add_fusion.at_ref, bf16[160,256]{1,0:T(8,128)(2,1)S(1)} %add_messages.9.own_ref, bf16[160,256]{1,0:T(8,128)(2,1)S(1)} %collective-permute-done.27.other_ref), custom_call_target="tpu_custom_call" | custom-call | flops 1 | bytes 1 | tf_op jit(solution)/shard_map/totals/pallas_call | solution.py:369
  90.4 0.9 finish.1
  (46 shorter events, 0.8 us)
Async XLA Ops:
  0.6 32.5 %copy-start = (f32[16,256]{1,0:T(8,128)S(1)}, f32[16,256]{1,0:T(8,128)}, u32[]{:S(2)}) copy-start(f32[16,256]{1,0:T(8,128)} %param.15) | copy-start | bytes 49156
  0.6 16.6 %copy-start.1 = (bf16[512,256]{1,0:T(8,128)(2,1)S(1)}, bf16[512,256]{1,0:T(8,128)(2,1)}, u32[]{:S(2)}) copy-start(bf16[512,256]{1,0:T(8,128)(2,1)} %refs_0_.3) | copy-start | bytes 786436
  0.7 14.4 %collective-permute-start = (bf16[512,256]{1,0:T(8,128)(2,1)}, bf16[512,256]{1,0:T(8,128)(2,1)S(1)}, u32[]{:S(2)}, u32[]{:S(2)}) collective-permute-start(bf16[512,256]{1,0:T(8,128)(2,1)} %refs_0_.3), channel_id=1, source_target_pairs={{0,8},{8,0},{16,24},{24,16},{1,9},{9,1},{17,25},{25,17},{2,10},{10... | collective-permute-start | bytes 786440 | tf_op jit(solution)/shard_map/ppermute | solution.py:452
  3.7 13.6 %collective-permute-start.1 = (bf16[512,256]{1,0:T(8,128)(2,1)}, bf16[512,256]{1,0:T(8,128)(2,1)S(1)}, u32[]{:S(2)}, u32[]{:S(2)}) collective-permute-start(bf16[512,256]{1,0:T(8,128)(2,1)} %refs_0_.3), channel_id=1, source_target_pairs={{0,16},{8,24},{16,0},{24,8},{1,17},{9,25},{17,1},{25,9},{2,18},{10... | collective-permute-start | bytes 786440 | tf_op jit(solution)/shard_map/ppermute | solution.py:452
  5.2 12.1 %collective-permute-start.2 = (bf16[512,256]{1,0:T(8,128)(2,1)}, bf16[512,256]{1,0:T(8,128)(2,1)S(1)}, u32[]{:S(2)}, u32[]{:S(2)}) collective-permute-start(bf16[512,256]{1,0:T(8,128)(2,1)} %refs_0_.3), channel_id=1, source_target_pairs={{0,24},{8,16},{16,8},{24,0},{1,25},{9,17},{17,9},{25,1},{2,26},{10... | collective-permute-start | bytes 786440 | tf_op jit(solution)/shard_map/ppermute | solution.py:452
  5.9 0.7 copy-start.4
  6.5 0.7 copy-start.5
  15.1 18.1 %copy-start.2 = (bf16[512,256]{1,0:T(8,128)(2,1)S(1)}, bf16[512,256]{1,0:T(8,128)(2,1)}, u32[]{:S(2)}) copy-start(bf16[512,256]{1,0:T(8,128)(2,1)} %cotangent_ref.1) | copy-start | bytes 786436
  15.1 18.1 %copy-start.6 = (s32[512]{0:T(512)S(1)}, s32[512]{0:T(512)}, u32[]{:S(2)}) copy-start(s32[512]{0:T(512)} %param.16) | copy-start | bytes 6148
  15.1 25.0 %copy-start.3 = (bf16[256,256]{1,0:T(8,128)(2,1)S(1)}, bf16[256,256]{1,0:T(8,128)(2,1)}, u32[]{:S(2)}) copy-start(bf16[256,256]{1,0:T(8,128)(2,1)} %weight_ref.3) | copy-start | bytes 393220
  20.3 3.7 %collective-permute-start.4 = (bf16[1024,256]{1,0:T(8,128)(2,1)S(1)}, bf16[1024,256]{1,0:T(8,128)(2,1)S(1)}, u32[]{:S(2)}, u32[]{:S(2)}) collective-permute-start(bf16[1024,256]{1,0:T(8,128)(2,1)S(1)} %get-tuple-element.45), channel_id=1, source_target_pairs={{0,1},{1,0},{2,3},{3,2},{4,5},{5,4},{6,7},{7,6},{8,9},{9,8},{10,11... | collective-permute-start | bytes 1572872 | tf_op jit(solution)/shard_map/ppermute | solution.py:452
  23.4 2.3 %collective-permute-start.3 = (bf16[1024,256]{1,0:T(8,128)(2,1)S(1)}, bf16[1024,256]{1,0:T(8,128)(2,1)S(1)}, u32[]{:S(2)}, u32[]{:S(2)}) collective-permute-start(bf16[1024,256]{1,0:T(8,128)(2,1)S(1)} %get-tuple-element.43), channel_id=1, source_target_pairs={{0,1},{1,0},{2,3},{3,2},{4,5},{5,4},{6,7},{7,6},{8,9},{9,8},{10,11... | collective-permute-start | bytes 1572872 | tf_op jit(solution)/shard_map/ppermute | solution.py:452
  24.0 6.4 %collective-permute-start.6 = (bf16[256,256]{1,0:T(8,128)(2,1)S(1)}, bf16[256,256]{1,0:T(8,128)(2,1)S(1)}, u32[]{:S(2)}, u32[]{:S(2)}) collective-permute-start(bf16[256,256]{1,0:T(8,128)(2,1)S(1)} %get-tuple-element.46), channel_id=1, source_target_pairs={{0,2},{1,3},{2,0},{3,1},{4,6},{5,7},{6,4},{7,5},{8,10},{9,11},{10,... | collective-permute-start | bytes 393224 | tf_op jit(solution)/shard_map/ppermute | solution.py:452
  25.7 9.5 %collective-permute-start.5 = (bf16[256,256]{1,0:T(8,128)(2,1)S(1)}, bf16[256,256]{1,0:T(8,128)(2,1)S(1)}, u32[]{:S(2)}, u32[]{:S(2)}) collective-permute-start(bf16[256,256]{1,0:T(8,128)(2,1)S(1)} %get-tuple-element.48), channel_id=1, source_target_pairs={{0,2},{1,3},{2,0},{3,1},{4,6},{5,7},{6,4},{7,5},{8,10},{9,11},{10,... | collective-permute-start | bytes 393224 | tf_op jit(solution)/shard_map/ppermute | solution.py:452
  27.2 12.9 %collective-permute-start.7 = (bf16[256,256]{1,0:T(8,128)(2,1)S(1)}, bf16[256,256]{1,0:T(8,128)(2,1)S(1)}, u32[]{:S(2)}, u32[]{:S(2)}) collective-permute-start(bf16[256,256]{1,0:T(8,128)(2,1)S(1)} %get-tuple-element.52), channel_id=1, source_target_pairs={{0,2},{1,3},{2,0},{3,1},{4,6},{5,7},{6,4},{7,5},{8,10},{9,11},{10,... | collective-permute-start | bytes 393224 | tf_op jit(solution)/shard_map/ppermute | solution.py:452
  30.5 9.6 %collective-permute-start.8 = (bf16[256,256]{1,0:T(8,128)(2,1)S(1)}, bf16[256,256]{1,0:T(8,128)(2,1)S(1)}, u32[]{:S(2)}, u32[]{:S(2)}) collective-permute-start(bf16[256,256]{1,0:T(8,128)(2,1)S(1)} %combine.6), channel_id=1, source_target_pairs={{0,4},{1,5},{2,6},{3,7},{4,0},{5,1},{6,2},{7,3},{8,12},{9,13},{10,... | collective-permute-start | bytes 393224 | tf_op jit(solution)/shard_map/ppermute | solution.py:452
  33.6 10.6 %collective-permute-start.10 = (bf16[256,256]{1,0:T(8,128)(2,1)S(1)}, bf16[256,256]{1,0:T(8,128)(2,1)S(1)}, u32[]{:S(2)}, u32[]{:S(2)}) collective-permute-start(bf16[256,256]{1,0:T(8,128)(2,1)S(1)} %get-tuple-element.55), channel_id=1, source_target_pairs={{0,2},{1,3},{2,0},{3,1},{4,6},{5,7},{6,4},{7,5},{8,10},{9,11},{10,... | collective-permute-start | bytes 393224 | tf_op jit(solution)/shard_map/ppermute | solution.py:452
  35.3 13.1 %collective-permute-start.11 = (bf16[256,256]{1,0:T(8,128)(2,1)S(1)}, bf16[256,256]{1,0:T(8,128)(2,1)S(1)}, u32[]{:S(2)}, u32[]{:S(2)}) collective-permute-start(bf16[256,256]{1,0:T(8,128)(2,1)S(1)} %combine.7), channel_id=1, source_target_pairs={{0,4},{1,5},{2,6},{3,7},{4,0},{5,1},{6,2},{7,3},{8,12},{9,13},{10,... | collective-permute-start | bytes 393224 | tf_op jit(solution)/shard_map/ppermute | solution.py:452
  40.5 14.2 %collective-permute-start.9 = (bf16[256,256]{1,0:T(8,128)(2,1)S(1)}, bf16[256,256]{1,0:T(8,128)(2,1)S(1)}, u32[]{:S(2)}, u32[]{:S(2)}) collective-permute-start(bf16[256,256]{1,0:T(8,128)(2,1)S(1)} %get-tuple-element.53.refs_0_), channel_id=1, source_target_pairs={{0,4},{1,5},{2,6},{3,7},{4,0},{5,1},{6,2},{7,3},{8,12},{9,13},{10,... | collective-permute-start | bytes 393224 | tf_op jit(solution)/shard_map/ppermute | solution.py:452
  48.8 10.6 %collective-permute-start.12 = (bf16[256,256]{1,0:T(8,128)(2,1)S(1)}, bf16[256,256]{1,0:T(8,128)(2,1)S(1)}, u32[]{:S(2)}, u32[]{:S(2)}) collective-permute-start(bf16[256,256]{1,0:T(8,128)(2,1)S(1)} %get-tuple-element.56.refs_0_), channel_id=1, source_target_pairs={{0,4},{1,5},{2,6},{3,7},{4,0},{5,1},{6,2},{7,3},{8,12},{9,13},{10,... | collective-permute-start | bytes 393224 | tf_op jit(solution)/shard_map/ppermute | solution.py:452
  48.9 10.6 %collective-permute-start.13 = (bf16[256,256]{1,0:T(8,128)(2,1)S(1)}, bf16[256,256]{1,0:T(8,128)(2,1)S(1)}, u32[]{:S(2)}, u32[]{:S(2)}) collective-permute-start(bf16[256,256]{1,0:T(8,128)(2,1)S(1)} %get-tuple-element.56.refs_0_), channel_id=1, source_target_pairs={{0,2},{1,3},{2,0},{3,1},{4,6},{5,7},{6,4},{7,5},{8,10},{9,11},{10,... | collective-permute-start | bytes 393224 | tf_op jit(solution)/shard_map/ppermute | solution.py:452
  54.7 6.2 %collective-permute-start.18 = (bf16[256,256]{1,0:T(8,128)(2,1)S(1)}, bf16[256,256]{1,0:T(8,128)(2,1)S(1)}, u32[]{:S(2)}, u32[]{:S(2)}) collective-permute-start(bf16[256,256]{1,0:T(8,128)(2,1)S(1)} %get-tuple-element.53.refs_0_), channel_id=1, source_target_pairs={{0,2},{1,3},{2,0},{3,1},{4,6},{5,7},{6,4},{7,5},{8,10},{9,11},{10,... | collective-permute-start | bytes 393224 | tf_op jit(solution)/shard_map/ppermute | solution.py:452
  54.7 6.7 %collective-permute-start.19 = (bf16[256,256]{1,0:T(8,128)(2,1)S(1)}, bf16[256,256]{1,0:T(8,128)(2,1)S(1)}, u32[]{:S(2)}, u32[]{:S(2)}) collective-permute-start(bf16[256,256]{1,0:T(8,128)(2,1)S(1)} %collective-permute-done.9.refs_1_), channel_id=1, source_target_pairs={{0,2},{1,3},{2,0},{3,1},{4,6},{5,7},{6,4},{7,5},{8,10},{9,11},{10,... | collective-permute-start | bytes 393224 | tf_op jit(solution)/shard_map/ppermute | solution.py:452
  58.2 1.3 %collective-permute-start.14 = (bf16[160,256]{1,0:T(8,128)(2,1)S(1)}, bf16[160,256]{1,0:T(8,128)(2,1)S(1)}, u32[]{:S(2)}, u32[]{:S(2)}) collective-permute-start(bf16[160,256]{1,0:T(8,128)(2,1)S(1)} %get-tuple-element.67), channel_id=1, source_target_pairs={{0,1},{1,0},{2,3},{3,2},{4,5},{5,4},{6,7},{7,6},{8,9},{9,8},{10,11... | collective-permute-start | bytes 245768 | tf_op jit(solution)/shard_map/ppermute | solution.py:452
  59.5 5.6 %collective-permute-start.15 = (bf16[256,256]{1,0:T(8,128)(2,1)S(1)}, bf16[256,256]{1,0:T(8,128)(2,1)S(1)}, u32[]{:S(2)}, u32[]{:S(2)}) collective-permute-start(bf16[256,256]{1,0:T(8,128)(2,1)S(1)} %collective-permute-done.12.refs_1_), channel_id=1, source_target_pairs={{0,2},{1,3},{2,0},{3,1},{4,6},{5,7},{6,4},{7,5},{8,10},{9,11},{10,... | collective-permute-start | bytes 393224 | tf_op jit(solution)/shard_map/ppermute | solution.py:452
  59.6 4.5 %collective-permute-start.16 = (bf16[160,256]{1,0:T(8,128)(2,1)S(1)}, bf16[160,256]{1,0:T(8,128)(2,1)S(1)}, u32[]{:S(2)}, u32[]{:S(2)}) collective-permute-start(bf16[160,256]{1,0:T(8,128)(2,1)S(1)} %add_messages.5.own_ref), channel_id=1, source_target_pairs={{0,8},{8,0},{16,24},{24,16},{1,9},{9,1},{17,25},{25,17},{2,10},{10... | collective-permute-start | bytes 245768 | tf_op jit(solution)/shard_map/ppermute | solution.py:452
  61.4 5.4 %collective-permute-start.20 = (bf16[1024,256]{1,0:T(8,128)(2,1)S(1)}, bf16[1024,256]{1,0:T(8,128)(2,1)S(1)}, u32[]{:S(2)}, u32[]{:S(2)}) collective-permute-start(bf16[1024,256]{1,0:T(8,128)(2,1)S(1)} %pad_maximum_fusion.1), channel_id=1, source_target_pairs={{0,1},{1,0},{2,3},{3,2},{4,5},{5,4},{6,7},{7,6},{8,9},{9,8},{10,11... | collective-permute-start | bytes 1572872 | tf_op jit(solution)/shard_map/ppermute | solution.py:452
  65.2 4.9 %collective-permute-start.17 = (bf16[1024,256]{1,0:T(8,128)(2,1)S(1)}, bf16[1024,256]{1,0:T(8,128)(2,1)S(1)}, u32[]{:S(2)}, u32[]{:S(2)}) collective-permute-start(bf16[1024,256]{1,0:T(8,128)(2,1)S(1)} %pad_maximum_fusion), channel_id=1, source_target_pairs={{0,1},{1,0},{2,3},{3,2},{4,5},{5,4},{6,7},{7,6},{8,9},{9,8},{10,11... | collective-permute-start | bytes 1572872 | tf_op jit(solution)/shard_map/ppermute | solution.py:452
  65.2 11.6 %collective-permute-start.24 = (bf16[160,256]{1,0:T(8,128)(2,1)S(1)}, bf16[160,256]{1,0:T(8,128)(2,1)S(1)}, u32[]{:S(2)}, u32[]{:S(2)}) collective-permute-start(bf16[160,256]{1,0:T(8,128)(2,1)S(1)} %add_messages.6.own_ref), channel_id=1, source_target_pairs={{0,16},{8,24},{16,0},{24,8},{1,17},{9,25},{17,1},{25,9},{2,18},{10... | collective-permute-start | bytes 245768 | tf_op jit(solution)/shard_map/ppermute | solution.py:452
  73.3 17.0 %collective-permute-start.21 = (bf16[256,512]{1,0:T(8,128)(2,1)S(1)}, bf16[256,512]{1,0:T(8,128)(2,1)S(1)}, u32[]{:S(2)}, u32[]{:S(2)}) collective-permute-start(bf16[256,512]{1,0:T(8,128)(2,1)S(1)} %get-tuple-element.75), channel_id=1, source_target_pairs={{0,8},{8,0},{16,24},{24,16},{1,9},{9,1},{17,25},{25,17},{2,10},{10... | collective-permute-start | bytes 786440 | tf_op jit(solution)/shard_map/ppermute | solution.py:452
  73.9 16.5 %collective-permute-start.22 = (bf16[256,512]{1,0:T(8,128)(2,1)S(1)}, bf16[256,512]{1,0:T(8,128)(2,1)S(1)}, u32[]{:S(2)}, u32[]{:S(2)}) collective-permute-start(bf16[256,512]{1,0:T(8,128)(2,1)S(1)} %get-tuple-element.76), channel_id=1, source_target_pairs={{0,16},{8,24},{16,0},{24,8},{1,17},{9,25},{17,1},{25,9},{2,18},{10... | collective-permute-start | bytes 786440 | tf_op jit(solution)/shard_map/ppermute | solution.py:452
  75.1 15.3 %collective-permute-start.23 = (bf16[256,512]{1,0:T(8,128)(2,1)S(1)}, bf16[256,512]{1,0:T(8,128)(2,1)S(1)}, u32[]{:S(2)}, u32[]{:S(2)}) collective-permute-start(bf16[256,512]{1,0:T(8,128)(2,1)S(1)} %get-tuple-element.77), channel_id=1, source_target_pairs={{0,24},{8,16},{16,8},{24,0},{1,25},{9,17},{17,9},{25,1},{2,26},{10... | collective-permute-start | bytes 786440 | tf_op jit(solution)/shard_map/ppermute | solution.py:452
  76.9 4.5 %collective-permute-start.25 = (bf16[160,256]{1,0:T(8,128)(2,1)S(1)}, bf16[160,256]{1,0:T(8,128)(2,1)S(1)}, u32[]{:S(2)}, u32[]{:S(2)}) collective-permute-start(bf16[160,256]{1,0:T(8,128)(2,1)S(1)} %add_messages.7.own_ref), channel_id=1, source_target_pairs={{0,2},{1,3},{2,0},{3,1},{4,6},{5,7},{6,4},{7,5},{8,10},{9,11},{10,... | collective-permute-start | bytes 245768 | tf_op jit(solution)/shard_map/ppermute | solution.py:452
  81.4 6.3 %collective-permute-start.26 = (bf16[160,256]{1,0:T(8,128)(2,1)S(1)}, bf16[160,256]{1,0:T(8,128)(2,1)S(1)}, u32[]{:S(2)}, u32[]{:S(2)}) collective-permute-start(bf16[160,256]{1,0:T(8,128)(2,1)S(1)} %add_messages.8.own_ref), channel_id=1, source_target_pairs={{0,4},{1,5},{2,6},{3,7},{4,0},{5,1},{6,2},{7,3},{8,12},{9,13},{10,... | collective-permute-start | bytes 245768 | tf_op jit(solution)/shard_map/ppermute | solution.py:452
  87.8 1.3 %collective-permute-start.27 = (bf16[160,256]{1,0:T(8,128)(2,1)S(1)}, bf16[160,256]{1,0:T(8,128)(2,1)S(1)}, u32[]{:S(2)}, u32[]{:S(2)}) collective-permute-start(bf16[160,256]{1,0:T(8,128)(2,1)S(1)} %add_messages.9.own_ref), channel_id=1, source_target_pairs={{0,1},{1,0},{2,3},{3,2},{4,5},{5,4},{6,7},{7,6},{8,9},{9,8},{10,11... | collective-permute-start | bytes 245768 | tf_op jit(solution)/shard_map/ppermute | solution.py:452

commit v4 on v3

v4 whole, which is shorter than its diff:
```python
import functools
import math

import jax
import jax.numpy as jnp
from jax import lax
from jax.experimental import pallas as pl
from jax.experimental.pallas import tpu as pltpu
from jax.sharding import PartitionSpec as P

BLOCK = 128
GROUP = 16
HEAVY = 16
CHUNKS = 2
MIB = 1 << 20
LIGHT = pl.CostEstimate(flops=1, bytes_accessed=1, transcendentals=0)


def bits_of(count):
    return [1 << b for b in range(count.bit_length() - 1)]


def shift_of(count):
    return count.bit_length() - 1


def block_order(count):
    return list(range(1, count, 2)) + list(range(0, count, 2))


def build_kernel(layout, at_ref, live_ref, rows_ref, cols_ref, slots_ref, tile_ref, buf, total, counts, most, sems):
    owners, per_owner, per_chunk = layout
    live = live_ref[0, 0]
    groups = (live + GROUP - 1) // GROUP
    row_blocks, col_blocks = tile_ref.shape[0] // BLOCK, tile_ref.shape[1] // BLOCK

    def fetch(group):
        return pltpu.make_async_copy(
            slots_ref.at[0, 0, pl.ds(group * GROUP, GROUP)], buf.at[group], sems.at[group]
        )

    @pl.loop(0, groups)
    def _(group):
        fetch(group).start()

    zeros = jnp.zeros((BLOCK, tile_ref.shape[1]), tile_ref.dtype)
    most[0] = 0

    @pl.loop(0, row_blocks)
    def _(r):
        tile_ref[pl.ds(pl.multiple_of(r * BLOCK, BLOCK), BLOCK), :] = zeros
        for c in range(col_blocks):
            counts[r * col_blocks + c] = 0

    own_row, own_col = at_ref[0], at_ref[1]

    def place(index):
        row = rows_ref[0, 0, index]
        k, inner = (row >> shift_of(per_owner)) ^ own_col, row & (per_owner - 1)
        k = ((k & 1) ^ 1) * (owners // 2) + (k >> 1)
        chunk, inner = inner >> shift_of(per_chunk), inner & (per_chunk - 1)
        row = (((chunk << shift_of(owners)) + k) << shift_of(per_chunk)) + inner
        return row, cols_ref[0, 0, index] ^ (own_row << shift_of(per_owner))

    def block(row, col):
        top, left = pl.multiple_of(row * BLOCK, BLOCK), pl.multiple_of(col * BLOCK, BLOCK)
        return pl.ds(top, BLOCK), pl.ds(left, BLOCK)

    @pl.loop(0, groups)
    def _(group):
        fetch(group).wait()

        def add(s):
            row, col = place(group * GROUP + s)
            here = counts[row * col_blocks + col] + 1
            counts[row * col_blocks + col] = here
            tile_ref[block(row, col)] += buf[group, s]
            return here

        here = live - group * GROUP

        @pl.when(here >= GROUP)
        def _():
            most[0] = functools.reduce(jnp.maximum, [add(s) for s in range(GROUP)], most[0])

        @pl.when(here < GROUP)
        def _():
            @pl.loop(0, here)
            def _(s):
                most[0] = jnp.maximum(most[0], add(s))

    @pl.when(most[0] > HEAVY)
    def _():
        @pl.loop(0, live)
        def _(index):
            p_row, p_col = place(index)
            p = p_row * col_blocks + p_col

            @pl.when(counts[p] > HEAVY)
            def _():
                counts[p] = 0
                total[...] = jnp.zeros_like(total)

                @pl.loop(index, live)
                def _(other):
                    row, col = place(other)

                    @pl.when(row * col_blocks + col == p)
                    def _():
                        total[...] += buf[other >> shift_of(GROUP), other & (GROUP - 1)].astype(jnp.float32)

                tile_ref[block(p_row, p_col)] = total[...].astype(tile_ref.dtype)


def build_tile(at, slots, rows, cols, live, row_blocks, col_blocks, layout):
    smem = pl.BlockSpec(memory_space=pltpu.SMEM)
    vmem = pl.BlockSpec(memory_space=pltpu.VMEM)
    groups = slots.shape[2] // GROUP
    return pl.pallas_call(
        functools.partial(build_kernel, layout),
        out_shape=pltpu.VMEM((row_blocks * BLOCK, col_blocks * BLOCK), jnp.bfloat16),
        in_specs=[smem, smem, smem, smem, pl.BlockSpec(memory_space=pl.ANY)],
        out_specs=vmem,
        scratch_shapes=[
            pltpu.VMEM((groups, GROUP, BLOCK, BLOCK), jnp.bfloat16),
            pltpu.VMEM((BLOCK, BLOCK), jnp.float32),
            pltpu.SMEM((row_blocks * col_blocks,), jnp.int32),
            pltpu.SMEM((1,), jnp.int32),
            pltpu.SemaphoreType.DMA((groups,)),
        ],
        compiler_params=pltpu.CompilerParams(vmem_limit_bytes=36 * MIB),
        cost_estimate=pl.CostEstimate(flops=0, bytes_accessed=20 * MIB, transcendentals=0),
        name="build_tile",
    )(at, live, rows, cols, slots)


def forward_kernel(chunk, first, tile_ref, *refs):
    *feature_refs, panel = refs
    if first:
        before_ref, (*feature_refs, send_ref, rest_ref) = feature_refs[0], feature_refs[1:]
    else:
        *feature_refs, sum_ref = feature_refs
    share = feature_refs[0].shape[0]
    for r, feature_ref in enumerate(feature_refs):
        panel[r * share : (r + 1) * share, :] = feature_ref[...]
    rows = tile_ref.shape[0] // CHUNKS
    half = rows // 2
    for m in range(0, rows, half):
        block = tile_ref[chunk * rows + m : chunk * rows + m + half, first * share : first * share + panel.shape[0]]
        product = jnp.dot(block, panel[...], preferred_element_type=jnp.float32)
        if first:
            into = rest_ref if m else send_ref
            into[...] = (before_ref[m : m + half, :] + product).astype(jnp.bfloat16)
        else:
            sum_ref[m : m + half, :] = product


def forward(chunk, tile, features, first, before=None):
    share, width = features[0].shape
    rows = tile.shape[0] // CHUNKS
    vmem = pl.BlockSpec(memory_space=pltpu.VMEM)
    if first:
        given, out_shape = [before, *features], [pltpu.VMEM((rows // 2, width), jnp.bfloat16)] * 2
    else:
        given, out_shape = features, pltpu.VMEM((rows, width), jnp.float32)
    return pl.pallas_call(
        functools.partial(forward_kernel, chunk, first),
        out_shape=out_shape,
        in_specs=[vmem] * (1 + len(given)),
        out_specs=[vmem] * 2 if first else vmem,
        scratch_shapes=[pltpu.VMEM((len(features) * share, width), jnp.bfloat16)],
        compiler_params=pltpu.CompilerParams(vmem_limit_bytes=8 * MIB),
        cost_estimate=pl.CostEstimate(
            flops=2 * rows * len(features) * share * width, bytes_accessed=0, transcendentals=0
        ),
        name="forward",
    )(tile, *given)


def silu_slope(values):
    sig = jax.nn.sigmoid(values)
    return sig * (1.0 + values * (1.0 - sig))


def wide(values):
    return values.astype(jnp.float32)


def dot_last(left, right):
    return lax.dot_general(left, right, (((1,), (1,)), ((), ())), preferred_element_type=jnp.float32)


def combine_kernel(specs, *refs):
    out_refs = refs[-len(specs) :]
    for spec, out_ref in zip(specs, out_refs):
        total = None
        for source, start in spec:
            term = wide(refs[source][start : start + out_ref.shape[0], :])
            total = term if total is None else total + term
        out_ref[...] = total.astype(out_ref.dtype)


def combine(step, sums):
    sources = list({id(x): x for terms in sums for x, _ in terms}.values())
    at = {id(x): i for i, x in enumerate(sources)}
    specs = [[(at[id(x)], start) for x, start in terms] for terms in sums]
    vmem = pl.BlockSpec(memory_space=pltpu.VMEM)
    return pl.pallas_call(
        functools.partial(combine_kernel, specs),
        out_shape=[pltpu.VMEM((step, sources[0].shape[1]), jnp.bfloat16)] * len(sums),
        in_specs=[vmem] * len(sources),
        out_specs=[vmem] * len(sums),
        compiler_params=pltpu.CompilerParams(vmem_limit_bytes=4 * MIB),
        cost_estimate=LIGHT,
        name="combine",
    )(*sources)


def gate_kernel(chunk, starts, upstream_ref, weight_ref, *refs):
    *term_refs, turned_ref, grad_ref, rows_ref, summed_ref = refs
    step = grad_ref.shape[0]
    rows = None
    for term_ref, start in zip(term_refs, starts):
        term = wide(term_ref[start : start + step, :])
        rows = term if rows is None else rows + term
    high = rows.astype(jnp.bfloat16)
    low = (rows - wide(high)).astype(jnp.bfloat16)
    weight = weight_ref[...]
    summed = jnp.dot(high, weight, preferred_element_type=jnp.float32) + jnp.dot(
        low, weight, preferred_element_type=jnp.float32
    )
    upstream = upstream_ref[chunk * step : (chunk + 1) * step, :]
    grad = (upstream * silu_slope(summed)).astype(jnp.bfloat16)
    turned_ref[...] = dot_last(grad, weight).astype(jnp.bfloat16)
    grad_ref[...] = grad
    rows_ref[...] = high
    summed_ref[...] = summed


def gate(chunk, upstream, weight, terms):
    shape = (upstream.shape[0] // CHUNKS, upstream.shape[1])
    vmem = pl.BlockSpec(memory_space=pltpu.VMEM)
    return pl.pallas_call(
        functools.partial(gate_kernel, chunk, [start for _, start in terms]),
        out_shape=[pltpu.VMEM(shape, jnp.bfloat16)] * 3 + [pltpu.VMEM(shape, jnp.float32)],
        in_specs=[vmem] * (2 + len(terms)),
        out_specs=[vmem] * 4,
        compiler_params=pltpu.CompilerParams(vmem_limit_bytes=8 * MIB),
        cost_estimate=LIGHT,
        name="gate",
    )(upstream, weight, *(x for x, _ in terms))


def pack(values, exact_rows):
    exact = values[values.shape[0] - exact_rows :]
    high = exact.astype(jnp.bfloat16)
    low = (exact - wide(high)).astype(jnp.bfloat16)
    return jnp.concatenate([values[: -exact_rows].astype(jnp.bfloat16), high, low], axis=0)


def unpack(message, exact_rows):
    values = wide(message)
    rows = message.shape[0] - 2 * exact_rows
    exact = values[rows : rows + exact_rows] + values[rows + exact_rows :]
    return jnp.concatenate([values[:rows], exact], axis=0)


def local_sums(chunk, members_ref, cotangent_ref, rows_ref, grad_ref, summed_ref):
    step = rows_ref.shape[0]
    at = slice(chunk * step, (chunk + 1) * step)
    summed = summed_ref[...]
    activated = summed * jax.nn.sigmoid(summed)
    weight_part = lax.dot_general(
        rows_ref[...], grad_ref[...], (((0,), (0,)), ((), ())), preferred_element_type=jnp.float32
    )
    members = members_ref[:, at]
    part_terms = jnp.dot(
        members,
        wide(cotangent_ref[at, :]) * activated,
        precision=lax.Precision.HIGHEST,
        preferred_element_type=jnp.float32,
    )
    sizes = jnp.sum(members, axis=1, keepdims=True)
    return jnp.concatenate([weight_part, part_terms, jnp.broadcast_to(sizes, part_terms.shape)], axis=0)


def local_first_kernel(members_ref, cotangent_ref, *refs):
    *given, sums_ref = refs
    sums_ref[...] = local_sums(0, members_ref, cotangent_ref, *given)


def local_last_kernel(at_ref, members_ref, cotangent_ref, before_ref, *refs):
    *given, keep_ref, send_ref, sums = refs
    terms = local_sums(CHUNKS - 1, members_ref, cotangent_ref, *given)
    sums[...] = before_ref[...] + terms
    core = at_ref[1] & 1
    count = members_ref.shape[0]
    width = sums.shape[1]
    rows = width // 2
    for half, message_ref in ((core, keep_ref), (1 - core, send_ref)):
        top = sums[pl.ds(pl.multiple_of(half * rows, rows), rows), :]
        bottom = sums[pl.ds(pl.multiple_of(width + half * count, count), count), :]
        message_ref[...] = pack(jnp.concatenate([top, bottom], axis=0), count)


def local_terms(at, members, cotangent, chunks):
    width = cotangent.shape[1]
    count = members.shape[0]
    vmem = pl.BlockSpec(memory_space=pltpu.VMEM)
    smem = pl.BlockSpec(memory_space=pltpu.SMEM)
    first, last = chunks
    sums = jax.ShapeDtypeStruct((width + 2 * count, width), jnp.float32)
    before = pl.pallas_call(
        local_first_kernel,
        out_shape=pltpu.VMEM(sums.shape, sums.dtype),
        in_specs=[vmem] * 5,
        out_specs=vmem,
        compiler_params=pltpu.CompilerParams(vmem_limit_bytes=8 * MIB),
        cost_estimate=LIGHT,
        name="local_first",
    )(members, cotangent, *first)
    message = pltpu.VMEM((width // 2 + 2 * count, width), jnp.bfloat16)
    return pl.pallas_call(
        local_last_kernel,
        out_shape=[message, message],
        in_specs=[smem] + [vmem] * 6,
        out_specs=[vmem] * 2,
        scratch_shapes=[pltpu.VMEM(sums.shape, sums.dtype)],
        compiler_params=pltpu.CompilerParams(vmem_limit_bytes=8 * MIB),
        cost_estimate=LIGHT,
        name="local_last",
    )(at, members, cotangent, before, *last)


def output_kernel(gains_ref, *refs):
    *summed_refs, out_ref = refs
    step = summed_refs[0].shape[0]
    for n, summed_ref in enumerate(summed_refs):
        at = slice(n * step, (n + 1) * step)
        summed = summed_ref[...]
        out_ref[at, :] = (summed * jax.nn.sigmoid(summed) * gains_ref[at, :]).astype(out_ref.dtype)


def output(gains, summed):
    vmem = pl.BlockSpec(memory_space=pltpu.VMEM)
    return pl.pallas_call(
        output_kernel,
        out_shape=jax.ShapeDtypeStruct(gains.shape, jnp.bfloat16),
        in_specs=[vmem] * (1 + len(summed)),
        out_specs=vmem,
        compiler_params=pltpu.CompilerParams(vmem_limit_bytes=8 * MIB),
        cost_estimate=LIGHT,
        name="output",
    )(gains, *summed)


def add_kernel(exact_rows, own_ref, other_ref, out_ref):
    out_ref[...] = pack(
        unpack(own_ref[...], exact_rows) + unpack(other_ref[...], exact_rows), exact_rows
    )


def add_messages(exact_rows, own, other):
    vmem = pl.BlockSpec(memory_space=pltpu.VMEM)
    return pl.pallas_call(
        functools.partial(add_kernel, exact_rows),
        out_shape=pltpu.VMEM(own.shape, jnp.bfloat16),
        in_specs=[vmem] * 2,
        out_specs=vmem,
        compiler_params=pltpu.CompilerParams(vmem_limit_bytes=4 * MIB),
        cost_estimate=LIGHT,
        name="add_messages",
    )(own, other)


def totals_kernel(exact_rows, scale, at_ref, own_ref, other_ref, weight_ref, gain_ref, exact):
    core = at_ref[1] & 1
    rows = weight_ref.shape[0] // 2
    for half, message_ref in ((core, own_ref), (1 - core, other_ref)):
        values = unpack(message_ref[...], exact_rows)
        weight_ref[pl.ds(pl.multiple_of(half * rows, rows), rows), :] = values[:rows] * scale
        exact[pl.ds(pl.multiple_of(half * exact_rows, exact_rows), exact_rows), :] = values[rows:]
    gain_ref[...] = exact[:exact_rows, :] / jnp.sqrt(exact[exact_rows:, :])


def totals(exact_rows, scale, at, own, other):
    width = own.shape[1]
    vmem = pl.BlockSpec(memory_space=pltpu.VMEM)
    smem = pl.BlockSpec(memory_space=pltpu.SMEM)
    return pl.pallas_call(
        functools.partial(totals_kernel, exact_rows, scale),
        out_shape=[
            jax.ShapeDtypeStruct((width, width), jnp.float32),
            jax.ShapeDtypeStruct((exact_rows, width), jnp.float32),
        ],
        in_specs=[smem] + [vmem] * 2,
        out_specs=[vmem] * 2,
        scratch_shapes=[pltpu.VMEM((2 * exact_rows, width), jnp.float32)],
        compiler_params=pltpu.CompilerParams(vmem_limit_bytes=4 * MIB),
        cost_estimate=LIGHT,
        name="totals",
    )(at, own, other)


def backward_kernel(chunk, targets, places, tile_ref, *refs):
    given, out_refs = refs[: -len(targets) - 1], refs[-len(targets) - 1 :]
    before_refs, block_refs = given[: len(given) - len(places)], given[len(given) - len(places) :]
    *part_refs, panel = out_refs
    for block_ref, (source, target, rows) in zip(block_refs, places):
        panel[target : target + rows, :] = block_ref[source : source + rows, :]
    share = part_refs[0].shape[0]
    depth = panel.shape[0]
    for i, r in enumerate(targets):
        product = lax.dot_general(
            tile_ref[chunk * depth : (chunk + 1) * depth, r * share : (r + 1) * share],
            panel[...],
            (((0,), (0,)), ((), ())),
            preferred_element_type=jnp.float32,
        )
        if before_refs:
            product = product + before_refs[i][...]
        part_refs[i][...] = product.astype(part_refs[i].dtype)


def backward(chunk, targets, kinds, tile, blocks, places, before, share):
    width = blocks[0].shape[1]
    depth = tile.shape[0] // CHUNKS
    vmem = pl.BlockSpec(memory_space=pltpu.VMEM)
    flops = (1 if chunk else 2) * depth * len(targets) * share * width
    return pl.pallas_call(
        functools.partial(backward_kernel, chunk, targets, places),
        out_shape=[pltpu.VMEM((share, width), kind) for kind in kinds]
        + [pltpu.VMEM((depth, width), jnp.bfloat16)],
        in_specs=[vmem] * (1 + len(before) + len(blocks)),
        out_specs=[vmem] * (len(targets) + 1),
        compiler_params=pltpu.CompilerParams(vmem_limit_bytes=8 * MIB),
        cost_estimate=pl.CostEstimate(flops=flops, bytes_accessed=0, transcendentals=0),
        name="backward",
    )(tile, *before, *blocks)


def finish_kernel(*refs):
    *part_refs, out_ref = refs
    total = None
    for part_ref in part_refs:
        term = wide(part_ref[...])
        total = term if total is None else total + term
    out_ref[...] = total.astype(out_ref.dtype)


def finish(parts):
    vmem = pl.BlockSpec(memory_space=pltpu.VMEM)
    return pl.pallas_call(
        finish_kernel,
        out_shape=jax.ShapeDtypeStruct(parts[0].shape, jnp.bfloat16),
        in_specs=[vmem] * len(parts),
        out_specs=vmem,
        compiler_params=pltpu.CompilerParams(vmem_limit_bytes=8 * MIB),
        cost_estimate=LIGHT,
        name="finish",
    )(*parts)


def swap(values, axis, mask, count):
    return lax.ppermute(values, axis, [(d, d ^ mask) for d in range(count)])


def after(values, *others):
    return lax.optimization_barrier((values, *others))[0]


def dense_device(
    row_count,
    col_count,
    features,
    weight,
    adjacency,
    block_rows,
    block_cols,
    live_blocks,
    part_gains,
    partition,
    cotangent,
):
    share, width = features.shape
    step = share // CHUNKS
    row_blocks = share * col_count // BLOCK
    at = jnp.stack([lax.axis_index("row"), lax.axis_index("col")]).astype(jnp.int32)
    gathered = [features] + [swap(features, "row", r, row_count) for r in range(1, row_count)]
    layout = (col_count, share // BLOCK, step // BLOCK)
    tile = build_tile(
        at, adjacency, block_rows, block_cols, live_blocks, row_blocks, share * row_count // BLOCK, layout
    )
    part_count = part_gains.shape[0]
    members = (
        partition[None, :] == jnp.arange(part_count, dtype=jnp.int32)[:, None]
    ).astype(jnp.float32)
    row_gains = lax.dot_general(
        members, part_gains, (((0,), (0,)), ((), ())), precision=lax.Precision.HIGHEST
    )
    upstream = wide(cotangent) * row_gains

    order = block_order(col_count)
    col_bits = bits_of(col_count)
    chunks = range(CHUNKS)
    early = row_count // 2
    sums = [forward(n, tile, gathered[:early], 0) for n in chunks]
    pending = []
    for n in chunks:
        send, rest = forward(n, tile, gathered[early:], early, sums[n])
        other = swap(send, "col", col_bits[0], col_count)
        kept = enumerate(order[len(order) // 2 :])
        pending.append({k: [(rest, t * step), (other, t * step)] for t, k in kept})
    last = None
    for bit in col_bits[1:]:
        for terms in pending:
            blocks = sorted((k for k in terms if k & bit), reverse=True)
            sums = [terms.pop(k) for k in blocks]
            if last is not None:
                x, start = sums[0][-1]
                sums[0][-1] = (after(x, last), start)
            outs = combine(step, sums)
            last = outs[0]
            for k, out in zip(blocks, outs):
                terms[k ^ bit].append((swap(out, "col", bit, col_count), 0))
    gated, held = [], []
    for n in chunks:
        gated.append(gate(n, after(upstream, last), weight, pending[n][0]))
        last = gated[-1][0]
        held.append({0: last})
    scale = 1.0 / math.sqrt(share * row_count * col_count)
    local = [(rows, grad, summed) for _, grad, rows, summed in gated]
    message, out = local_terms(at, members, cotangent, local)
    other = swap(out, "col", col_bits[0], col_count)
    messages = [add_messages(part_count, message, other)]
    for bit in reversed(col_bits[1:]):
        for n in chunks:
            for k in list(held[n]):
                sent = held[n][k]
                if k and n == 0:
                    sent = after(sent, message)
                if k and n:
                    sent = after(sent, messages[0], *held[n].values())
                held[n][k ^ bit] = swap(sent, "col", bit, col_count)
    stages = [("row", bit, row_count) for bit in bits_of(row_count)]
    stages += [("col", bit, col_count) for bit in col_bits[1:]]
    for stage in stages:
        messages.append(add_messages(part_count, messages[-1], swap(messages[-1], *stage)))
    other = swap(messages[-1], "col", col_bits[0], col_count)
    weight_grad, gain_grad = totals(part_count, scale, at, messages[-1], other)

    layer_out = output(after(row_gains, messages[4]), [g[3] for g in gated])
    sums = []
    bit = col_bits[0]
    for n in chunks:
        blocks, places = [], []
        *ready, late = held[n]
        for group in (ready, [late]):
            sent = jnp.concatenate([held[n][k] for k in group], axis=0)
            if n and group is not ready:
                sent = after(sent, messages[2])
            arrived = swap(sent, "col", bit, col_count)
            for t, k in enumerate(group):
                blocks += [held[n][k], arrived]
                places += [(0, order.index(k) * step, step), (t * step, order.index(k ^ bit) * step, step)]
        rows = list(range(row_count))
        if n < CHUNKS - 1:
            kinds = [jnp.float32] * row_count
            *sums, _ = backward(n, rows, kinds, tile, blocks, places, sums, share)
    parts = [None] * row_count
    farthest = row_count - 1
    for targets in ([farthest], rows[1:farthest], [0]):
        if not targets:
            continue
        kinds = [jnp.float32 if r == 0 else jnp.bfloat16 for r in targets]
        *outs, panel = backward(
            CHUNKS - 1, targets, kinds, tile, blocks, places, [sums[r] for r in targets], share
        )
        blocks, places = [after(panel, messages[3], *outs)], [(0, 0, panel.shape[0])]
        for r, out in zip(targets, outs):
            parts[r] = swap(out, "row", r, row_count) if r else out
    feature_grad = finish(parts)

    return (layer_out, feature_grad, weight_grad, gain_grad)


def slot_sum(tile_values, row_index, col_index, live_count, panels, out_blocks, forward_way):
    slot_count = tile_values.shape[0]
    feature_width = panels.shape[1]
    panel_blocks = panels.reshape(-1, BLOCK, feature_width)

    def one_slot(slot, totals):
        values = lax.dynamic_index_in_dim(tile_values, slot, 0, keepdims=False)
        source, target = col_index[slot], row_index[slot]
        if not forward_way:
            values, source, target = values.T, target, source
        panel = lax.dynamic_index_in_dim(panel_blocks, source, 0, keepdims=False)
        product = jnp.dot(values, panel, preferred_element_type=jnp.float32)
        return totals.at[target].add(product)

    start = jnp.zeros((out_blocks, BLOCK, feature_width), jnp.float32)
    totals = lax.fori_loop(0, jnp.minimum(live_count, slot_count), one_slot, start)
    return totals.reshape(out_blocks * BLOCK, feature_width)


def slot_device(
    features,
    weight,
    adjacency,
    block_rows,
    block_cols,
    live_blocks,
    part_gains,
    partition,
    cotangent,
):
    node_count = features.shape[0]
    row_total = node_count * lax.axis_size("col") // BLOCK
    col_total = node_count * lax.axis_size("row") // BLOCK
    slots = (adjacency[0, 0], block_rows[0, 0], block_cols[0, 0], live_blocks[0, 0])
    hidden = jnp.dot(features, weight, preferred_element_type=jnp.float32).astype(jnp.bfloat16)
    panels = lax.all_gather(hidden, "row", axis=0, tiled=True)
    member = (
        partition[:, None] == jnp.arange(part_gains.shape[0], dtype=jnp.int32)[None, :]
    ).astype(jnp.float32)
    row_gains = jnp.dot(member, part_gains, precision=lax.Precision.HIGHEST)
    upstream = cotangent.astype(jnp.float32) * row_gains
    partial_rows = slot_sum(*slots, panels, row_total, True)
    summed = lax.psum_scatter(
        partial_rows.astype(jnp.bfloat16), "col", scatter_dimension=0, tiled=True
    ).astype(jnp.float32)
    local_grad = (upstream * silu_slope(summed)).astype(jnp.bfloat16)
    agg_grad = lax.all_gather(local_grad, "col", axis=0, tiled=True)
    activated = jax.nn.silu(summed)
    layer_out = (activated * row_gains).astype(jnp.bfloat16)
    partial_cols = slot_sum(*slots, agg_grad, col_total, False)
    hidden_grad = lax.psum_scatter(
        partial_cols.astype(jnp.bfloat16), "row", scatter_dimension=0, tiled=True
    )
    feature_grad = lax.dot_general(
        hidden_grad, weight, (((1,), (1,)), ((), ())), preferred_element_type=jnp.float32
    ).astype(jnp.bfloat16)
    weight_part = lax.dot_general(
        features, hidden_grad, (((0,), (0,)), ((), ())), preferred_element_type=jnp.float32
    )
    part_terms = jnp.dot(
        member.T, cotangent.astype(jnp.float32) * activated, precision=lax.Precision.HIGHEST
    )
    part_sizes = jnp.sum(member, axis=0)
    weight_total, part_total, size_total = lax.psum(
        (weight_part, part_terms, part_sizes), ("row", "col")
    )
    total_nodes = node_count * lax.axis_size("row") * lax.axis_size("col")
    weight_grad = weight_total / jnp.sqrt(jnp.float32(total_nodes))
    gain_grad = part_total / jnp.sqrt(size_total)[:, None]
    return (layer_out, feature_grad, weight_grad, gain_grad)


def solution(mesh):
    row_count, col_count = mesh.shape["row"], mesh.shape["col"]

    def per_device(features, *others):
        share = features.shape[0]
        tile_bytes = 2 * share**2 * row_count * col_count
        sizes = (row_count // 2, col_count // 2, share // (BLOCK * CHUNKS))
        whole = share % (BLOCK * CHUNKS) == 0 and others[1].shape[2] % GROUP == 0
        if tile_bytes <= 20 * MIB and whole and all(n & (n - 1) == 0 < n for n in sizes):
            return dense_device(row_count, col_count, features, *others)
        return slot_device(features, *others)

    in_specs = (
        P(("row", "col"), None),
        P(),
        P("row", "col", None, None, None),
        P("row", "col", None),
        P("row", "col", None),
        P("row", "col"),
        P(),
        P(("row", "col")),
        P(("row", "col"), None),
    )
    out_specs = (P(("row", "col"), None), P(("row", "col"), None), P(), P())
    return jax.shard_map(
        per_device, mesh=mesh, in_specs=in_specs, out_specs=out_specs, check_vma=False
    )
```

time: 91.5 us -> 83.9 us (0.917)
  Pallas kernels: 25.1 us -> 20.5 us
  waiting for transfers between devices: 29.2 us -> 27 us
    pallas_call x1, Pallas kernels: 7.78 us -> 3.91 us  [build_tile(): pl.pallas_call(functools.partial(build_kernel, layout), out_shape=pltpu.V...]
    ppermute x28 -> x30, waiting for transfers between devices: 29.2 us -> 27 us  [swap(): return lax.ppermute(values, axis, [(d, d ^ mask) for d in range(count)])]
    ppermute x28 -> x30, starting transfers between devices: 33.5 us -> 32.7 us  [swap(): return lax.ppermute(values, axis, [(d, d ^ mask) for d in range(count)])]
    pallas_call x6 -> x12, Pallas kernels: 14.9 us -> 14.1 us  [the longest x4 6.22 us: backward(): pl.pallas_call(functools.partial(backward_kernel, chunk, targets, places)...]
  transfers between devices with their start and end apart: 28 -> 30, of which waited for: 12 -> 11; matrix products, arithmetic and copies ran while one was open for 1% -> 1% of each run, Pallas kernels for 23% -> 19%
where the time goes in v4:
time: 83.9 us; the launch traced here: 83.7 us
  starting transfers between devices  32.7 us (39%)
  waiting for transfers between devices  27 us (32%)
  Pallas kernels  20.5 us (24%)
  between operations  1.55 us (2%)
  local copies, waits for them, and re-layouts  1.39 us (2%)
    ppermute x30, starting transfers between devices, swap(): return lax.ppermute(values, axis, [(d, d ^ mask) for d in range(count)])  32.7 us
    ppermute x30, waiting for transfers between devices, swap(): return lax.ppermute(values, axis, [(d, d ^ mask) for d in range(count)])  27 us
    pallas_call x4, Pallas kernels, backward(): pl.pallas_call(functools.partial(backward_kernel, chunk, targets, places)...  6.22 us
    pallas_call x4, Pallas kernels, forward(): pl.pallas_call(functools.partial(forward_kernel, chunk, first), out_shape...  5.03 us
    pallas_call x1, Pallas kernels, build_tile(): pl.pallas_call(functools.partial(build_kernel, layout), out_shape=pltpu.V...  3.91 us
  transfers between devices with their start and end apart: 30, of which 11 were waited for; matrix products, arithmetic and copies ran while one was open for 1% of the time, Pallas kernels for 19%

profile of v4, /device:TPU:0, one launch (start us, length us, event | category | flops | bytes accessed | tf_op | source)
XLA Modules:
  0.0 83.7 jit_solution(10139982064818293487)
XLA Ops:
  0.6 3.0 %collective-permute-start = (bf16[512,256]{1,0:T(8,128)(2,1)}, bf16[512,256]{1,0:T(8,128)(2,1)S(1)}, u32[]{:S(2)}, u32[]{:S(2)}) collective-permute-start(bf16[512,256]{1,0:T(8,128)(2,1)} %refs_0_.3), channel_id=1, source_target_pairs={{0,8},{8,0},{16,24},{24,16},{1,9},{9,1},{17,25},{25,17},{2,10},{10... | collective-permute-start | bytes 786440 | tf_op jit(solution)/shard_map/ppermute | solution.py:465
  3.6 1.5 %collective-permute-start.1 = (bf16[512,256]{1,0:T(8,128)(2,1)}, bf16[512,256]{1,0:T(8,128)(2,1)S(1)}, u32[]{:S(2)}, u32[]{:S(2)}) collective-permute-start(bf16[512,256]{1,0:T(8,128)(2,1)} %refs_0_.3), channel_id=1, source_target_pairs={{0,16},{8,24},{16,0},{24,8},{1,17},{9,25},{17,1},{25,9},{2,18},{10... | collective-permute-start | bytes 786440 | tf_op jit(solution)/shard_map/ppermute | solution.py:465
  5.9 0.7 copy-done.4
  6.6 0.7 copy-done.5
  7.3 3.9 %build_tile.1.tile_ref = bf16[4096,2048]{1,0:T(8,128)(2,1)S(1)} custom-call(s32[2]{0:T(128)S(1)} %pad_add_fusion.at_ref, s32[1,1]{1,0:T(1,128)S(6)} %copy.13.live_ref, s32[1,1,384]{2,1,0:T(1,128)S(1)} %copy-done.4, s32[1,1,384]{2,1,0:T(1,128)S(1)} %copy-done.5, bf16[1,1,384,128,128]{4,3,2,1,0:T(8,128)(2,1)} %slots_ref.1), custom_call_target="tpu_custom_call" | custom-call | bytes 20971520 | tf_op jit(solution)/shard_map/build_tile/pallas_call | solution.py:119
  11.2 1.2 %forward.6.refs_0_ = f32[2048,256]{1,0:T(8,128)S(1)} custom-call(bf16[4096,2048]{1,0:T(8,128)(2,1)S(1)} %build_tile.1.tile_ref, bf16[512,256]{1,0:T(8,128)(2,1)S(1)} %copy-done.2, bf16[512,256]{1,0:T(8,128)(2,1)S(1)} %collective-permute-done.refs_1_), custom_call_target="tpu_custom_call" | custom-call | flops 1073741824 | tf_op jit(solution)/shard_map/forward/pallas_call | solution.py:166
  12.5 4.8 %collective-permute-done.1.refs_1_ = bf16[512,256]{1,0:T(8,128)(2,1)S(1)} collective-permute-done((bf16[512,256]{1,0:T(8,128)(2,1)}, bf16[512,256]{1,0:T(8,128)(2,1)S(1)}, u32[]{:S(2)}, u32[]{:S(2)}) %collective-permute-start.1) | collective-permute-done | bytes 262176 | tf_op jit(solution)/shard_map/ppermute | solution.py:465
  17.2 1.3 %forward.7 = (bf16[1024,256]{1,0:T(8,128)(2,1)S(1)}, bf16[1024,256]{1,0:T(8,128)(2,1)S(1)}) custom-call(bf16[4096,2048]{1,0:T(8,128)(2,1)S(1)} %build_tile.1.tile_ref, f32[2048,256]{1,0:T(8,128)S(1)} %forward.6.refs_0_, bf16[512,256]{1,0:T(8,128)(2,1)S(1)} %collective-permute-done.1.refs_1_, bf16[512,256]{1,0:T(8,128)(2,1)S(1)} %collective-permute-done.2.refs_2_), custom_call_target="tpu_custom_call" | custom-call | flops 1073741824 | tf_op jit(solution)/shard_map/forward/pallas_call | solution.py:166
  18.6 1.2 %forward.4.refs_0_ = f32[2048,256]{1,0:T(8,128)S(1)} custom-call(bf16[4096,2048]{1,0:T(8,128)(2,1)S(1)} %build_tile.1.tile_ref, bf16[512,256]{1,0:T(8,128)(2,1)S(1)} %copy-done.2, bf16[512,256]{1,0:T(8,128)(2,1)S(1)} %collective-permute-done.refs_1_), custom_call_target="tpu_custom_call" | custom-call | flops 1073741824 | tf_op jit(solution)/shard_map/forward/pallas_call | solution.py:166
  19.9 1.3 %forward.5 = (bf16[1024,256]{1,0:T(8,128)(2,1)S(1)}, bf16[1024,256]{1,0:T(8,128)(2,1)S(1)}) custom-call(bf16[4096,2048]{1,0:T(8,128)(2,1)S(1)} %build_tile.1.tile_ref, f32[2048,256]{1,0:T(8,128)S(1)} %forward.4.refs_0_, bf16[512,256]{1,0:T(8,128)(2,1)S(1)} %collective-permute-done.1.refs_1_, bf16[512,256]{1,0:T(8,128)(2,1)S(1)} %collective-permute-done.2.refs_2_), custom_call_target="tpu_custom_call" | custom-call | flops 1073741824 | tf_op jit(solution)/shard_map/forward/pallas_call | solution.py:166
  21.2 0.6 collective-permute-start.3
  21.8 1.6 %collective-permute-start.6 = (bf16[256,256]{1,0:T(8,128)(2,1)S(1)}, bf16[256,256]{1,0:T(8,128)(2,1)S(1)}, u32[]{:S(2)}, u32[]{:S(2)}) collective-permute-start(bf16[256,256]{1,0:T(8,128)(2,1)S(1)} %get-tuple-element.49), channel_id=1, source_target_pairs={{0,2},{1,3},{2,0},{3,1},{4,6},{5,7},{6,4},{7,5},{8,10},{9,11},{10,... | collective-permute-start | bytes 393224 | tf_op jit(solution)/shard_map/ppermute | solution.py:465
  23.5 1.5 %collective-permute-start.5 = (bf16[256,256]{1,0:T(8,128)(2,1)S(1)}, bf16[256,256]{1,0:T(8,128)(2,1)S(1)}, u32[]{:S(2)}, u32[]{:S(2)}) collective-permute-start(bf16[256,256]{1,0:T(8,128)(2,1)S(1)} %get-tuple-element.51), channel_id=1, source_target_pairs={{0,2},{1,3},{2,0},{3,1},{4,6},{5,7},{6,4},{7,5},{8,10},{9,11},{10,... | collective-permute-start | bytes 393224 | tf_op jit(solution)/shard_map/ppermute | solution.py:465
  25.0 0.6 collective-permute-start.7
  25.6 2.6 %collective-permute-done.6.refs_2_ = bf16[256,256]{1,0:T(8,128)(2,1)S(1)} collective-permute-done((bf16[256,256]{1,0:T(8,128)(2,1)S(1)}, bf16[256,256]{1,0:T(8,128)(2,1)S(1)}, u32[]{:S(2)}, u32[]{:S(2)}) %collective-permute-start.6) | collective-permute-done | bytes 131104 | tf_op jit(solution)/shard_map/ppermute | solution.py:465
  28.3 2.6 %collective-permute-start.8 = (bf16[256,256]{1,0:T(8,128)(2,1)S(1)}, bf16[256,256]{1,0:T(8,128)(2,1)S(1)}, u32[]{:S(2)}, u32[]{:S(2)}) collective-permute-start(bf16[256,256]{1,0:T(8,128)(2,1)S(1)} %combine.6), channel_id=1, source_target_pairs={{0,4},{1,5},{2,6},{3,7},{4,0},{5,1},{6,2},{7,3},{8,12},{9,13},{10,... | collective-permute-start | bytes 393224 | tf_op jit(solution)/shard_map/ppermute | solution.py:465
  30.9 0.4 convert_multiply_fusion
  31.4 1.6 %collective-permute-start.9 = (bf16[256,256]{1,0:T(8,128)(2,1)S(1)}, bf16[256,256]{1,0:T(8,128)(2,1)S(1)}, u32[]{:S(2)}, u32[]{:S(2)}) collective-permute-start(bf16[256,256]{1,0:T(8,128)(2,1)S(1)} %get-tuple-element.61), channel_id=1, source_target_pairs={{0,2},{1,3},{2,0},{3,1},{4,6},{5,7},{6,4},{7,5},{8,10},{9,11},{10,... | collective-permute-start | bytes 393224 | tf_op jit(solution)/shard_map/ppermute | solution.py:465
  33.1 1.2 %collective-permute-start.10 = (bf16[256,256]{1,0:T(8,128)(2,1)S(1)}, bf16[256,256]{1,0:T(8,128)(2,1)S(1)}, u32[]{:S(2)}, u32[]{:S(2)}) collective-permute-start(bf16[256,256]{1,0:T(8,128)(2,1)S(1)} %combine.7), channel_id=1, source_target_pairs={{0,4},{1,5},{2,6},{3,7},{4,0},{5,1},{6,2},{7,3},{8,12},{9,13},{10,... | collective-permute-start | bytes 393224 | tf_op jit(solution)/shard_map/ppermute | solution.py:465
  34.2 3.6 %collective-permute-done.7.refs_2_ = bf16[256,256]{1,0:T(8,128)(2,1)S(1)} collective-permute-done((bf16[256,256]{1,0:T(8,128)(2,1)S(1)}, bf16[256,256]{1,0:T(8,128)(2,1)S(1)}, u32[]{:S(2)}, u32[]{:S(2)}) %collective-permute-start.7) | collective-permute-done | bytes 131104 | tf_op jit(solution)/shard_map/ppermute | solution.py:465
  38.3 1.5 %collective-permute-start.17 = (bf16[256,256]{1,0:T(8,128)(2,1)S(1)}, bf16[256,256]{1,0:T(8,128)(2,1)S(1)}, u32[]{:S(2)}, u32[]{:S(2)}) collective-permute-start(bf16[256,256]{1,0:T(8,128)(2,1)S(1)} %get-tuple-element.59.refs_0_), channel_id=1, source_target_pairs={{0,2},{1,3},{2,0},{3,1},{4,6},{5,7},{6,4},{7,5},{8,10},{9,11},{10,... | collective-permute-start | bytes 393224 | tf_op jit(solution)/shard_map/ppermute | solution.py:465
  39.7 3.3 %collective-permute-start.16 = (bf16[256,256]{1,0:T(8,128)(2,1)S(1)}, bf16[256,256]{1,0:T(8,128)(2,1)S(1)}, u32[]{:S(2)}, u32[]{:S(2)}) collective-permute-start(bf16[256,256]{1,0:T(8,128)(2,1)S(1)} %get-tuple-element.59.refs_0_), channel_id=1, source_target_pairs={{0,4},{1,5},{2,6},{3,7},{4,0},{5,1},{6,2},{7,3},{8,12},{9,13},{10,... | collective-permute-start | bytes 393224 | tf_op jit(solution)/shard_map/ppermute | solution.py:465
  43.5 1.9 %collective-permute-start.22 = (bf16[256,256]{1,0:T(8,128)(2,1)S(1)}, bf16[256,256]{1,0:T(8,128)(2,1)S(1)}, u32[]{:S(2)}, u32[]{:S(2)}) collective-permute-start(bf16[256,256]{1,0:T(8,128)(2,1)S(1)} %get-tuple-element.73.refs_1_), channel_id=1, source_target_pairs={{0,2},{1,3},{2,0},{3,1},{4,6},{5,7},{6,4},{7,5},{8,10},{9,11},{10,... | collective-permute-start | bytes 393224 | tf_op jit(solution)/shard_map/ppermute | solution.py:465
  45.4 2.7 %collective-permute-start.21 = (bf16[256,256]{1,0:T(8,128)(2,1)S(1)}, bf16[256,256]{1,0:T(8,128)(2,1)S(1)}, u32[]{:S(2)}, u32[]{:S(2)}) collective-permute-start(bf16[256,256]{1,0:T(8,128)(2,1)S(1)} %get-tuple-element.73.refs_1_), channel_id=1, source_target_pairs={{0,4},{1,5},{2,6},{3,7},{4,0},{5,1},{6,2},{7,3},{8,12},{9,13},{10,... | collective-permute-start | bytes 393224 | tf_op jit(solution)/shard_map/ppermute | solution.py:465
  48.3 0.9 %local_last.1 = (bf16[160,256]{1,0:T(8,128)(2,1)S(1)}, bf16[160,256]{1,0:T(8,128)(2,1)S(1)}) custom-call(s32[2]{0:T(128)S(1)} %pad_add_fusion.at_ref, f32[16,512]{1,0:T(8,128)S(1)} %fusion.members_ref, bf16[512,256]{1,0:T(8,128)(2,1)S(1)} %copy-done.1, f32[288,256]{1,0:T(8,128)S(1)} %local_first.1.before_ref, ...), custom_call_target="tpu_custom_call" | custom-call | flops 1 | bytes 1 | tf_op jit(solution)/shard_map/local_last/pallas_call | solution.py:323
  49.4 0.5 collective-permute-start.18
  50.0 0.7 collective-permute-done.11.other_ref
  50.6 1.2 %collective-permute-start.12 = (bf16[160,256]{1,0:T(8,128)(2,1)S(1)}, bf16[160,256]{1,0:T(8,128)(2,1)S(1)}, u32[]{:S(2)}, u32[]{:S(2)}) collective-permute-start(bf16[160,256]{1,0:T(8,128)(2,1)S(1)} %add_messages.5.own_ref), channel_id=1, source_target_pairs={{0,8},{8,0},{16,24},{24,16},{1,9},{9,1},{17,25},{25,17},{2,10},{10... | collective-permute-start | bytes 245768 | tf_op jit(solution)/shard_map/ppermute | solution.py:465
  51.9 0.6 collective-permute-done.22.refs_5_
  52.7 2.5 %collective-permute-done.12.other_ref = bf16[160,256]{1,0:T(8,128)(2,1)S(1)} collective-permute-done((bf16[160,256]{1,0:T(8,128)(2,1)S(1)}, bf16[160,256]{1,0:T(8,128)(2,1)S(1)}, u32[]{:S(2)}, u32[]{:S(2)}) %collective-permute-start.12) | collective-permute-done | bytes 81952 | tf_op jit(solution)/shard_map/ppermute | solution.py:465
  55.2 1.6 %collective-permute-start.13 = (bf16[160,256]{1,0:T(8,128)(2,1)S(1)}, bf16[160,256]{1,0:T(8,128)(2,1)S(1)}, u32[]{:S(2)}, u32[]{:S(2)}) collective-permute-start(bf16[160,256]{1,0:T(8,128)(2,1)S(1)} %add_messages.6.own_ref), channel_id=1, source_target_pairs={{0,16},{8,24},{16,0},{24,8},{1,17},{9,25},{17,1},{25,9},{2,18},{10... | collective-permute-start | bytes 245768 | tf_op jit(solution)/shard_map/ppermute | solution.py:465
  57.1 2.6 %collective-permute-done.13.other_ref = bf16[160,256]{1,0:T(8,128)(2,1)S(1)} collective-permute-done((bf16[160,256]{1,0:T(8,128)(2,1)S(1)}, bf16[160,256]{1,0:T(8,128)(2,1)S(1)}, u32[]{:S(2)}, u32[]{:S(2)}) %collective-permute-start.13) | collective-permute-done | bytes 81952 | tf_op jit(solution)/shard_map/ppermute | solution.py:465
  59.8 0.5 collective-permute-start.14
  60.3 2.4 %collective-permute-done.24.refs_7_ = bf16[256,256]{1,0:T(8,128)(2,1)S(1)} collective-permute-done((bf16[256,256]{1,0:T(8,128)(2,1)S(1)}, bf16[256,256]{1,0:T(8,128)(2,1)S(1)}, u32[]{:S(2)}, u32[]{:S(2)}) %collective-permute-start.24) | collective-permute-done | bytes 131104 | tf_op jit(solution)/shard_map/ppermute | solution.py:465
  62.7 1.6 %collective-permute-done.14.other_ref = bf16[160,256]{1,0:T(8,128)(2,1)S(1)} collective-permute-done((bf16[160,256]{1,0:T(8,128)(2,1)S(1)}, bf16[160,256]{1,0:T(8,128)(2,1)S(1)}, u32[]{:S(2)}, u32[]{:S(2)}) %collective-permute-start.14) | collective-permute-done | bytes 81952 | tf_op jit(solution)/shard_map/ppermute | solution.py:465
  64.3 2.6 %backward.4 = (f32[512,256]{1,0:T(8,128)S(1)}, f32[512,256]{1,0:T(8,128)S(1)}, f32[512,256]{1,0:T(8,128)S(1)}, f32[512,256]{1,0:T(8,128)S(1)}, bf16[2048,256]{1,0:T(8,128)(2,1)}) custom-call(bf16[4096,2048]{1,0:T(8,128)(2,1)S(1)} %build_tile.1.tile_ref, bf16[256,256]{1,0:T(8,128)(2,1)S(1)} %get-tuple-element.59.refs_0_, ...), custom_call_target="tpu_custom_call" | custom-call | flops 2147483648 | tf_op jit(solution)/shard_map/backward/pallas_call | solution.py:430
  66.9 0.8 backward.5
  67.7 1.4 %backward.6 = (bf16[512,256]{1,0:T(8,128)(2,1)S(1)}, bf16[512,256]{1,0:T(8,128)(2,1)S(1)}, bf16[2048,256]{1,0:T(8,128)(2,1)S(1)}) custom-call(bf16[4096,2048]{1,0:T(8,128)(2,1)S(1)} %build_tile.1.tile_ref, f32[512,256]{1,0:T(8,128)S(1)} %get-tuple-element.70.refs_0_, f32[512,256]{1,0:T(8,128)S(1)} %get-tuple-element.71.refs_1_, ...), custom_call_target="tpu_custom_call" | custom-call | flops 536870912 | tf_op jit(solution)/shard_map/backward/pallas_call | solution.py:430
  69.1 1.2 %collective-permute-start.26 = (bf16[512,256]{1,0:T(8,128)(2,1)S(1)}, bf16[512,256]{1,0:T(8,128)(2,1)S(1)}, u32[]{:S(2)}, u32[]{:S(2)}) collective-permute-start(bf16[512,256]{1,0:T(8,128)(2,1)S(1)} %get-tuple-element.80), channel_id=1, source_target_pairs={{0,8},{8,0},{16,24},{24,16},{1,9},{9,1},{17,25},{25,17},{2,10},{10... | collective-permute-start | bytes 786440 | tf_op jit(solution)/shard_map/ppermute | solution.py:465
  70.3 1.0 %collective-permute-start.27 = (bf16[512,256]{1,0:T(8,128)(2,1)S(1)}, bf16[512,256]{1,0:T(8,128)(2,1)S(1)}, u32[]{:S(2)}, u32[]{:S(2)}) collective-permute-start(bf16[512,256]{1,0:T(8,128)(2,1)S(1)} %get-tuple-element.81), channel_id=1, source_target_pairs={{0,16},{8,24},{16,0},{24,8},{1,17},{9,25},{17,1},{25,9},{2,18},{10... | collective-permute-start | bytes 786440 | tf_op jit(solution)/shard_map/ppermute | solution.py:465
  71.2 1.4 %collective-permute-start.28 = (bf16[512,256]{1,0:T(8,128)(2,1)S(1)}, bf16[512,256]{1,0:T(8,128)(2,1)S(1)}, u32[]{:S(2)}, u32[]{:S(2)}) collective-permute-start(bf16[512,256]{1,0:T(8,128)(2,1)S(1)} %get-tuple-element.77), channel_id=1, source_target_pairs={{0,24},{8,16},{16,8},{24,0},{1,25},{9,17},{17,9},{25,1},{2,26},{10... | collective-permute-start | bytes 786440 | tf_op jit(solution)/shard_map/ppermute | solution.py:465
  72.7 1.0 %collective-permute-start.15 = (bf16[160,256]{1,0:T(8,128)(2,1)S(1)}, bf16[160,256]{1,0:T(8,128)(2,1)S(1)}, u32[]{:S(2)}, u32[]{:S(2)}) collective-permute-start(bf16[160,256]{1,0:T(8,128)(2,1)S(1)} %add_messages.8.own_ref), channel_id=1, source_target_pairs={{0,4},{1,5},{2,6},{3,7},{4,0},{5,1},{6,2},{7,3},{8,12},{9,13},{10,... | collective-permute-start | bytes 245768 | tf_op jit(solution)/shard_map/ppermute | solution.py:465
  73.7 5.1 %collective-permute-done.15.other_ref = bf16[160,256]{1,0:T(8,128)(2,1)S(1)} collective-permute-done((bf16[160,256]{1,0:T(8,128)(2,1)S(1)}, bf16[160,256]{1,0:T(8,128)(2,1)S(1)}, u32[]{:S(2)}, u32[]{:S(2)}) %collective-permute-start.15) | collective-permute-done | bytes 81952 | tf_op jit(solution)/shard_map/ppermute | solution.py:465
  78.9 0.8 output.1
  79.7 0.5 collective-permute-done.29.other_ref
  80.1 1.3 %totals.1 = (f32[256,256]{1,0:T(8,128)}, f32[16,256]{1,0:T(8,128)}) custom-call(s32[2]{0:T(128)S(1)} %pad_add_fusion.at_ref, bf16[160,256]{1,0:T(8,128)(2,1)S(1)} %add_messages.9.own_ref, bf16[160,256]{1,0:T(8,128)(2,1)S(1)} %collective-permute-done.29.other_ref), custom_call_target="tpu_custom_call" | custom-call | flops 1 | bytes 1 | tf_op jit(solution)/shard_map/totals/pallas_call | solution.py:390
  81.4 1.5 %backward.7 = (f32[512,256]{1,0:T(8,128)S(1)}, bf16[2048,256]{1,0:T(8,128)(2,1)}) custom-call(bf16[4096,2048]{1,0:T(8,128)(2,1)S(1)} %build_tile.1.tile_ref, f32[512,256]{1,0:T(8,128)S(1)} %get-tuple-element.69.refs_0_, bf16[2048,256]{1,0:T(8,128)(2,1)S(1)} %get-tuple-element.82.refs_1_), custom_call_target="tpu_custom_call" | custom-call | flops 268435456 | tf_op jit(solution)/shard_map/backward/pallas_call | solution.py:430
  82.9 0.8 %finish.1 = bf16[512,256]{1,0:T(8,128)(2,1)} custom-call(f32[512,256]{1,0:T(8,128)S(1)} %get-tuple-element.83.refs_0_, bf16[512,256]{1,0:T(8,128)(2,1)S(1)} %collective-permute-done.26.refs_1_, bf16[512,256]{1,0:T(8,128)(2,1)S(1)} %collective-permute-done.27.refs_2_, bf16[512,256]{1,0:T(8,128)(2,1)S(1)} %collective-permute-done.28.refs_3_), custom_call_target="tpu_custom_call" | custom-call | flops 1 | bytes 1 | tf_op jit(solution)/shard_map/finish/pallas_call | solution.py:453
  (56 shorter events, 2.4 us)
Async XLA Ops:
  0.6 30.3 %copy-start = (f32[16,256]{1,0:T(8,128)S(1)}, f32[16,256]{1,0:T(8,128)}, u32[]{:S(2)}) copy-start(f32[16,256]{1,0:T(8,128)} %param.15) | copy-start | bytes 49156
  0.6 10.6 %collective-permute-start = (bf16[512,256]{1,0:T(8,128)(2,1)}, bf16[512,256]{1,0:T(8,128)(2,1)S(1)}, u32[]{:S(2)}, u32[]{:S(2)}) collective-permute-start(bf16[512,256]{1,0:T(8,128)(2,1)} %refs_0_.3), channel_id=1, source_target_pairs={{0,8},{8,0},{16,24},{24,16},{1,9},{9,1},{17,25},{25,17},{2,10},{10... | collective-permute-start | bytes 786440 | tf_op jit(solution)/shard_map/ppermute | solution.py:465
  3.6 13.6 %collective-permute-start.1 = (bf16[512,256]{1,0:T(8,128)(2,1)}, bf16[512,256]{1,0:T(8,128)(2,1)S(1)}, u32[]{:S(2)}, u32[]{:S(2)}) collective-permute-start(bf16[512,256]{1,0:T(8,128)(2,1)} %refs_0_.3), channel_id=1, source_target_pairs={{0,16},{8,24},{16,0},{24,8},{1,17},{9,25},{17,1},{25,9},{2,18},{10... | collective-permute-start | bytes 786440 | tf_op jit(solution)/shard_map/ppermute | solution.py:465
  5.2 12.1 %collective-permute-start.2 = (bf16[512,256]{1,0:T(8,128)(2,1)}, bf16[512,256]{1,0:T(8,128)(2,1)S(1)}, u32[]{:S(2)}, u32[]{:S(2)}) collective-permute-start(bf16[512,256]{1,0:T(8,128)(2,1)} %refs_0_.3), channel_id=1, source_target_pairs={{0,24},{8,16},{16,8},{24,0},{1,25},{9,17},{17,9},{25,1},{2,26},{10... | collective-permute-start | bytes 786440 | tf_op jit(solution)/shard_map/ppermute | solution.py:465
  5.9 0.7 copy-start.4
  6.6 0.7 copy-start.5
  7.3 3.9 %copy-start.2 = (bf16[512,256]{1,0:T(8,128)(2,1)S(1)}, bf16[512,256]{1,0:T(8,128)(2,1)}, u32[]{:S(2)}) copy-start(bf16[512,256]{1,0:T(8,128)(2,1)} %refs_0_.3) | copy-start | bytes 786436
  18.5 3.2 %collective-permute-start.4 = (bf16[1024,256]{1,0:T(8,128)(2,1)S(1)}, bf16[1024,256]{1,0:T(8,128)(2,1)S(1)}, u32[]{:S(2)}, u32[]{:S(2)}) collective-permute-start(bf16[1024,256]{1,0:T(8,128)(2,1)S(1)} %get-tuple-element.48), channel_id=1, source_target_pairs={{0,1},{1,0},{2,3},{3,2},{4,5},{5,4},{6,7},{7,6},{8,9},{9,8},{10,11... | collective-permute-start | bytes 1572872 | tf_op jit(solution)/shard_map/ppermute | solution.py:465
  19.8 11.1 %copy-start.1 = (bf16[512,256]{1,0:T(8,128)(2,1)S(1)}, bf16[512,256]{1,0:T(8,128)(2,1)}, u32[]{:S(2)}) copy-start(bf16[512,256]{1,0:T(8,128)(2,1)} %cotangent_ref.3) | copy-start | bytes 786436
  19.9 11.1 %copy-start.6 = (s32[512]{0:T(512)S(1)}, s32[512]{0:T(512)}, u32[]{:S(2)}) copy-start(s32[512]{0:T(512)} %param.16) | copy-start | bytes 6148
  19.9 18.0 %copy-start.3 = (bf16[256,256]{1,0:T(8,128)(2,1)S(1)}, bf16[256,256]{1,0:T(8,128)(2,1)}, u32[]{:S(2)}) copy-start(bf16[256,256]{1,0:T(8,128)(2,1)} %weight_ref.3) | copy-start | bytes 393220
  21.2 2.3 %collective-permute-start.3 = (bf16[1024,256]{1,0:T(8,128)(2,1)S(1)}, bf16[1024,256]{1,0:T(8,128)(2,1)S(1)}, u32[]{:S(2)}, u32[]{:S(2)}) collective-permute-start(bf16[1024,256]{1,0:T(8,128)(2,1)S(1)} %get-tuple-element.46), channel_id=1, source_target_pairs={{0,1},{1,0},{2,3},{3,2},{4,5},{5,4},{6,7},{7,6},{8,9},{9,8},{10,11... | collective-permute-start | bytes 1572872 | tf_op jit(solution)/shard_map/ppermute | solution.py:465
  21.8 6.4 %collective-permute-start.6 = (bf16[256,256]{1,0:T(8,128)(2,1)S(1)}, bf16[256,256]{1,0:T(8,128)(2,1)S(1)}, u32[]{:S(2)}, u32[]{:S(2)}) collective-permute-start(bf16[256,256]{1,0:T(8,128)(2,1)S(1)} %get-tuple-element.49), channel_id=1, source_target_pairs={{0,2},{1,3},{2,0},{3,1},{4,6},{5,7},{6,4},{7,5},{8,10},{9,11},{10,... | collective-permute-start | bytes 393224 | tf_op jit(solution)/shard_map/ppermute | solution.py:465
  23.5 9.5 %collective-permute-start.5 = (bf16[256,256]{1,0:T(8,128)(2,1)S(1)}, bf16[256,256]{1,0:T(8,128)(2,1)S(1)}, u32[]{:S(2)}, u32[]{:S(2)}) collective-permute-start(bf16[256,256]{1,0:T(8,128)(2,1)S(1)} %get-tuple-element.51), channel_id=1, source_target_pairs={{0,2},{1,3},{2,0},{3,1},{4,6},{5,7},{6,4},{7,5},{8,10},{9,11},{10,... | collective-permute-start | bytes 393224 | tf_op jit(solution)/shard_map/ppermute | solution.py:465
  25.0 12.9 %collective-permute-start.7 = (bf16[256,256]{1,0:T(8,128)(2,1)S(1)}, bf16[256,256]{1,0:T(8,128)(2,1)S(1)}, u32[]{:S(2)}, u32[]{:S(2)}) collective-permute-start(bf16[256,256]{1,0:T(8,128)(2,1)S(1)} %get-tuple-element.55), channel_id=1, source_target_pairs={{0,2},{1,3},{2,0},{3,1},{4,6},{5,7},{6,4},{7,5},{8,10},{9,11},{10,... | collective-permute-start | bytes 393224 | tf_op jit(solution)/shard_map/ppermute | solution.py:465
  28.3 9.6 %collective-permute-start.8 = (bf16[256,256]{1,0:T(8,128)(2,1)S(1)}, bf16[256,256]{1,0:T(8,128)(2,1)S(1)}, u32[]{:S(2)}, u32[]{:S(2)}) collective-permute-start(bf16[256,256]{1,0:T(8,128)(2,1)S(1)} %combine.6), channel_id=1, source_target_pairs={{0,4},{1,5},{2,6},{3,7},{4,0},{5,1},{6,2},{7,3},{8,12},{9,13},{10,... | collective-permute-start | bytes 393224 | tf_op jit(solution)/shard_map/ppermute | solution.py:465
  31.4 11.6 %collective-permute-start.9 = (bf16[256,256]{1,0:T(8,128)(2,1)S(1)}, bf16[256,256]{1,0:T(8,128)(2,1)S(1)}, u32[]{:S(2)}, u32[]{:S(2)}) collective-permute-start(bf16[256,256]{1,0:T(8,128)(2,1)S(1)} %get-tuple-element.61), channel_id=1, source_target_pairs={{0,2},{1,3},{2,0},{3,1},{4,6},{5,7},{6,4},{7,5},{8,10},{9,11},{10,... | collective-permute-start | bytes 393224 | tf_op jit(solution)/shard_map/ppermute | solution.py:465
  33.1 9.9 %collective-permute-start.10 = (bf16[256,256]{1,0:T(8,128)(2,1)S(1)}, bf16[256,256]{1,0:T(8,128)(2,1)S(1)}, u32[]{:S(2)}, u32[]{:S(2)}) collective-permute-start(bf16[256,256]{1,0:T(8,128)(2,1)S(1)} %combine.7), channel_id=1, source_target_pairs={{0,4},{1,5},{2,6},{3,7},{4,0},{5,1},{6,2},{7,3},{8,12},{9,13},{10,... | collective-permute-start | bytes 393224 | tf_op jit(solution)/shard_map/ppermute | solution.py:465
  38.3 11.1 %collective-permute-start.17 = (bf16[256,256]{1,0:T(8,128)(2,1)S(1)}, bf16[256,256]{1,0:T(8,128)(2,1)S(1)}, u32[]{:S(2)}, u32[]{:S(2)}) collective-permute-start(bf16[256,256]{1,0:T(8,128)(2,1)S(1)} %get-tuple-element.59.refs_0_), channel_id=1, source_target_pairs={{0,2},{1,3},{2,0},{3,1},{4,6},{5,7},{6,4},{7,5},{8,10},{9,11},{10,... | collective-permute-start | bytes 393224 | tf_op jit(solution)/shard_map/ppermute | solution.py:465
  39.7 9.6 %collective-permute-start.16 = (bf16[256,256]{1,0:T(8,128)(2,1)S(1)}, bf16[256,256]{1,0:T(8,128)(2,1)S(1)}, u32[]{:S(2)}, u32[]{:S(2)}) collective-permute-start(bf16[256,256]{1,0:T(8,128)(2,1)S(1)} %get-tuple-element.59.refs_0_), channel_id=1, source_target_pairs={{0,4},{1,5},{2,6},{3,7},{4,0},{5,1},{6,2},{7,3},{8,12},{9,13},{10,... | collective-permute-start | bytes 393224 | tf_op jit(solution)/shard_map/ppermute | solution.py:465
  43.5 9.1 %collective-permute-start.22 = (bf16[256,256]{1,0:T(8,128)(2,1)S(1)}, bf16[256,256]{1,0:T(8,128)(2,1)S(1)}, u32[]{:S(2)}, u32[]{:S(2)}) collective-permute-start(bf16[256,256]{1,0:T(8,128)(2,1)S(1)} %get-tuple-element.73.refs_1_), channel_id=1, source_target_pairs={{0,2},{1,3},{2,0},{3,1},{4,6},{5,7},{6,4},{7,5},{8,10},{9,11},{10,... | collective-permute-start | bytes 393224 | tf_op jit(solution)/shard_map/ppermute | solution.py:465
  45.4 7.2 %collective-permute-start.21 = (bf16[256,256]{1,0:T(8,128)(2,1)S(1)}, bf16[256,256]{1,0:T(8,128)(2,1)S(1)}, u32[]{:S(2)}, u32[]{:S(2)}) collective-permute-start(bf16[256,256]{1,0:T(8,128)(2,1)S(1)} %get-tuple-element.73.refs_1_), channel_id=1, source_target_pairs={{0,4},{1,5},{2,6},{3,7},{4,0},{5,1},{6,2},{7,3},{8,12},{9,13},{10,... | collective-permute-start | bytes 393224 | tf_op jit(solution)/shard_map/ppermute | solution.py:465
  49.3 1.3 %collective-permute-start.11 = (bf16[160,256]{1,0:T(8,128)(2,1)S(1)}, bf16[160,256]{1,0:T(8,128)(2,1)S(1)}, u32[]{:S(2)}, u32[]{:S(2)}) collective-permute-start(bf16[160,256]{1,0:T(8,128)(2,1)S(1)} %get-tuple-element.66), channel_id=1, source_target_pairs={{0,1},{1,0},{2,3},{3,2},{4,5},{5,4},{6,7},{7,6},{8,9},{9,8},{10,11... | collective-permute-start | bytes 245768 | tf_op jit(solution)/shard_map/ppermute | solution.py:465
  49.4 14.9 %collective-permute-start.18 = (bf16[768,256]{1,0:T(8,128)(2,1)S(1)}, bf16[768,256]{1,0:T(8,128)(2,1)S(1)}, u32[]{:S(2)}, u32[]{:S(2)}) collective-permute-start(bf16[768,256]{1,0:T(8,128)(2,1)S(1)} %pad_maximum_fusion), channel_id=1, source_target_pairs={{0,1},{1,0},{2,3},{3,2},{4,5},{5,4},{6,7},{7,6},{8,9},{9,8},{10,11... | collective-permute-start | bytes 1179656 | tf_op jit(solution)/shard_map/ppermute | solution.py:465
  50.6 4.6 %collective-permute-start.12 = (bf16[160,256]{1,0:T(8,128)(2,1)S(1)}, bf16[160,256]{1,0:T(8,128)(2,1)S(1)}, u32[]{:S(2)}, u32[]{:S(2)}) collective-permute-start(bf16[160,256]{1,0:T(8,128)(2,1)S(1)} %add_messages.5.own_ref), channel_id=1, source_target_pairs={{0,8},{8,0},{16,24},{24,16},{1,9},{9,1},{17,25},{25,17},{2,10},{10... | collective-permute-start | bytes 245768 | tf_op jit(solution)/shard_map/ppermute | solution.py:465
  51.8 5.3 %collective-permute-start.19 = (bf16[256,256]{1,0:T(8,128)(2,1)S(1)}, bf16[256,256]{1,0:T(8,128)(2,1)S(1)}, u32[]{:S(2)}, u32[]{:S(2)}) collective-permute-start(bf16[256,256]{1,0:T(8,128)(2,1)S(1)} %collective-permute-done.16.refs_2_), channel_id=1, source_target_pairs={{0,2},{1,3},{2,0},{3,1},{4,6},{5,7},{6,4},{7,5},{8,10},{9,11},{10,... | collective-permute-start | bytes 393224 | tf_op jit(solution)/shard_map/ppermute | solution.py:465
  52.6 14.3 %collective-permute-start.23 = (bf16[768,256]{1,0:T(8,128)(2,1)S(1)}, bf16[768,256]{1,0:T(8,128)(2,1)S(1)}, u32[]{:S(2)}, u32[]{:S(2)}) collective-permute-start(bf16[768,256]{1,0:T(8,128)(2,1)S(1)} %pad_maximum_fusion.1), channel_id=1, source_target_pairs={{0,1},{1,0},{2,3},{3,2},{4,5},{5,4},{6,7},{7,6},{8,9},{9,8},{10,11... | collective-permute-start | bytes 1179656 | tf_op jit(solution)/shard_map/ppermute | solution.py:465
  55.2 4.5 %collective-permute-start.13 = (bf16[160,256]{1,0:T(8,128)(2,1)S(1)}, bf16[160,256]{1,0:T(8,128)(2,1)S(1)}, u32[]{:S(2)}, u32[]{:S(2)}) collective-permute-start(bf16[160,256]{1,0:T(8,128)(2,1)S(1)} %add_messages.6.own_ref), channel_id=1, source_target_pairs={{0,16},{8,24},{16,0},{24,8},{1,17},{9,25},{17,1},{25,9},{2,18},{10... | collective-permute-start | bytes 245768 | tf_op jit(solution)/shard_map/ppermute | solution.py:465
  56.8 5.8 %collective-permute-start.24 = (bf16[256,256]{1,0:T(8,128)(2,1)S(1)}, bf16[256,256]{1,0:T(8,128)(2,1)S(1)}, u32[]{:S(2)}, u32[]{:S(2)}) collective-permute-start(bf16[256,256]{1,0:T(8,128)(2,1)S(1)} %collective-permute-done.21.refs_3_), channel_id=1, source_target_pairs={{0,2},{1,3},{2,0},{3,1},{4,6},{5,7},{6,4},{7,5},{8,10},{9,11},{10,... | collective-permute-start | bytes 393224 | tf_op jit(solution)/shard_map/ppermute | solution.py:465
  57.1 7.2 %collective-permute-start.20 = (bf16[256,256]{1,0:T(8,128)(2,1)S(1)}, bf16[256,256]{1,0:T(8,128)(2,1)S(1)}, u32[]{:S(2)}, u32[]{:S(2)}) collective-permute-start(bf16[256,256]{1,0:T(8,128)(2,1)S(1)} %collective-permute-done.19.refs_6_), channel_id=1, source_target_pairs={{0,1},{1,0},{2,3},{3,2},{4,5},{5,4},{6,7},{7,6},{8,9},{9,8},{10,11... | collective-permute-start | bytes 393224 | tf_op jit(solution)/shard_map/ppermute | solution.py:465
  59.8 4.5 %collective-permute-start.14 = (bf16[160,256]{1,0:T(8,128)(2,1)S(1)}, bf16[160,256]{1,0:T(8,128)(2,1)S(1)}, u32[]{:S(2)}, u32[]{:S(2)}) collective-permute-start(bf16[160,256]{1,0:T(8,128)(2,1)S(1)} %add_messages.7.own_ref), channel_id=1, source_target_pairs={{0,2},{1,3},{2,0},{3,1},{4,6},{5,7},{6,4},{7,5},{8,10},{9,11},{10,... | collective-permute-start | bytes 245768 | tf_op jit(solution)/shard_map/ppermute | solution.py:465
  62.7 4.2 %collective-permute-start.25 = (bf16[256,256]{1,0:T(8,128)(2,1)S(1)}, bf16[256,256]{1,0:T(8,128)(2,1)S(1)}, u32[]{:S(2)}, u32[]{:S(2)}) collective-permute-start(bf16[256,256]{1,0:T(8,128)(2,1)S(1)} %collective-permute-done.24.refs_7_), channel_id=1, source_target_pairs={{0,1},{1,0},{2,3},{3,2},{4,5},{5,4},{6,7},{7,6},{8,9},{9,8},{10,11... | collective-permute-start | bytes 393224 | tf_op jit(solution)/shard_map/ppermute | solution.py:465
  69.1 13.8 %collective-permute-start.26 = (bf16[512,256]{1,0:T(8,128)(2,1)S(1)}, bf16[512,256]{1,0:T(8,128)(2,1)S(1)}, u32[]{:S(2)}, u32[]{:S(2)}) collective-permute-start(bf16[512,256]{1,0:T(8,128)(2,1)S(1)} %get-tuple-element.80), channel_id=1, source_target_pairs={{0,8},{8,0},{16,24},{24,16},{1,9},{9,1},{17,25},{25,17},{2,10},{10... | collective-permute-start | bytes 786440 | tf_op jit(solution)/shard_map/ppermute | solution.py:465
  70.3 12.6 %collective-permute-start.27 = (bf16[512,256]{1,0:T(8,128)(2,1)S(1)}, bf16[512,256]{1,0:T(8,128)(2,1)S(1)}, u32[]{:S(2)}, u32[]{:S(2)}) collective-permute-start(bf16[512,256]{1,0:T(8,128)(2,1)S(1)} %get-tuple-element.81), channel_id=1, source_target_pairs={{0,16},{8,24},{16,0},{24,8},{1,17},{9,25},{17,1},{25,9},{2,18},{10... | collective-permute-start | bytes 786440 | tf_op jit(solution)/shard_map/ppermute | solution.py:465
  71.2 11.7 %collective-permute-start.28 = (bf16[512,256]{1,0:T(8,128)(2,1)S(1)}, bf16[512,256]{1,0:T(8,128)(2,1)S(1)}, u32[]{:S(2)}, u32[]{:S(2)}) collective-permute-start(bf16[512,256]{1,0:T(8,128)(2,1)S(1)} %get-tuple-element.77), channel_id=1, source_target_pairs={{0,24},{8,16},{16,8},{24,0},{1,25},{9,17},{17,9},{25,1},{2,26},{10... | collective-permute-start | bytes 786440 | tf_op jit(solution)/shard_map/ppermute | solution.py:465
  72.7 6.1 %collective-permute-start.15 = (bf16[160,256]{1,0:T(8,128)(2,1)S(1)}, bf16[160,256]{1,0:T(8,128)(2,1)S(1)}, u32[]{:S(2)}, u32[]{:S(2)}) collective-permute-start(bf16[160,256]{1,0:T(8,128)(2,1)S(1)} %add_messages.8.own_ref), channel_id=1, source_target_pairs={{0,4},{1,5},{2,6},{3,7},{4,0},{5,1},{6,2},{7,3},{8,12},{9,13},{10,... | collective-permute-start | bytes 245768 | tf_op jit(solution)/shard_map/ppermute | solution.py:465
  78.8 1.3 %collective-permute-start.29 = (bf16[160,256]{1,0:T(8,128)(2,1)S(1)}, bf16[160,256]{1,0:T(8,128)(2,1)S(1)}, u32[]{:S(2)}, u32[]{:S(2)}) collective-permute-start(bf16[160,256]{1,0:T(8,128)(2,1)S(1)} %add_messages.9.own_ref), channel_id=1, source_target_pairs={{0,1},{1,0},{2,3},{3,2},{4,5},{5,4},{6,7},{7,6},{8,9},{9,8},{10,11... | collective-permute-start | bytes 245768 | tf_op jit(solution)/shard_map/ppermute | solution.py:465

commit v5 on v4

--- a/solution.py
+++ b/solution.py
@@ -426,7 +426,8 @@
     width = blocks[0].shape[1]
     depth = tile.shape[0] // CHUNKS
     vmem = pl.BlockSpec(memory_space=pltpu.VMEM)
-    flops = (1 if chunk else 2) * depth * len(targets) * share * width
+    scale = 2 if chunk == 0 else 8 if len(targets) > 1 else 1
+    flops = scale * depth * len(targets) * share * width
     return pl.pallas_call(
         functools.partial(backward_kernel, chunk, targets, places),
         out_shape=[pltpu.VMEM((share, width), kind) for kind in kinds]
@@ -558,7 +559,7 @@
         for group in (ready, [late]):
             sent = jnp.concatenate([held[n][k] for k in group], axis=0)
             if n and group is not ready:
-                sent = after(sent, messages[2])
+                sent = after(sent, messages[1])
             arrived = swap(sent, "col", bit, col_count)
             for t, k in enumerate(group):
                 blocks += [held[n][k], arrived]

time: 83.9 us -> 83.9 us (level)
  waiting for transfers between devices: 27 us -> 25.8 us
  Pallas kernels: 20.5 us -> 21.6 us
    ppermute x30, waiting for transfers between devices: 27 us -> 25.8 us  [swap(): return lax.ppermute(values, axis, [(d, d ^ mask) for d in range(count)])]
    pallas_call x1, Pallas kernels: 3.91 us -> 5.05 us  [build_tile(): pl.pallas_call(functools.partial(build_kernel, layout), out_shape=pltpu.V...]
  transfers between devices with their start and end apart: 30 -> 30, of which waited for: 11 -> 12; matrix products, arithmetic and copies ran while one was open for 1% -> 1% of each run, Pallas kernels for 19% -> 21%
where the time goes in v5:
time: 83.9 us; the launch traced here: 83.7 us
  starting transfers between devices  32.8 us (39%)
  waiting for transfers between devices  25.8 us (31%)
  Pallas kernels  21.6 us (26%)
  between operations  1.55 us (2%)
  local copies, waits for them, and re-layouts  1.39 us (2%)
    ppermute x30, starting transfers between devices, swap(): return lax.ppermute(values, axis, [(d, d ^ mask) for d in range(count)])  32.8 us
    ppermute x30, waiting for transfers between devices, swap(): return lax.ppermute(values, axis, [(d, d ^ mask) for d in range(count)])  25.8 us
    pallas_call x4, Pallas kernels, backward(): pl.pallas_call(functools.partial(backward_kernel, chunk, targets, places)...  6.22 us
    pallas_call x1, Pallas kernels, build_tile(): pl.pallas_call(functools.partial(build_kernel, layout), out_shape=pltpu.V...  5.05 us
    pallas_call x4, Pallas kernels, forward(): pl.pallas_call(functools.partial(forward_kernel, chunk, first), out_shape...  5.03 us
  transfers between devices with their start and end apart: 30, of which 12 were waited for; matrix products, arithmetic and copies ran while one was open for 1% of the time, Pallas kernels for 21%

profile of v5, /device:TPU:0, one launch (start us, length us, event | category | flops | bytes accessed | tf_op | source)
XLA Modules:
  0.0 83.7 jit_solution(10139982064818293487)
XLA Ops:
  0.6 3.0 %collective-permute-start = (bf16[512,256]{1,0:T(8,128)(2,1)}, bf16[512,256]{1,0:T(8,128)(2,1)S(1)}, u32[]{:S(2)}, u32[]{:S(2)}) collective-permute-start(bf16[512,256]{1,0:T(8,128)(2,1)} %refs_0_.3), channel_id=1, source_target_pairs={{0,8},{8,0},{16,24},{24,16},{1,9},{9,1},{17,25},{25,17},{2,10},{10... | collective-permute-start | bytes 786440 | tf_op jit(solution)/shard_map/ppermute | solution.py:466
  3.6 1.5 %collective-permute-start.1 = (bf16[512,256]{1,0:T(8,128)(2,1)}, bf16[512,256]{1,0:T(8,128)(2,1)S(1)}, u32[]{:S(2)}, u32[]{:S(2)}) collective-permute-start(bf16[512,256]{1,0:T(8,128)(2,1)} %refs_0_.3), channel_id=1, source_target_pairs={{0,16},{8,24},{16,0},{24,8},{1,17},{9,25},{17,1},{25,9},{2,18},{10... | collective-permute-start | bytes 786440 | tf_op jit(solution)/shard_map/ppermute | solution.py:466
  5.9 0.7 copy-done.4
  6.6 0.7 copy-done.5
  7.3 5.1 %build_tile.1.tile_ref = bf16[4096,2048]{1,0:T(8,128)(2,1)S(1)} custom-call(s32[2]{0:T(128)S(1)} %pad_add_fusion.at_ref, s32[1,1]{1,0:T(1,128)S(6)} %copy.13.live_ref, s32[1,1,384]{2,1,0:T(1,128)S(1)} %copy-done.4, s32[1,1,384]{2,1,0:T(1,128)S(1)} %copy-done.5, bf16[1,1,384,128,128]{4,3,2,1,0:T(8,128)(2,1)} %slots_ref.1), custom_call_target="tpu_custom_call" | custom-call | bytes 20971520 | tf_op jit(solution)/shard_map/build_tile/pallas_call | solution.py:119
  12.4 1.2 %forward.6.refs_0_ = f32[2048,256]{1,0:T(8,128)S(1)} custom-call(bf16[4096,2048]{1,0:T(8,128)(2,1)S(1)} %build_tile.1.tile_ref, bf16[512,256]{1,0:T(8,128)(2,1)S(1)} %copy-done.2, bf16[512,256]{1,0:T(8,128)(2,1)S(1)} %collective-permute-done.refs_1_), custom_call_target="tpu_custom_call" | custom-call | flops 1073741824 | tf_op jit(solution)/shard_map/forward/pallas_call | solution.py:166
  13.6 3.6 %collective-permute-done.1.refs_1_ = bf16[512,256]{1,0:T(8,128)(2,1)S(1)} collective-permute-done((bf16[512,256]{1,0:T(8,128)(2,1)}, bf16[512,256]{1,0:T(8,128)(2,1)S(1)}, u32[]{:S(2)}, u32[]{:S(2)}) %collective-permute-start.1) | collective-permute-done | bytes 262176 | tf_op jit(solution)/shard_map/ppermute | solution.py:466
  17.2 1.3 %forward.7 = (bf16[1024,256]{1,0:T(8,128)(2,1)S(1)}, bf16[1024,256]{1,0:T(8,128)(2,1)S(1)}) custom-call(bf16[4096,2048]{1,0:T(8,128)(2,1)S(1)} %build_tile.1.tile_ref, f32[2048,256]{1,0:T(8,128)S(1)} %forward.6.refs_0_, bf16[512,256]{1,0:T(8,128)(2,1)S(1)} %collective-permute-done.1.refs_1_, bf16[512,256]{1,0:T(8,128)(2,1)S(1)} %collective-permute-done.2.refs_2_), custom_call_target="tpu_custom_call" | custom-call | flops 1073741824 | tf_op jit(solution)/shard_map/forward/pallas_call | solution.py:166
  18.6 1.2 %forward.4.refs_0_ = f32[2048,256]{1,0:T(8,128)S(1)} custom-call(bf16[4096,2048]{1,0:T(8,128)(2,1)S(1)} %build_tile.1.tile_ref, bf16[512,256]{1,0:T(8,128)(2,1)S(1)} %copy-done.2, bf16[512,256]{1,0:T(8,128)(2,1)S(1)} %collective-permute-done.refs_1_), custom_call_target="tpu_custom_call" | custom-call | flops 1073741824 | tf_op jit(solution)/shard_map/forward/pallas_call | solution.py:166
  19.9 1.3 %forward.5 = (bf16[1024,256]{1,0:T(8,128)(2,1)S(1)}, bf16[1024,256]{1,0:T(8,128)(2,1)S(1)}) custom-call(bf16[4096,2048]{1,0:T(8,128)(2,1)S(1)} %build_tile.1.tile_ref, f32[2048,256]{1,0:T(8,128)S(1)} %forward.4.refs_0_, bf16[512,256]{1,0:T(8,128)(2,1)S(1)} %collective-permute-done.1.refs_1_, bf16[512,256]{1,0:T(8,128)(2,1)S(1)} %collective-permute-done.2.refs_2_), custom_call_target="tpu_custom_call" | custom-call | flops 1073741824 | tf_op jit(solution)/shard_map/forward/pallas_call | solution.py:166
  21.2 0.6 collective-permute-start.3
  21.8 1.6 %collective-permute-start.6 = (bf16[256,256]{1,0:T(8,128)(2,1)S(1)}, bf16[256,256]{1,0:T(8,128)(2,1)S(1)}, u32[]{:S(2)}, u32[]{:S(2)}) collective-permute-start(bf16[256,256]{1,0:T(8,128)(2,1)S(1)} %get-tuple-element.49), channel_id=1, source_target_pairs={{0,2},{1,3},{2,0},{3,1},{4,6},{5,7},{6,4},{7,5},{8,10},{9,11},{10,... | collective-permute-start | bytes 393224 | tf_op jit(solution)/shard_map/ppermute | solution.py:466
  23.5 1.5 %collective-permute-start.5 = (bf16[256,256]{1,0:T(8,128)(2,1)S(1)}, bf16[256,256]{1,0:T(8,128)(2,1)S(1)}, u32[]{:S(2)}, u32[]{:S(2)}) collective-permute-start(bf16[256,256]{1,0:T(8,128)(2,1)S(1)} %get-tuple-element.51), channel_id=1, source_target_pairs={{0,2},{1,3},{2,0},{3,1},{4,6},{5,7},{6,4},{7,5},{8,10},{9,11},{10,... | collective-permute-start | bytes 393224 | tf_op jit(solution)/shard_map/ppermute | solution.py:466
  25.0 0.6 collective-permute-start.7
  25.6 2.6 %collective-permute-done.6.refs_2_ = bf16[256,256]{1,0:T(8,128)(2,1)S(1)} collective-permute-done((bf16[256,256]{1,0:T(8,128)(2,1)S(1)}, bf16[256,256]{1,0:T(8,128)(2,1)S(1)}, u32[]{:S(2)}, u32[]{:S(2)}) %collective-permute-start.6) | collective-permute-done | bytes 131104 | tf_op jit(solution)/shard_map/ppermute | solution.py:466
  28.3 2.6 %collective-permute-start.8 = (bf16[256,256]{1,0:T(8,128)(2,1)S(1)}, bf16[256,256]{1,0:T(8,128)(2,1)S(1)}, u32[]{:S(2)}, u32[]{:S(2)}) collective-permute-start(bf16[256,256]{1,0:T(8,128)(2,1)S(1)} %combine.6), channel_id=1, source_target_pairs={{0,4},{1,5},{2,6},{3,7},{4,0},{5,1},{6,2},{7,3},{8,12},{9,13},{10,... | collective-permute-start | bytes 393224 | tf_op jit(solution)/shard_map/ppermute | solution.py:466
  30.9 0.4 convert_multiply_fusion
  31.4 1.6 %collective-permute-start.9 = (bf16[256,256]{1,0:T(8,128)(2,1)S(1)}, bf16[256,256]{1,0:T(8,128)(2,1)S(1)}, u32[]{:S(2)}, u32[]{:S(2)}) collective-permute-start(bf16[256,256]{1,0:T(8,128)(2,1)S(1)} %get-tuple-element.61), channel_id=1, source_target_pairs={{0,2},{1,3},{2,0},{3,1},{4,6},{5,7},{6,4},{7,5},{8,10},{9,11},{10,... | collective-permute-start | bytes 393224 | tf_op jit(solution)/shard_map/ppermute | solution.py:466
  33.1 1.2 %collective-permute-start.10 = (bf16[256,256]{1,0:T(8,128)(2,1)S(1)}, bf16[256,256]{1,0:T(8,128)(2,1)S(1)}, u32[]{:S(2)}, u32[]{:S(2)}) collective-permute-start(bf16[256,256]{1,0:T(8,128)(2,1)S(1)} %combine.7), channel_id=1, source_target_pairs={{0,4},{1,5},{2,6},{3,7},{4,0},{5,1},{6,2},{7,3},{8,12},{9,13},{10,... | collective-permute-start | bytes 393224 | tf_op jit(solution)/shard_map/ppermute | solution.py:466
  34.2 3.6 %collective-permute-done.7.refs_2_ = bf16[256,256]{1,0:T(8,128)(2,1)S(1)} collective-permute-done((bf16[256,256]{1,0:T(8,128)(2,1)S(1)}, bf16[256,256]{1,0:T(8,128)(2,1)S(1)}, u32[]{:S(2)}, u32[]{:S(2)}) %collective-permute-start.7) | collective-permute-done | bytes 131104 | tf_op jit(solution)/shard_map/ppermute | solution.py:466
  38.3 1.5 %collective-permute-start.17 = (bf16[256,256]{1,0:T(8,128)(2,1)S(1)}, bf16[256,256]{1,0:T(8,128)(2,1)S(1)}, u32[]{:S(2)}, u32[]{:S(2)}) collective-permute-start(bf16[256,256]{1,0:T(8,128)(2,1)S(1)} %get-tuple-element.59.refs_0_), channel_id=1, source_target_pairs={{0,2},{1,3},{2,0},{3,1},{4,6},{5,7},{6,4},{7,5},{8,10},{9,11},{10,... | collective-permute-start | bytes 393224 | tf_op jit(solution)/shard_map/ppermute | solution.py:466
  39.7 3.3 %collective-permute-start.16 = (bf16[256,256]{1,0:T(8,128)(2,1)S(1)}, bf16[256,256]{1,0:T(8,128)(2,1)S(1)}, u32[]{:S(2)}, u32[]{:S(2)}) collective-permute-start(bf16[256,256]{1,0:T(8,128)(2,1)S(1)} %get-tuple-element.59.refs_0_), channel_id=1, source_target_pairs={{0,4},{1,5},{2,6},{3,7},{4,0},{5,1},{6,2},{7,3},{8,12},{9,13},{10,... | collective-permute-start | bytes 393224 | tf_op jit(solution)/shard_map/ppermute | solution.py:466
  43.5 1.9 %collective-permute-start.22 = (bf16[256,256]{1,0:T(8,128)(2,1)S(1)}, bf16[256,256]{1,0:T(8,128)(2,1)S(1)}, u32[]{:S(2)}, u32[]{:S(2)}) collective-permute-start(bf16[256,256]{1,0:T(8,128)(2,1)S(1)} %get-tuple-element.73.refs_1_), channel_id=1, source_target_pairs={{0,2},{1,3},{2,0},{3,1},{4,6},{5,7},{6,4},{7,5},{8,10},{9,11},{10,... | collective-permute-start | bytes 393224 | tf_op jit(solution)/shard_map/ppermute | solution.py:466
  45.4 2.7 %collective-permute-start.21 = (bf16[256,256]{1,0:T(8,128)(2,1)S(1)}, bf16[256,256]{1,0:T(8,128)(2,1)S(1)}, u32[]{:S(2)}, u32[]{:S(2)}) collective-permute-start(bf16[256,256]{1,0:T(8,128)(2,1)S(1)} %get-tuple-element.73.refs_1_), channel_id=1, source_target_pairs={{0,4},{1,5},{2,6},{3,7},{4,0},{5,1},{6,2},{7,3},{8,12},{9,13},{10,... | collective-permute-start | bytes 393224 | tf_op jit(solution)/shard_map/ppermute | solution.py:466
  48.3 0.9 %local_last.1 = (bf16[160,256]{1,0:T(8,128)(2,1)S(1)}, bf16[160,256]{1,0:T(8,128)(2,1)S(1)}) custom-call(s32[2]{0:T(128)S(1)} %pad_add_fusion.at_ref, f32[16,512]{1,0:T(8,128)S(1)} %fusion.members_ref, bf16[512,256]{1,0:T(8,128)(2,1)S(1)} %copy-done.1, f32[288,256]{1,0:T(8,128)S(1)} %local_first.1.before_ref, ...), custom_call_target="tpu_custom_call" | custom-call | flops 1 | bytes 1 | tf_op jit(solution)/shard_map/local_last/pallas_call | solution.py:323
  49.4 0.5 collective-permute-start.18
  50.0 0.7 collective-permute-done.11.other_ref
  50.6 1.3 %collective-permute-start.12 = (bf16[160,256]{1,0:T(8,128)(2,1)S(1)}, bf16[160,256]{1,0:T(8,128)(2,1)S(1)}, u32[]{:S(2)}, u32[]{:S(2)}) collective-permute-start(bf16[160,256]{1,0:T(8,128)(2,1)S(1)} %add_messages.5.own_ref), channel_id=1, source_target_pairs={{0,8},{8,0},{16,24},{24,16},{1,9},{9,1},{17,25},{25,17},{2,10},{10... | collective-permute-start | bytes 245768 | tf_op jit(solution)/shard_map/ppermute | solution.py:466
  52.0 0.5 collective-permute-done.22.refs_5_
  52.7 2.5 %collective-permute-done.12.other_ref = bf16[160,256]{1,0:T(8,128)(2,1)S(1)} collective-permute-done((bf16[160,256]{1,0:T(8,128)(2,1)S(1)}, bf16[160,256]{1,0:T(8,128)(2,1)S(1)}, u32[]{:S(2)}, u32[]{:S(2)}) %collective-permute-start.12) | collective-permute-done | bytes 81952 | tf_op jit(solution)/shard_map/ppermute | solution.py:466
  55.2 1.6 %collective-permute-start.13 = (bf16[160,256]{1,0:T(8,128)(2,1)S(1)}, bf16[160,256]{1,0:T(8,128)(2,1)S(1)}, u32[]{:S(2)}, u32[]{:S(2)}) collective-permute-start(bf16[160,256]{1,0:T(8,128)(2,1)S(1)} %add_messages.6.own_ref), channel_id=1, source_target_pairs={{0,16},{8,24},{16,0},{24,8},{1,17},{9,25},{17,1},{25,9},{2,18},{10... | collective-permute-start | bytes 245768 | tf_op jit(solution)/shard_map/ppermute | solution.py:466
  57.2 2.5 %collective-permute-done.13.other_ref = bf16[160,256]{1,0:T(8,128)(2,1)S(1)} collective-permute-done((bf16[160,256]{1,0:T(8,128)(2,1)S(1)}, bf16[160,256]{1,0:T(8,128)(2,1)S(1)}, u32[]{:S(2)}, u32[]{:S(2)}) %collective-permute-start.13) | collective-permute-done | bytes 81952 | tf_op jit(solution)/shard_map/ppermute | solution.py:466
  59.8 0.5 collective-permute-start.14
  60.3 2.4 %collective-permute-done.24.refs_7_ = bf16[256,256]{1,0:T(8,128)(2,1)S(1)} collective-permute-done((bf16[256,256]{1,0:T(8,128)(2,1)S(1)}, bf16[256,256]{1,0:T(8,128)(2,1)S(1)}, u32[]{:S(2)}, u32[]{:S(2)}) %collective-permute-start.24) | collective-permute-done | bytes 131104 | tf_op jit(solution)/shard_map/ppermute | solution.py:466
  62.7 1.6 %collective-permute-done.14.other_ref = bf16[160,256]{1,0:T(8,128)(2,1)S(1)} collective-permute-done((bf16[160,256]{1,0:T(8,128)(2,1)S(1)}, bf16[160,256]{1,0:T(8,128)(2,1)S(1)}, u32[]{:S(2)}, u32[]{:S(2)}) %collective-permute-start.14) | collective-permute-done | bytes 81952 | tf_op jit(solution)/shard_map/ppermute | solution.py:466
  64.3 2.6 %backward.4 = (f32[512,256]{1,0:T(8,128)S(1)}, f32[512,256]{1,0:T(8,128)S(1)}, f32[512,256]{1,0:T(8,128)S(1)}, f32[512,256]{1,0:T(8,128)S(1)}, bf16[2048,256]{1,0:T(8,128)(2,1)}) custom-call(bf16[4096,2048]{1,0:T(8,128)(2,1)S(1)} %build_tile.1.tile_ref, bf16[256,256]{1,0:T(8,128)(2,1)S(1)} %get-tuple-element.59.refs_0_, ...), custom_call_target="tpu_custom_call" | custom-call | flops 2147483648 | tf_op jit(solution)/shard_map/backward/pallas_call | solution.py:431
  66.9 0.8 backward.5
  67.7 1.4 %backward.6 = (bf16[512,256]{1,0:T(8,128)(2,1)S(1)}, bf16[512,256]{1,0:T(8,128)(2,1)S(1)}, bf16[2048,256]{1,0:T(8,128)(2,1)S(1)}) custom-call(bf16[4096,2048]{1,0:T(8,128)(2,1)S(1)} %build_tile.1.tile_ref, f32[512,256]{1,0:T(8,128)S(1)} %get-tuple-element.70.refs_0_, f32[512,256]{1,0:T(8,128)S(1)} %get-tuple-element.71.refs_1_, ...), custom_call_target="tpu_custom_call" | custom-call | flops 4294967296 | tf_op jit(solution)/shard_map/backward/pallas_call | solution.py:431
  69.1 1.3 %collective-permute-start.26 = (bf16[512,256]{1,0:T(8,128)(2,1)S(1)}, bf16[512,256]{1,0:T(8,128)(2,1)S(1)}, u32[]{:S(2)}, u32[]{:S(2)}) collective-permute-start(bf16[512,256]{1,0:T(8,128)(2,1)S(1)} %get-tuple-element.80), channel_id=1, source_target_pairs={{0,8},{8,0},{16,24},{24,16},{1,9},{9,1},{17,25},{25,17},{2,10},{10... | collective-permute-start | bytes 786440 | tf_op jit(solution)/shard_map/ppermute | solution.py:466
  70.4 0.8 collective-permute-start.27
  71.2 1.4 %collective-permute-start.28 = (bf16[512,256]{1,0:T(8,128)(2,1)S(1)}, bf16[512,256]{1,0:T(8,128)(2,1)S(1)}, u32[]{:S(2)}, u32[]{:S(2)}) collective-permute-start(bf16[512,256]{1,0:T(8,128)(2,1)S(1)} %get-tuple-element.77), channel_id=1, source_target_pairs={{0,24},{8,16},{16,8},{24,0},{1,25},{9,17},{17,9},{25,1},{2,26},{10... | collective-permute-start | bytes 786440 | tf_op jit(solution)/shard_map/ppermute | solution.py:466
  72.7 1.0 %collective-permute-start.15 = (bf16[160,256]{1,0:T(8,128)(2,1)S(1)}, bf16[160,256]{1,0:T(8,128)(2,1)S(1)}, u32[]{:S(2)}, u32[]{:S(2)}) collective-permute-start(bf16[160,256]{1,0:T(8,128)(2,1)S(1)} %add_messages.8.own_ref), channel_id=1, source_target_pairs={{0,4},{1,5},{2,6},{3,7},{4,0},{5,1},{6,2},{7,3},{8,12},{9,13},{10,... | collective-permute-start | bytes 245768 | tf_op jit(solution)/shard_map/ppermute | solution.py:466
  73.7 5.1 %collective-permute-done.15.other_ref = bf16[160,256]{1,0:T(8,128)(2,1)S(1)} collective-permute-done((bf16[160,256]{1,0:T(8,128)(2,1)S(1)}, bf16[160,256]{1,0:T(8,128)(2,1)S(1)}, u32[]{:S(2)}, u32[]{:S(2)}) %collective-permute-start.15) | collective-permute-done | bytes 81952 | tf_op jit(solution)/shard_map/ppermute | solution.py:466
  78.9 0.8 output.1
  79.7 0.5 collective-permute-done.29.other_ref
  80.1 1.3 %totals.1 = (f32[256,256]{1,0:T(8,128)}, f32[16,256]{1,0:T(8,128)}) custom-call(s32[2]{0:T(128)S(1)} %pad_add_fusion.at_ref, bf16[160,256]{1,0:T(8,128)(2,1)S(1)} %add_messages.9.own_ref, bf16[160,256]{1,0:T(8,128)(2,1)S(1)} %collective-permute-done.29.other_ref), custom_call_target="tpu_custom_call" | custom-call | flops 1 | bytes 1 | tf_op jit(solution)/shard_map/totals/pallas_call | solution.py:390
  81.4 1.5 %backward.7 = (f32[512,256]{1,0:T(8,128)S(1)}, bf16[2048,256]{1,0:T(8,128)(2,1)}) custom-call(bf16[4096,2048]{1,0:T(8,128)(2,1)S(1)} %build_tile.1.tile_ref, f32[512,256]{1,0:T(8,128)S(1)} %get-tuple-element.69.refs_0_, bf16[2048,256]{1,0:T(8,128)(2,1)S(1)} %get-tuple-element.82.refs_1_), custom_call_target="tpu_custom_call" | custom-call | flops 268435456 | tf_op jit(solution)/shard_map/backward/pallas_call | solution.py:431
  82.9 0.8 %finish.1 = bf16[512,256]{1,0:T(8,128)(2,1)} custom-call(f32[512,256]{1,0:T(8,128)S(1)} %get-tuple-element.83.refs_0_, bf16[512,256]{1,0:T(8,128)(2,1)S(1)} %collective-permute-done.26.refs_1_, bf16[512,256]{1,0:T(8,128)(2,1)S(1)} %collective-permute-done.27.refs_2_, bf16[512,256]{1,0:T(8,128)(2,1)S(1)} %collective-permute-done.28.refs_3_), custom_call_target="tpu_custom_call" | custom-call | flops 1 | bytes 1 | tf_op jit(solution)/shard_map/finish/pallas_call | solution.py:454
  (56 shorter events, 2.5 us)
Async XLA Ops:
  0.6 30.3 %copy-start = (f32[16,256]{1,0:T(8,128)S(1)}, f32[16,256]{1,0:T(8,128)}, u32[]{:S(2)}) copy-start(f32[16,256]{1,0:T(8,128)} %param.15) | copy-start | bytes 49156
  0.6 11.7 %collective-permute-start = (bf16[512,256]{1,0:T(8,128)(2,1)}, bf16[512,256]{1,0:T(8,128)(2,1)S(1)}, u32[]{:S(2)}, u32[]{:S(2)}) collective-permute-start(bf16[512,256]{1,0:T(8,128)(2,1)} %refs_0_.3), channel_id=1, source_target_pairs={{0,8},{8,0},{16,24},{24,16},{1,9},{9,1},{17,25},{25,17},{2,10},{10... | collective-permute-start | bytes 786440 | tf_op jit(solution)/shard_map/ppermute | solution.py:466
  3.6 13.6 %collective-permute-start.1 = (bf16[512,256]{1,0:T(8,128)(2,1)}, bf16[512,256]{1,0:T(8,128)(2,1)S(1)}, u32[]{:S(2)}, u32[]{:S(2)}) collective-permute-start(bf16[512,256]{1,0:T(8,128)(2,1)} %refs_0_.3), channel_id=1, source_target_pairs={{0,16},{8,24},{16,0},{24,8},{1,17},{9,25},{17,1},{25,9},{2,18},{10... | collective-permute-start | bytes 786440 | tf_op jit(solution)/shard_map/ppermute | solution.py:466
  5.2 12.1 %collective-permute-start.2 = (bf16[512,256]{1,0:T(8,128)(2,1)}, bf16[512,256]{1,0:T(8,128)(2,1)S(1)}, u32[]{:S(2)}, u32[]{:S(2)}) collective-permute-start(bf16[512,256]{1,0:T(8,128)(2,1)} %refs_0_.3), channel_id=1, source_target_pairs={{0,24},{8,16},{16,8},{24,0},{1,25},{9,17},{17,9},{25,1},{2,26},{10... | collective-permute-start | bytes 786440 | tf_op jit(solution)/shard_map/ppermute | solution.py:466
  5.9 0.7 copy-start.4
  6.6 0.7 copy-start.5
  7.3 5.1 %copy-start.2 = (bf16[512,256]{1,0:T(8,128)(2,1)S(1)}, bf16[512,256]{1,0:T(8,128)(2,1)}, u32[]{:S(2)}) copy-start(bf16[512,256]{1,0:T(8,128)(2,1)} %refs_0_.3) | copy-start | bytes 786436
  18.5 3.2 %collective-permute-start.4 = (bf16[1024,256]{1,0:T(8,128)(2,1)S(1)}, bf16[1024,256]{1,0:T(8,128)(2,1)S(1)}, u32[]{:S(2)}, u32[]{:S(2)}) collective-permute-start(bf16[1024,256]{1,0:T(8,128)(2,1)S(1)} %get-tuple-element.48), channel_id=1, source_target_pairs={{0,1},{1,0},{2,3},{3,2},{4,5},{5,4},{6,7},{7,6},{8,9},{9,8},{10,11... | collective-permute-start | bytes 1572872 | tf_op jit(solution)/shard_map/ppermute | solution.py:466
  19.8 11.1 %copy-start.1 = (bf16[512,256]{1,0:T(8,128)(2,1)S(1)}, bf16[512,256]{1,0:T(8,128)(2,1)}, u32[]{:S(2)}) copy-start(bf16[512,256]{1,0:T(8,128)(2,1)} %cotangent_ref.3) | copy-start | bytes 786436
  19.9 11.1 %copy-start.6 = (s32[512]{0:T(512)S(1)}, s32[512]{0:T(512)}, u32[]{:S(2)}) copy-start(s32[512]{0:T(512)} %param.16) | copy-start | bytes 6148
  19.9 18.0 %copy-start.3 = (bf16[256,256]{1,0:T(8,128)(2,1)S(1)}, bf16[256,256]{1,0:T(8,128)(2,1)}, u32[]{:S(2)}) copy-start(bf16[256,256]{1,0:T(8,128)(2,1)} %weight_ref.3) | copy-start | bytes 393220
  21.2 2.3 %collective-permute-start.3 = (bf16[1024,256]{1,0:T(8,128)(2,1)S(1)}, bf16[1024,256]{1,0:T(8,128)(2,1)S(1)}, u32[]{:S(2)}, u32[]{:S(2)}) collective-permute-start(bf16[1024,256]{1,0:T(8,128)(2,1)S(1)} %get-tuple-element.46), channel_id=1, source_target_pairs={{0,1},{1,0},{2,3},{3,2},{4,5},{5,4},{6,7},{7,6},{8,9},{9,8},{10,11... | collective-permute-start | bytes 1572872 | tf_op jit(solution)/shard_map/ppermute | solution.py:466
  21.8 6.4 %collective-permute-start.6 = (bf16[256,256]{1,0:T(8,128)(2,1)S(1)}, bf16[256,256]{1,0:T(8,128)(2,1)S(1)}, u32[]{:S(2)}, u32[]{:S(2)}) collective-permute-start(bf16[256,256]{1,0:T(8,128)(2,1)S(1)} %get-tuple-element.49), channel_id=1, source_target_pairs={{0,2},{1,3},{2,0},{3,1},{4,6},{5,7},{6,4},{7,5},{8,10},{9,11},{10,... | collective-permute-start | bytes 393224 | tf_op jit(solution)/shard_map/ppermute | solution.py:466
  23.5 9.5 %collective-permute-start.5 = (bf16[256,256]{1,0:T(8,128)(2,1)S(1)}, bf16[256,256]{1,0:T(8,128)(2,1)S(1)}, u32[]{:S(2)}, u32[]{:S(2)}) collective-permute-start(bf16[256,256]{1,0:T(8,128)(2,1)S(1)} %get-tuple-element.51), channel_id=1, source_target_pairs={{0,2},{1,3},{2,0},{3,1},{4,6},{5,7},{6,4},{7,5},{8,10},{9,11},{10,... | collective-permute-start | bytes 393224 | tf_op jit(solution)/shard_map/ppermute | solution.py:466
  25.0 12.9 %collective-permute-start.7 = (bf16[256,256]{1,0:T(8,128)(2,1)S(1)}, bf16[256,256]{1,0:T(8,128)(2,1)S(1)}, u32[]{:S(2)}, u32[]{:S(2)}) collective-permute-start(bf16[256,256]{1,0:T(8,128)(2,1)S(1)} %get-tuple-element.55), channel_id=1, source_target_pairs={{0,2},{1,3},{2,0},{3,1},{4,6},{5,7},{6,4},{7,5},{8,10},{9,11},{10,... | collective-permute-start | bytes 393224 | tf_op jit(solution)/shard_map/ppermute | solution.py:466
  28.3 9.6 %collective-permute-start.8 = (bf16[256,256]{1,0:T(8,128)(2,1)S(1)}, bf16[256,256]{1,0:T(8,128)(2,1)S(1)}, u32[]{:S(2)}, u32[]{:S(2)}) collective-permute-start(bf16[256,256]{1,0:T(8,128)(2,1)S(1)} %combine.6), channel_id=1, source_target_pairs={{0,4},{1,5},{2,6},{3,7},{4,0},{5,1},{6,2},{7,3},{8,12},{9,13},{10,... | collective-permute-start | bytes 393224 | tf_op jit(solution)/shard_map/ppermute | solution.py:466
  31.4 11.6 %collective-permute-start.9 = (bf16[256,256]{1,0:T(8,128)(2,1)S(1)}, bf16[256,256]{1,0:T(8,128)(2,1)S(1)}, u32[]{:S(2)}, u32[]{:S(2)}) collective-permute-start(bf16[256,256]{1,0:T(8,128)(2,1)S(1)} %get-tuple-element.61), channel_id=1, source_target_pairs={{0,2},{1,3},{2,0},{3,1},{4,6},{5,7},{6,4},{7,5},{8,10},{9,11},{10,... | collective-permute-start | bytes 393224 | tf_op jit(solution)/shard_map/ppermute | solution.py:466
  33.1 9.9 %collective-permute-start.10 = (bf16[256,256]{1,0:T(8,128)(2,1)S(1)}, bf16[256,256]{1,0:T(8,128)(2,1)S(1)}, u32[]{:S(2)}, u32[]{:S(2)}) collective-permute-start(bf16[256,256]{1,0:T(8,128)(2,1)S(1)} %combine.7), channel_id=1, source_target_pairs={{0,4},{1,5},{2,6},{3,7},{4,0},{5,1},{6,2},{7,3},{8,12},{9,13},{10,... | collective-permute-start | bytes 393224 | tf_op jit(solution)/shard_map/ppermute | solution.py:466
  38.3 11.1 %collective-permute-start.17 = (bf16[256,256]{1,0:T(8,128)(2,1)S(1)}, bf16[256,256]{1,0:T(8,128)(2,1)S(1)}, u32[]{:S(2)}, u32[]{:S(2)}) collective-permute-start(bf16[256,256]{1,0:T(8,128)(2,1)S(1)} %get-tuple-element.59.refs_0_), channel_id=1, source_target_pairs={{0,2},{1,3},{2,0},{3,1},{4,6},{5,7},{6,4},{7,5},{8,10},{9,11},{10,... | collective-permute-start | bytes 393224 | tf_op jit(solution)/shard_map/ppermute | solution.py:466
  39.7 9.6 %collective-permute-start.16 = (bf16[256,256]{1,0:T(8,128)(2,1)S(1)}, bf16[256,256]{1,0:T(8,128)(2,1)S(1)}, u32[]{:S(2)}, u32[]{:S(2)}) collective-permute-start(bf16[256,256]{1,0:T(8,128)(2,1)S(1)} %get-tuple-element.59.refs_0_), channel_id=1, source_target_pairs={{0,4},{1,5},{2,6},{3,7},{4,0},{5,1},{6,2},{7,3},{8,12},{9,13},{10,... | collective-permute-start | bytes 393224 | tf_op jit(solution)/shard_map/ppermute | solution.py:466
  43.5 9.1 %collective-permute-start.22 = (bf16[256,256]{1,0:T(8,128)(2,1)S(1)}, bf16[256,256]{1,0:T(8,128)(2,1)S(1)}, u32[]{:S(2)}, u32[]{:S(2)}) collective-permute-start(bf16[256,256]{1,0:T(8,128)(2,1)S(1)} %get-tuple-element.73.refs_1_), channel_id=1, source_target_pairs={{0,2},{1,3},{2,0},{3,1},{4,6},{5,7},{6,4},{7,5},{8,10},{9,11},{10,... | collective-permute-start | bytes 393224 | tf_op jit(solution)/shard_map/ppermute | solution.py:466
  45.4 7.2 %collective-permute-start.21 = (bf16[256,256]{1,0:T(8,128)(2,1)S(1)}, bf16[256,256]{1,0:T(8,128)(2,1)S(1)}, u32[]{:S(2)}, u32[]{:S(2)}) collective-permute-start(bf16[256,256]{1,0:T(8,128)(2,1)S(1)} %get-tuple-element.73.refs_1_), channel_id=1, source_target_pairs={{0,4},{1,5},{2,6},{3,7},{4,0},{5,1},{6,2},{7,3},{8,12},{9,13},{10,... | collective-permute-start | bytes 393224 | tf_op jit(solution)/shard_map/ppermute | solution.py:466
  49.3 1.3 %collective-permute-start.11 = (bf16[160,256]{1,0:T(8,128)(2,1)S(1)}, bf16[160,256]{1,0:T(8,128)(2,1)S(1)}, u32[]{:S(2)}, u32[]{:S(2)}) collective-permute-start(bf16[160,256]{1,0:T(8,128)(2,1)S(1)} %get-tuple-element.66), channel_id=1, source_target_pairs={{0,1},{1,0},{2,3},{3,2},{4,5},{5,4},{6,7},{7,6},{8,9},{9,8},{10,11... | collective-permute-start | bytes 245768 | tf_op jit(solution)/shard_map/ppermute | solution.py:466
  49.4 14.9 %collective-permute-start.18 = (bf16[768,256]{1,0:T(8,128)(2,1)S(1)}, bf16[768,256]{1,0:T(8,128)(2,1)S(1)}, u32[]{:S(2)}, u32[]{:S(2)}) collective-permute-start(bf16[768,256]{1,0:T(8,128)(2,1)S(1)} %pad_maximum_fusion), channel_id=1, source_target_pairs={{0,1},{1,0},{2,3},{3,2},{4,5},{5,4},{6,7},{7,6},{8,9},{9,8},{10,11... | collective-permute-start | bytes 1179656 | tf_op jit(solution)/shard_map/ppermute | solution.py:466
  50.6 4.6 %collective-permute-start.12 = (bf16[160,256]{1,0:T(8,128)(2,1)S(1)}, bf16[160,256]{1,0:T(8,128)(2,1)S(1)}, u32[]{:S(2)}, u32[]{:S(2)}) collective-permute-start(bf16[160,256]{1,0:T(8,128)(2,1)S(1)} %add_messages.5.own_ref), channel_id=1, source_target_pairs={{0,8},{8,0},{16,24},{24,16},{1,9},{9,1},{17,25},{25,17},{2,10},{10... | collective-permute-start | bytes 245768 | tf_op jit(solution)/shard_map/ppermute | solution.py:466
  51.9 5.3 %collective-permute-start.19 = (bf16[256,256]{1,0:T(8,128)(2,1)S(1)}, bf16[256,256]{1,0:T(8,128)(2,1)S(1)}, u32[]{:S(2)}, u32[]{:S(2)}) collective-permute-start(bf16[256,256]{1,0:T(8,128)(2,1)S(1)} %collective-permute-done.16.refs_2_), channel_id=1, source_target_pairs={{0,2},{1,3},{2,0},{3,1},{4,6},{5,7},{6,4},{7,5},{8,10},{9,11},{10,... | collective-permute-start | bytes 393224 | tf_op jit(solution)/shard_map/ppermute | solution.py:466
  52.6 14.3 %collective-permute-start.23 = (bf16[768,256]{1,0:T(8,128)(2,1)S(1)}, bf16[768,256]{1,0:T(8,128)(2,1)S(1)}, u32[]{:S(2)}, u32[]{:S(2)}) collective-permute-start(bf16[768,256]{1,0:T(8,128)(2,1)S(1)} %pad_maximum_fusion.1), channel_id=1, source_target_pairs={{0,1},{1,0},{2,3},{3,2},{4,5},{5,4},{6,7},{7,6},{8,9},{9,8},{10,11... | collective-permute-start | bytes 1179656 | tf_op jit(solution)/shard_map/ppermute | solution.py:466
  55.2 4.5 %collective-permute-start.13 = (bf16[160,256]{1,0:T(8,128)(2,1)S(1)}, bf16[160,256]{1,0:T(8,128)(2,1)S(1)}, u32[]{:S(2)}, u32[]{:S(2)}) collective-permute-start(bf16[160,256]{1,0:T(8,128)(2,1)S(1)} %add_messages.6.own_ref), channel_id=1, source_target_pairs={{0,16},{8,24},{16,0},{24,8},{1,17},{9,25},{17,1},{25,9},{2,18},{10... | collective-permute-start | bytes 245768 | tf_op jit(solution)/shard_map/ppermute | solution.py:466
  56.8 5.8 %collective-permute-start.24 = (bf16[256,256]{1,0:T(8,128)(2,1)S(1)}, bf16[256,256]{1,0:T(8,128)(2,1)S(1)}, u32[]{:S(2)}, u32[]{:S(2)}) collective-permute-start(bf16[256,256]{1,0:T(8,128)(2,1)S(1)} %collective-permute-done.21.refs_3_), channel_id=1, source_target_pairs={{0,2},{1,3},{2,0},{3,1},{4,6},{5,7},{6,4},{7,5},{8,10},{9,11},{10,... | collective-permute-start | bytes 393224 | tf_op jit(solution)/shard_map/ppermute | solution.py:466
  57.2 7.1 %collective-permute-start.20 = (bf16[256,256]{1,0:T(8,128)(2,1)S(1)}, bf16[256,256]{1,0:T(8,128)(2,1)S(1)}, u32[]{:S(2)}, u32[]{:S(2)}) collective-permute-start(bf16[256,256]{1,0:T(8,128)(2,1)S(1)} %collective-permute-done.19.refs_6_), channel_id=1, source_target_pairs={{0,1},{1,0},{2,3},{3,2},{4,5},{5,4},{6,7},{7,6},{8,9},{9,8},{10,11... | collective-permute-start | bytes 393224 | tf_op jit(solution)/shard_map/ppermute | solution.py:466
  59.8 4.5 %collective-permute-start.14 = (bf16[160,256]{1,0:T(8,128)(2,1)S(1)}, bf16[160,256]{1,0:T(8,128)(2,1)S(1)}, u32[]{:S(2)}, u32[]{:S(2)}) collective-permute-start(bf16[160,256]{1,0:T(8,128)(2,1)S(1)} %add_messages.7.own_ref), channel_id=1, source_target_pairs={{0,2},{1,3},{2,0},{3,1},{4,6},{5,7},{6,4},{7,5},{8,10},{9,11},{10,... | collective-permute-start | bytes 245768 | tf_op jit(solution)/shard_map/ppermute | solution.py:466
  62.7 4.2 %collective-permute-start.25 = (bf16[256,256]{1,0:T(8,128)(2,1)S(1)}, bf16[256,256]{1,0:T(8,128)(2,1)S(1)}, u32[]{:S(2)}, u32[]{:S(2)}) collective-permute-start(bf16[256,256]{1,0:T(8,128)(2,1)S(1)} %collective-permute-done.24.refs_7_), channel_id=1, source_target_pairs={{0,1},{1,0},{2,3},{3,2},{4,5},{5,4},{6,7},{7,6},{8,9},{9,8},{10,11... | collective-permute-start | bytes 393224 | tf_op jit(solution)/shard_map/ppermute | solution.py:466
  69.1 13.8 %collective-permute-start.26 = (bf16[512,256]{1,0:T(8,128)(2,1)S(1)}, bf16[512,256]{1,0:T(8,128)(2,1)S(1)}, u32[]{:S(2)}, u32[]{:S(2)}) collective-permute-start(bf16[512,256]{1,0:T(8,128)(2,1)S(1)} %get-tuple-element.80), channel_id=1, source_target_pairs={{0,8},{8,0},{16,24},{24,16},{1,9},{9,1},{17,25},{25,17},{2,10},{10... | collective-permute-start | bytes 786440 | tf_op jit(solution)/shard_map/ppermute | solution.py:466
  70.4 12.5 %collective-permute-start.27 = (bf16[512,256]{1,0:T(8,128)(2,1)S(1)}, bf16[512,256]{1,0:T(8,128)(2,1)S(1)}, u32[]{:S(2)}, u32[]{:S(2)}) collective-permute-start(bf16[512,256]{1,0:T(8,128)(2,1)S(1)} %get-tuple-element.81), channel_id=1, source_target_pairs={{0,16},{8,24},{16,0},{24,8},{1,17},{9,25},{17,1},{25,9},{2,18},{10... | collective-permute-start | bytes 786440 | tf_op jit(solution)/shard_map/ppermute | solution.py:466
  71.2 11.7 %collective-permute-start.28 = (bf16[512,256]{1,0:T(8,128)(2,1)S(1)}, bf16[512,256]{1,0:T(8,128)(2,1)S(1)}, u32[]{:S(2)}, u32[]{:S(2)}) collective-permute-start(bf16[512,256]{1,0:T(8,128)(2,1)S(1)} %get-tuple-element.77), channel_id=1, source_target_pairs={{0,24},{8,16},{16,8},{24,0},{1,25},{9,17},{17,9},{25,1},{2,26},{10... | collective-permute-start | bytes 786440 | tf_op jit(solution)/shard_map/ppermute | solution.py:466
  72.7 6.1 %collective-permute-start.15 = (bf16[160,256]{1,0:T(8,128)(2,1)S(1)}, bf16[160,256]{1,0:T(8,128)(2,1)S(1)}, u32[]{:S(2)}, u32[]{:S(2)}) collective-permute-start(bf16[160,256]{1,0:T(8,128)(2,1)S(1)} %add_messages.8.own_ref), channel_id=1, source_target_pairs={{0,4},{1,5},{2,6},{3,7},{4,0},{5,1},{6,2},{7,3},{8,12},{9,13},{10,... | collective-permute-start | bytes 245768 | tf_op jit(solution)/shard_map/ppermute | solution.py:466
  78.8 1.3 %collective-permute-start.29 = (bf16[160,256]{1,0:T(8,128)(2,1)S(1)}, bf16[160,256]{1,0:T(8,128)(2,1)S(1)}, u32[]{:S(2)}, u32[]{:S(2)}) collective-permute-start(bf16[160,256]{1,0:T(8,128)(2,1)S(1)} %add_messages.9.own_ref), channel_id=1, source_target_pairs={{0,1},{1,0},{2,3},{3,2},{4,5},{5,4},{6,7},{7,6},{8,9},{9,8},{10,11... | collective-permute-start | bytes 245768 | tf_op jit(solution)/shard_map/ppermute | solution.py:466

commit v6 on v5

--- a/solution.py
+++ b/solution.py
@@ -545,12 +545,8 @@
                 held[n][k ^ bit] = swap(sent, "col", bit, col_count)
     stages = [("row", bit, row_count) for bit in bits_of(row_count)]
     stages += [("col", bit, col_count) for bit in col_bits[1:]]
-    for stage in stages:
+    for stage in stages[:-1]:
         messages.append(add_messages(part_count, messages[-1], swap(messages[-1], *stage)))
-    other = swap(messages[-1], "col", col_bits[0], col_count)
-    weight_grad, gain_grad = totals(part_count, scale, at, messages[-1], other)
-
-    layer_out = output(after(row_gains, messages[4]), [g[3] for g in gated])
     sums = []
     bit = col_bits[0]
     for n in chunks:
@@ -580,7 +576,13 @@
         blocks, places = [after(panel, messages[3], *outs)], [(0, 0, panel.shape[0])]
         for r, out in zip(targets, outs):
             parts[r] = swap(out, "row", r, row_count) if r else out
+    arrived = swap(messages[-1], *stages[-1])
+    own = after(messages[-1], parts[0])
+    messages.append(add_messages(part_count, own, arrived))
+    other = swap(messages[-1], "col", col_bits[0], col_count)
+    weight_grad, gain_grad = totals(part_count, scale, at, messages[-1], other)
     feature_grad = finish(parts)
+    layer_out = output(after(row_gains, messages[-1]), [g[3] for g in gated])
 
     return (layer_out, feature_grad, weight_grad, gain_grad)
 

time: 83.9 us -> 83 us (0.989)
  transfers between devices with their start and end apart: 30 -> 30, of which waited for: 12 -> 13; matrix products, arithmetic and copies ran while one was open for 1% -> 1% of each run, Pallas kernels for 21% -> 20%
where the time goes in v6:
time: 83 us; the launch traced here: 82.8 us
  starting transfers between devices  32.8 us (40%)
  waiting for transfers between devices  25.3 us (30%)
  Pallas kernels  21.2 us (26%)
  between operations  1.55 us (2%)
  local copies, waits for them, and re-layouts  1.39 us (2%)
    ppermute x30, starting transfers between devices, swap(): return lax.ppermute(values, axis, [(d, d ^ mask) for d in range(count)])  32.8 us
    ppermute x30, waiting for transfers between devices, swap(): return lax.ppermute(values, axis, [(d, d ^ mask) for d in range(count)])  25.3 us
    pallas_call x4, Pallas kernels, backward(): pl.pallas_call(functools.partial(backward_kernel, chunk, targets, places)...  6.22 us
    pallas_call x4, Pallas kernels, forward(): pl.pallas_call(functools.partial(forward_kernel, chunk, first), out_shape...  5.03 us
    pallas_call x1, Pallas kernels, build_tile(): pl.pallas_call(functools.partial(build_kernel, layout), out_shape=pltpu.V...  4.64 us
  transfers between devices with their start and end apart: 30, of which 13 were waited for; matrix products, arithmetic and copies ran while one was open for 1% of the time, Pallas kernels for 20%

profile of v6, /device:TPU:0, one launch (start us, length us, event | category | flops | bytes accessed | tf_op | source)
XLA Modules:
  0.0 82.8 jit_solution(17391984250676833199)
XLA Ops:
  0.6 3.0 %collective-permute-start = (bf16[512,256]{1,0:T(8,128)(2,1)}, bf16[512,256]{1,0:T(8,128)(2,1)S(1)}, u32[]{:S(2)}, u32[]{:S(2)}) collective-permute-start(bf16[512,256]{1,0:T(8,128)(2,1)} %refs_0_.3), channel_id=1, source_target_pairs={{0,8},{8,0},{16,24},{24,16},{1,9},{9,1},{17,25},{25,17},{2,10},{10... | collective-permute-start | bytes 786440 | tf_op jit(solution)/shard_map/ppermute | solution.py:466
  3.6 1.5 %collective-permute-start.1 = (bf16[512,256]{1,0:T(8,128)(2,1)}, bf16[512,256]{1,0:T(8,128)(2,1)S(1)}, u32[]{:S(2)}, u32[]{:S(2)}) collective-permute-start(bf16[512,256]{1,0:T(8,128)(2,1)} %refs_0_.3), channel_id=1, source_target_pairs={{0,16},{8,24},{16,0},{24,8},{1,17},{9,25},{17,1},{25,9},{2,18},{10... | collective-permute-start | bytes 786440 | tf_op jit(solution)/shard_map/ppermute | solution.py:466
  5.9 0.7 copy-done.4
  6.6 0.7 copy-done.5
  7.3 4.6 %build_tile.1.tile_ref = bf16[4096,2048]{1,0:T(8,128)(2,1)S(1)} custom-call(s32[2]{0:T(128)S(1)} %pad_add_fusion.at_ref, s32[1,1]{1,0:T(1,128)S(6)} %copy.13.live_ref, s32[1,1,384]{2,1,0:T(1,128)S(1)} %copy-done.4, s32[1,1,384]{2,1,0:T(1,128)S(1)} %copy-done.5, bf16[1,1,384,128,128]{4,3,2,1,0:T(8,128)(2,1)} %slots_ref.1), custom_call_target="tpu_custom_call" | custom-call | bytes 20971520 | tf_op jit(solution)/shard_map/build_tile/pallas_call | solution.py:119
  12.0 1.2 %forward.6.refs_0_ = f32[2048,256]{1,0:T(8,128)S(1)} custom-call(bf16[4096,2048]{1,0:T(8,128)(2,1)S(1)} %build_tile.1.tile_ref, bf16[512,256]{1,0:T(8,128)(2,1)S(1)} %copy-done.2, bf16[512,256]{1,0:T(8,128)(2,1)S(1)} %collective-permute-done.refs_1_), custom_call_target="tpu_custom_call" | custom-call | flops 1073741824 | tf_op jit(solution)/shard_map/forward/pallas_call | solution.py:166
  13.2 4.0 %collective-permute-done.1.refs_1_ = bf16[512,256]{1,0:T(8,128)(2,1)S(1)} collective-permute-done((bf16[512,256]{1,0:T(8,128)(2,1)}, bf16[512,256]{1,0:T(8,128)(2,1)S(1)}, u32[]{:S(2)}, u32[]{:S(2)}) %collective-permute-start.1) | collective-permute-done | bytes 262176 | tf_op jit(solution)/shard_map/ppermute | solution.py:466
  17.2 1.3 %forward.7 = (bf16[1024,256]{1,0:T(8,128)(2,1)S(1)}, bf16[1024,256]{1,0:T(8,128)(2,1)S(1)}) custom-call(bf16[4096,2048]{1,0:T(8,128)(2,1)S(1)} %build_tile.1.tile_ref, f32[2048,256]{1,0:T(8,128)S(1)} %forward.6.refs_0_, bf16[512,256]{1,0:T(8,128)(2,1)S(1)} %collective-permute-done.1.refs_1_, bf16[512,256]{1,0:T(8,128)(2,1)S(1)} %collective-permute-done.2.refs_2_), custom_call_target="tpu_custom_call" | custom-call | flops 1073741824 | tf_op jit(solution)/shard_map/forward/pallas_call | solution.py:166
  18.6 1.2 %forward.4.refs_0_ = f32[2048,256]{1,0:T(8,128)S(1)} custom-call(bf16[4096,2048]{1,0:T(8,128)(2,1)S(1)} %build_tile.1.tile_ref, bf16[512,256]{1,0:T(8,128)(2,1)S(1)} %copy-done.2, bf16[512,256]{1,0:T(8,128)(2,1)S(1)} %collective-permute-done.refs_1_), custom_call_target="tpu_custom_call" | custom-call | flops 1073741824 | tf_op jit(solution)/shard_map/forward/pallas_call | solution.py:166
  19.9 1.3 %forward.5 = (bf16[1024,256]{1,0:T(8,128)(2,1)S(1)}, bf16[1024,256]{1,0:T(8,128)(2,1)S(1)}) custom-call(bf16[4096,2048]{1,0:T(8,128)(2,1)S(1)} %build_tile.1.tile_ref, f32[2048,256]{1,0:T(8,128)S(1)} %forward.4.refs_0_, bf16[512,256]{1,0:T(8,128)(2,1)S(1)} %collective-permute-done.1.refs_1_, bf16[512,256]{1,0:T(8,128)(2,1)S(1)} %collective-permute-done.2.refs_2_), custom_call_target="tpu_custom_call" | custom-call | flops 1073741824 | tf_op jit(solution)/shard_map/forward/pallas_call | solution.py:166
  21.2 0.6 collective-permute-start.3
  21.8 1.6 %collective-permute-start.6 = (bf16[256,256]{1,0:T(8,128)(2,1)S(1)}, bf16[256,256]{1,0:T(8,128)(2,1)S(1)}, u32[]{:S(2)}, u32[]{:S(2)}) collective-permute-start(bf16[256,256]{1,0:T(8,128)(2,1)S(1)} %get-tuple-element.50), channel_id=1, source_target_pairs={{0,2},{1,3},{2,0},{3,1},{4,6},{5,7},{6,4},{7,5},{8,10},{9,11},{10,... | collective-permute-start | bytes 393224 | tf_op jit(solution)/shard_map/ppermute | solution.py:466
  23.5 1.5 %collective-permute-start.5 = (bf16[256,256]{1,0:T(8,128)(2,1)S(1)}, bf16[256,256]{1,0:T(8,128)(2,1)S(1)}, u32[]{:S(2)}, u32[]{:S(2)}) collective-permute-start(bf16[256,256]{1,0:T(8,128)(2,1)S(1)} %get-tuple-element.52), channel_id=1, source_target_pairs={{0,2},{1,3},{2,0},{3,1},{4,6},{5,7},{6,4},{7,5},{8,10},{9,11},{10,... | collective-permute-start | bytes 393224 | tf_op jit(solution)/shard_map/ppermute | solution.py:466
  25.0 0.6 collective-permute-start.7
  25.6 2.6 %collective-permute-done.6.refs_2_ = bf16[256,256]{1,0:T(8,128)(2,1)S(1)} collective-permute-done((bf16[256,256]{1,0:T(8,128)(2,1)S(1)}, bf16[256,256]{1,0:T(8,128)(2,1)S(1)}, u32[]{:S(2)}, u32[]{:S(2)}) %collective-permute-start.6) | collective-permute-done | bytes 131104 | tf_op jit(solution)/shard_map/ppermute | solution.py:466
  28.3 2.6 %collective-permute-start.8 = (bf16[256,256]{1,0:T(8,128)(2,1)S(1)}, bf16[256,256]{1,0:T(8,128)(2,1)S(1)}, u32[]{:S(2)}, u32[]{:S(2)}) collective-permute-start(bf16[256,256]{1,0:T(8,128)(2,1)S(1)} %combine.6), channel_id=1, source_target_pairs={{0,4},{1,5},{2,6},{3,7},{4,0},{5,1},{6,2},{7,3},{8,12},{9,13},{10,... | collective-permute-start | bytes 393224 | tf_op jit(solution)/shard_map/ppermute | solution.py:466
  31.4 1.6 %collective-permute-start.9 = (bf16[256,256]{1,0:T(8,128)(2,1)S(1)}, bf16[256,256]{1,0:T(8,128)(2,1)S(1)}, u32[]{:S(2)}, u32[]{:S(2)}) collective-permute-start(bf16[256,256]{1,0:T(8,128)(2,1)S(1)} %get-tuple-element.62), channel_id=1, source_target_pairs={{0,2},{1,3},{2,0},{3,1},{4,6},{5,7},{6,4},{7,5},{8,10},{9,11},{10,... | collective-permute-start | bytes 393224 | tf_op jit(solution)/shard_map/ppermute | solution.py:466
  33.1 1.2 %collective-permute-start.10 = (bf16[256,256]{1,0:T(8,128)(2,1)S(1)}, bf16[256,256]{1,0:T(8,128)(2,1)S(1)}, u32[]{:S(2)}, u32[]{:S(2)}) collective-permute-start(bf16[256,256]{1,0:T(8,128)(2,1)S(1)} %combine.7), channel_id=1, source_target_pairs={{0,4},{1,5},{2,6},{3,7},{4,0},{5,1},{6,2},{7,3},{8,12},{9,13},{10,... | collective-permute-start | bytes 393224 | tf_op jit(solution)/shard_map/ppermute | solution.py:466
  34.2 3.6 %collective-permute-done.7.refs_2_ = bf16[256,256]{1,0:T(8,128)(2,1)S(1)} collective-permute-done((bf16[256,256]{1,0:T(8,128)(2,1)S(1)}, bf16[256,256]{1,0:T(8,128)(2,1)S(1)}, u32[]{:S(2)}, u32[]{:S(2)}) %collective-permute-start.7) | collective-permute-done | bytes 131104 | tf_op jit(solution)/shard_map/ppermute | solution.py:466
  38.3 1.5 %collective-permute-start.16 = (bf16[256,256]{1,0:T(8,128)(2,1)S(1)}, bf16[256,256]{1,0:T(8,128)(2,1)S(1)}, u32[]{:S(2)}, u32[]{:S(2)}) collective-permute-start(bf16[256,256]{1,0:T(8,128)(2,1)S(1)} %get-tuple-element.60.refs_0_), channel_id=1, source_target_pairs={{0,2},{1,3},{2,0},{3,1},{4,6},{5,7},{6,4},{7,5},{8,10},{9,11},{10,... | collective-permute-start | bytes 393224 | tf_op jit(solution)/shard_map/ppermute | solution.py:466
  39.7 3.3 %collective-permute-start.15 = (bf16[256,256]{1,0:T(8,128)(2,1)S(1)}, bf16[256,256]{1,0:T(8,128)(2,1)S(1)}, u32[]{:S(2)}, u32[]{:S(2)}) collective-permute-start(bf16[256,256]{1,0:T(8,128)(2,1)S(1)} %get-tuple-element.60.refs_0_), channel_id=1, source_target_pairs={{0,4},{1,5},{2,6},{3,7},{4,0},{5,1},{6,2},{7,3},{8,12},{9,13},{10,... | collective-permute-start | bytes 393224 | tf_op jit(solution)/shard_map/ppermute | solution.py:466
  43.5 1.9 %collective-permute-start.21 = (bf16[256,256]{1,0:T(8,128)(2,1)S(1)}, bf16[256,256]{1,0:T(8,128)(2,1)S(1)}, u32[]{:S(2)}, u32[]{:S(2)}) collective-permute-start(bf16[256,256]{1,0:T(8,128)(2,1)S(1)} %get-tuple-element.73.refs_1_), channel_id=1, source_target_pairs={{0,2},{1,3},{2,0},{3,1},{4,6},{5,7},{6,4},{7,5},{8,10},{9,11},{10,... | collective-permute-start | bytes 393224 | tf_op jit(solution)/shard_map/ppermute | solution.py:466
  45.4 2.7 %collective-permute-start.20 = (bf16[256,256]{1,0:T(8,128)(2,1)S(1)}, bf16[256,256]{1,0:T(8,128)(2,1)S(1)}, u32[]{:S(2)}, u32[]{:S(2)}) collective-permute-start(bf16[256,256]{1,0:T(8,128)(2,1)S(1)} %get-tuple-element.73.refs_1_), channel_id=1, source_target_pairs={{0,4},{1,5},{2,6},{3,7},{4,0},{5,1},{6,2},{7,3},{8,12},{9,13},{10,... | collective-permute-start | bytes 393224 | tf_op jit(solution)/shard_map/ppermute | solution.py:466
  48.3 0.9 %local_last.1 = (bf16[160,256]{1,0:T(8,128)(2,1)S(1)}, bf16[160,256]{1,0:T(8,128)(2,1)S(1)}) custom-call(s32[2]{0:T(128)S(1)} %pad_add_fusion.at_ref, f32[16,512]{1,0:T(8,128)S(1)} %fusion.members_ref, bf16[512,256]{1,0:T(8,128)(2,1)S(1)} %copy-done.1, f32[288,256]{1,0:T(8,128)S(1)} %local_first.1.before_ref, ...), custom_call_target="tpu_custom_call" | custom-call | flops 1 | bytes 1 | tf_op jit(solution)/shard_map/local_last/pallas_call | solution.py:323
  49.4 0.5 collective-permute-start.17
  50.0 0.7 collective-permute-done.11.other_ref
  50.6 1.3 %collective-permute-start.12 = (bf16[160,256]{1,0:T(8,128)(2,1)S(1)}, bf16[160,256]{1,0:T(8,128)(2,1)S(1)}, u32[]{:S(2)}, u32[]{:S(2)}) collective-permute-start(bf16[160,256]{1,0:T(8,128)(2,1)S(1)} %add_messages.5.own_ref), channel_id=1, source_target_pairs={{0,8},{8,0},{16,24},{24,16},{1,9},{9,1},{17,25},{25,17},{2,10},{10... | collective-permute-start | bytes 245768 | tf_op jit(solution)/shard_map/ppermute | solution.py:466
  52.0 0.5 collective-permute-done.21.refs_5_
  52.7 2.5 %collective-permute-done.12.other_ref = bf16[160,256]{1,0:T(8,128)(2,1)S(1)} collective-permute-done((bf16[160,256]{1,0:T(8,128)(2,1)S(1)}, bf16[160,256]{1,0:T(8,128)(2,1)S(1)}, u32[]{:S(2)}, u32[]{:S(2)}) %collective-permute-start.12) | collective-permute-done | bytes 81952 | tf_op jit(solution)/shard_map/ppermute | solution.py:466
  55.2 1.6 %collective-permute-start.13 = (bf16[160,256]{1,0:T(8,128)(2,1)S(1)}, bf16[160,256]{1,0:T(8,128)(2,1)S(1)}, u32[]{:S(2)}, u32[]{:S(2)}) collective-permute-start(bf16[160,256]{1,0:T(8,128)(2,1)S(1)} %add_messages.6.own_ref), channel_id=1, source_target_pairs={{0,16},{8,24},{16,0},{24,8},{1,17},{9,25},{17,1},{25,9},{2,18},{10... | collective-permute-start | bytes 245768 | tf_op jit(solution)/shard_map/ppermute | solution.py:466
  57.2 2.5 %collective-permute-done.13.other_ref = bf16[160,256]{1,0:T(8,128)(2,1)S(1)} collective-permute-done((bf16[160,256]{1,0:T(8,128)(2,1)S(1)}, bf16[160,256]{1,0:T(8,128)(2,1)S(1)}, u32[]{:S(2)}, u32[]{:S(2)}) %collective-permute-start.13) | collective-permute-done | bytes 81952 | tf_op jit(solution)/shard_map/ppermute | solution.py:466
  59.8 0.5 collective-permute-start.14
  60.3 2.4 %collective-permute-done.23.refs_7_ = bf16[256,256]{1,0:T(8,128)(2,1)S(1)} collective-permute-done((bf16[256,256]{1,0:T(8,128)(2,1)S(1)}, bf16[256,256]{1,0:T(8,128)(2,1)S(1)}, u32[]{:S(2)}, u32[]{:S(2)}) %collective-permute-start.23) | collective-permute-done | bytes 131104 | tf_op jit(solution)/shard_map/ppermute | solution.py:466
  62.7 1.6 %collective-permute-done.14.other_ref = bf16[160,256]{1,0:T(8,128)(2,1)S(1)} collective-permute-done((bf16[160,256]{1,0:T(8,128)(2,1)S(1)}, bf16[160,256]{1,0:T(8,128)(2,1)S(1)}, u32[]{:S(2)}, u32[]{:S(2)}) %collective-permute-start.14) | collective-permute-done | bytes 81952 | tf_op jit(solution)/shard_map/ppermute | solution.py:466
  64.3 2.6 %backward.4 = (f32[512,256]{1,0:T(8,128)S(1)}, f32[512,256]{1,0:T(8,128)S(1)}, f32[512,256]{1,0:T(8,128)S(1)}, f32[512,256]{1,0:T(8,128)S(1)}, bf16[2048,256]{1,0:T(8,128)(2,1)}) custom-call(bf16[4096,2048]{1,0:T(8,128)(2,1)S(1)} %build_tile.1.tile_ref, bf16[256,256]{1,0:T(8,128)(2,1)S(1)} %get-tuple-element.60.refs_0_, ...), custom_call_target="tpu_custom_call" | custom-call | flops 2147483648 | tf_op jit(solution)/shard_map/backward/pallas_call | solution.py:431
  66.9 0.8 backward.5
  67.7 1.4 %backward.6 = (bf16[512,256]{1,0:T(8,128)(2,1)S(1)}, bf16[512,256]{1,0:T(8,128)(2,1)S(1)}, bf16[2048,256]{1,0:T(8,128)(2,1)S(1)}) custom-call(bf16[4096,2048]{1,0:T(8,128)(2,1)S(1)} %build_tile.1.tile_ref, f32[512,256]{1,0:T(8,128)S(1)} %get-tuple-element.70.refs_0_, f32[512,256]{1,0:T(8,128)S(1)} %get-tuple-element.71.refs_1_, ...), custom_call_target="tpu_custom_call" | custom-call | flops 4294967296 | tf_op jit(solution)/shard_map/backward/pallas_call | solution.py:431
  69.1 1.3 %collective-permute-start.26 = (bf16[512,256]{1,0:T(8,128)(2,1)S(1)}, bf16[512,256]{1,0:T(8,128)(2,1)S(1)}, u32[]{:S(2)}, u32[]{:S(2)}) collective-permute-start(bf16[512,256]{1,0:T(8,128)(2,1)S(1)} %get-tuple-element.80), channel_id=1, source_target_pairs={{0,8},{8,0},{16,24},{24,16},{1,9},{9,1},{17,25},{25,17},{2,10},{10... | collective-permute-start | bytes 786440 | tf_op jit(solution)/shard_map/ppermute | solution.py:466
  70.4 0.8 collective-permute-start.27
  71.2 1.4 %collective-permute-start.28 = (bf16[512,256]{1,0:T(8,128)(2,1)S(1)}, bf16[512,256]{1,0:T(8,128)(2,1)S(1)}, u32[]{:S(2)}, u32[]{:S(2)}) collective-permute-start(bf16[512,256]{1,0:T(8,128)(2,1)S(1)} %get-tuple-element.77), channel_id=1, source_target_pairs={{0,24},{8,16},{16,8},{24,0},{1,25},{9,17},{17,9},{25,1},{2,26},{10... | collective-permute-start | bytes 786440 | tf_op jit(solution)/shard_map/ppermute | solution.py:466
  72.7 1.0 %collective-permute-start.25 = (bf16[160,256]{1,0:T(8,128)(2,1)S(1)}, bf16[160,256]{1,0:T(8,128)(2,1)S(1)}, u32[]{:S(2)}, u32[]{:S(2)}) collective-permute-start(bf16[160,256]{1,0:T(8,128)(2,1)S(1)} %add_messages.8.own_ref), channel_id=1, source_target_pairs={{0,4},{1,5},{2,6},{3,7},{4,0},{5,1},{6,2},{7,3},{8,12},{9,13},{10,... | collective-permute-start | bytes 245768 | tf_op jit(solution)/shard_map/ppermute | solution.py:466
  73.7 1.5 %backward.7 = (f32[512,256]{1,0:T(8,128)S(1)}, bf16[2048,256]{1,0:T(8,128)(2,1)}) custom-call(bf16[4096,2048]{1,0:T(8,128)(2,1)S(1)} %build_tile.1.tile_ref, f32[512,256]{1,0:T(8,128)S(1)} %get-tuple-element.69.refs_0_, bf16[2048,256]{1,0:T(8,128)(2,1)S(1)} %get-tuple-element.82.refs_1_), custom_call_target="tpu_custom_call" | custom-call | flops 268435456 | tf_op jit(solution)/shard_map/backward/pallas_call | solution.py:431
  75.2 3.6 %collective-permute-done.25.other_ref = bf16[160,256]{1,0:T(8,128)(2,1)S(1)} collective-permute-done((bf16[160,256]{1,0:T(8,128)(2,1)S(1)}, bf16[160,256]{1,0:T(8,128)(2,1)S(1)}, u32[]{:S(2)}, u32[]{:S(2)}) %collective-permute-start.25) | collective-permute-done | bytes 81952 | tf_op jit(solution)/shard_map/ppermute | solution.py:466
  78.9 0.8 output.1
  79.7 0.5 collective-permute-done.29.other_ref
  80.1 1.3 %totals.1 = (f32[256,256]{1,0:T(8,128)}, f32[16,256]{1,0:T(8,128)}) custom-call(s32[2]{0:T(128)S(1)} %pad_add_fusion.at_ref, bf16[160,256]{1,0:T(8,128)(2,1)S(1)} %add_messages.9.own_ref, bf16[160,256]{1,0:T(8,128)(2,1)S(1)} %collective-permute-done.29.other_ref), custom_call_target="tpu_custom_call" | custom-call | flops 1 | bytes 1 | tf_op jit(solution)/shard_map/totals/pallas_call | solution.py:390
  81.4 0.6 collective-permute-done.27.refs_2_
  82.0 0.8 %finish.1 = bf16[512,256]{1,0:T(8,128)(2,1)} custom-call(f32[512,256]{1,0:T(8,128)S(1)} %get-tuple-element.83.refs_0_, bf16[512,256]{1,0:T(8,128)(2,1)S(1)} %collective-permute-done.26.refs_1_, bf16[512,256]{1,0:T(8,128)(2,1)S(1)} %collective-permute-done.27.refs_2_, bf16[512,256]{1,0:T(8,128)(2,1)S(1)} %collective-permute-done.28.refs_3_), custom_call_target="tpu_custom_call" | custom-call | flops 1 | bytes 1 | tf_op jit(solution)/shard_map/finish/pallas_call | solution.py:454
  (56 shorter events, 2.9 us)
Async XLA Ops:
  0.6 30.3 %copy-start = (f32[16,256]{1,0:T(8,128)S(1)}, f32[16,256]{1,0:T(8,128)}, u32[]{:S(2)}) copy-start(f32[16,256]{1,0:T(8,128)} %param.15) | copy-start | bytes 49156
  0.6 11.3 %collective-permute-start = (bf16[512,256]{1,0:T(8,128)(2,1)}, bf16[512,256]{1,0:T(8,128)(2,1)S(1)}, u32[]{:S(2)}, u32[]{:S(2)}) collective-permute-start(bf16[512,256]{1,0:T(8,128)(2,1)} %refs_0_.3), channel_id=1, source_target_pairs={{0,8},{8,0},{16,24},{24,16},{1,9},{9,1},{17,25},{25,17},{2,10},{10... | collective-permute-start | bytes 786440 | tf_op jit(solution)/shard_map/ppermute | solution.py:466
  3.6 13.6 %collective-permute-start.1 = (bf16[512,256]{1,0:T(8,128)(2,1)}, bf16[512,256]{1,0:T(8,128)(2,1)S(1)}, u32[]{:S(2)}, u32[]{:S(2)}) collective-permute-start(bf16[512,256]{1,0:T(8,128)(2,1)} %refs_0_.3), channel_id=1, source_target_pairs={{0,16},{8,24},{16,0},{24,8},{1,17},{9,25},{17,1},{25,9},{2,18},{10... | collective-permute-start | bytes 786440 | tf_op jit(solution)/shard_map/ppermute | solution.py:466
  5.2 12.1 %collective-permute-start.2 = (bf16[512,256]{1,0:T(8,128)(2,1)}, bf16[512,256]{1,0:T(8,128)(2,1)S(1)}, u32[]{:S(2)}, u32[]{:S(2)}) collective-permute-start(bf16[512,256]{1,0:T(8,128)(2,1)} %refs_0_.3), channel_id=1, source_target_pairs={{0,24},{8,16},{16,8},{24,0},{1,25},{9,17},{17,9},{25,1},{2,26},{10... | collective-permute-start | bytes 786440 | tf_op jit(solution)/shard_map/ppermute | solution.py:466
  5.9 0.7 copy-start.4
  6.6 0.7 copy-start.5
  7.3 4.7 %copy-start.2 = (bf16[512,256]{1,0:T(8,128)(2,1)S(1)}, bf16[512,256]{1,0:T(8,128)(2,1)}, u32[]{:S(2)}) copy-start(bf16[512,256]{1,0:T(8,128)(2,1)} %refs_0_.3) | copy-start | bytes 786436
  18.5 3.2 %collective-permute-start.4 = (bf16[1024,256]{1,0:T(8,128)(2,1)S(1)}, bf16[1024,256]{1,0:T(8,128)(2,1)S(1)}, u32[]{:S(2)}, u32[]{:S(2)}) collective-permute-start(bf16[1024,256]{1,0:T(8,128)(2,1)S(1)} %get-tuple-element.49), channel_id=1, source_target_pairs={{0,1},{1,0},{2,3},{3,2},{4,5},{5,4},{6,7},{7,6},{8,9},{9,8},{10,11... | collective-permute-start | bytes 1572872 | tf_op jit(solution)/shard_map/ppermute | solution.py:466
  19.8 11.1 %copy-start.1 = (bf16[512,256]{1,0:T(8,128)(2,1)S(1)}, bf16[512,256]{1,0:T(8,128)(2,1)}, u32[]{:S(2)}) copy-start(bf16[512,256]{1,0:T(8,128)(2,1)} %cotangent_ref.3) | copy-start | bytes 786436
  19.9 11.1 %copy-start.6 = (s32[512]{0:T(512)S(1)}, s32[512]{0:T(512)}, u32[]{:S(2)}) copy-start(s32[512]{0:T(512)} %param.16) | copy-start | bytes 6148
  19.9 18.0 %copy-start.3 = (bf16[256,256]{1,0:T(8,128)(2,1)S(1)}, bf16[256,256]{1,0:T(8,128)(2,1)}, u32[]{:S(2)}) copy-start(bf16[256,256]{1,0:T(8,128)(2,1)} %weight_ref.3) | copy-start | bytes 393220
  21.2 2.3 %collective-permute-start.3 = (bf16[1024,256]{1,0:T(8,128)(2,1)S(1)}, bf16[1024,256]{1,0:T(8,128)(2,1)S(1)}, u32[]{:S(2)}, u32[]{:S(2)}) collective-permute-start(bf16[1024,256]{1,0:T(8,128)(2,1)S(1)} %get-tuple-element.47), channel_id=1, source_target_pairs={{0,1},{1,0},{2,3},{3,2},{4,5},{5,4},{6,7},{7,6},{8,9},{9,8},{10,11... | collective-permute-start | bytes 1572872 | tf_op jit(solution)/shard_map/ppermute | solution.py:466
  21.8 6.4 %collective-permute-start.6 = (bf16[256,256]{1,0:T(8,128)(2,1)S(1)}, bf16[256,256]{1,0:T(8,128)(2,1)S(1)}, u32[]{:S(2)}, u32[]{:S(2)}) collective-permute-start(bf16[256,256]{1,0:T(8,128)(2,1)S(1)} %get-tuple-element.50), channel_id=1, source_target_pairs={{0,2},{1,3},{2,0},{3,1},{4,6},{5,7},{6,4},{7,5},{8,10},{9,11},{10,... | collective-permute-start | bytes 393224 | tf_op jit(solution)/shard_map/ppermute | solution.py:466
  23.5 9.5 %collective-permute-start.5 = (bf16[256,256]{1,0:T(8,128)(2,1)S(1)}, bf16[256,256]{1,0:T(8,128)(2,1)S(1)}, u32[]{:S(2)}, u32[]{:S(2)}) collective-permute-start(bf16[256,256]{1,0:T(8,128)(2,1)S(1)} %get-tuple-element.52), channel_id=1, source_target_pairs={{0,2},{1,3},{2,0},{3,1},{4,6},{5,7},{6,4},{7,5},{8,10},{9,11},{10,... | collective-permute-start | bytes 393224 | tf_op jit(solution)/shard_map/ppermute | solution.py:466
  25.0 12.9 %collective-permute-start.7 = (bf16[256,256]{1,0:T(8,128)(2,1)S(1)}, bf16[256,256]{1,0:T(8,128)(2,1)S(1)}, u32[]{:S(2)}, u32[]{:S(2)}) collective-permute-start(bf16[256,256]{1,0:T(8,128)(2,1)S(1)} %get-tuple-element.56), channel_id=1, source_target_pairs={{0,2},{1,3},{2,0},{3,1},{4,6},{5,7},{6,4},{7,5},{8,10},{9,11},{10,... | collective-permute-start | bytes 393224 | tf_op jit(solution)/shard_map/ppermute | solution.py:466
  28.3 9.6 %collective-permute-start.8 = (bf16[256,256]{1,0:T(8,128)(2,1)S(1)}, bf16[256,256]{1,0:T(8,128)(2,1)S(1)}, u32[]{:S(2)}, u32[]{:S(2)}) collective-permute-start(bf16[256,256]{1,0:T(8,128)(2,1)S(1)} %combine.6), channel_id=1, source_target_pairs={{0,4},{1,5},{2,6},{3,7},{4,0},{5,1},{6,2},{7,3},{8,12},{9,13},{10,... | collective-permute-start | bytes 393224 | tf_op jit(solution)/shard_map/ppermute | solution.py:466
  31.4 11.6 %collective-permute-start.9 = (bf16[256,256]{1,0:T(8,128)(2,1)S(1)}, bf16[256,256]{1,0:T(8,128)(2,1)S(1)}, u32[]{:S(2)}, u32[]{:S(2)}) collective-permute-start(bf16[256,256]{1,0:T(8,128)(2,1)S(1)} %get-tuple-element.62), channel_id=1, source_target_pairs={{0,2},{1,3},{2,0},{3,1},{4,6},{5,7},{6,4},{7,5},{8,10},{9,11},{10,... | collective-permute-start | bytes 393224 | tf_op jit(solution)/shard_map/ppermute | solution.py:466
  33.1 9.9 %collective-permute-start.10 = (bf16[256,256]{1,0:T(8,128)(2,1)S(1)}, bf16[256,256]{1,0:T(8,128)(2,1)S(1)}, u32[]{:S(2)}, u32[]{:S(2)}) collective-permute-start(bf16[256,256]{1,0:T(8,128)(2,1)S(1)} %combine.7), channel_id=1, source_target_pairs={{0,4},{1,5},{2,6},{3,7},{4,0},{5,1},{6,2},{7,3},{8,12},{9,13},{10,... | collective-permute-start | bytes 393224 | tf_op jit(solution)/shard_map/ppermute | solution.py:466
  38.3 11.1 %collective-permute-start.16 = (bf16[256,256]{1,0:T(8,128)(2,1)S(1)}, bf16[256,256]{1,0:T(8,128)(2,1)S(1)}, u32[]{:S(2)}, u32[]{:S(2)}) collective-permute-start(bf16[256,256]{1,0:T(8,128)(2,1)S(1)} %get-tuple-element.60.refs_0_), channel_id=1, source_target_pairs={{0,2},{1,3},{2,0},{3,1},{4,6},{5,7},{6,4},{7,5},{8,10},{9,11},{10,... | collective-permute-start | bytes 393224 | tf_op jit(solution)/shard_map/ppermute | solution.py:466
  39.7 9.6 %collective-permute-start.15 = (bf16[256,256]{1,0:T(8,128)(2,1)S(1)}, bf16[256,256]{1,0:T(8,128)(2,1)S(1)}, u32[]{:S(2)}, u32[]{:S(2)}) collective-permute-start(bf16[256,256]{1,0:T(8,128)(2,1)S(1)} %get-tuple-element.60.refs_0_), channel_id=1, source_target_pairs={{0,4},{1,5},{2,6},{3,7},{4,0},{5,1},{6,2},{7,3},{8,12},{9,13},{10,... | collective-permute-start | bytes 393224 | tf_op jit(solution)/shard_map/ppermute | solution.py:466
  43.5 9.1 %collective-permute-start.21 = (bf16[256,256]{1,0:T(8,128)(2,1)S(1)}, bf16[256,256]{1,0:T(8,128)(2,1)S(1)}, u32[]{:S(2)}, u32[]{:S(2)}) collective-permute-start(bf16[256,256]{1,0:T(8,128)(2,1)S(1)} %get-tuple-element.73.refs_1_), channel_id=1, source_target_pairs={{0,2},{1,3},{2,0},{3,1},{4,6},{5,7},{6,4},{7,5},{8,10},{9,11},{10,... | collective-permute-start | bytes 393224 | tf_op jit(solution)/shard_map/ppermute | solution.py:466
  45.4 7.2 %collective-permute-start.20 = (bf16[256,256]{1,0:T(8,128)(2,1)S(1)}, bf16[256,256]{1,0:T(8,128)(2,1)S(1)}, u32[]{:S(2)}, u32[]{:S(2)}) collective-permute-start(bf16[256,256]{1,0:T(8,128)(2,1)S(1)} %get-tuple-element.73.refs_1_), channel_id=1, source_target_pairs={{0,4},{1,5},{2,6},{3,7},{4,0},{5,1},{6,2},{7,3},{8,12},{9,13},{10,... | collective-permute-start | bytes 393224 | tf_op jit(solution)/shard_map/ppermute | solution.py:466
  49.3 1.3 %collective-permute-start.11 = (bf16[160,256]{1,0:T(8,128)(2,1)S(1)}, bf16[160,256]{1,0:T(8,128)(2,1)S(1)}, u32[]{:S(2)}, u32[]{:S(2)}) collective-permute-start(bf16[160,256]{1,0:T(8,128)(2,1)S(1)} %get-tuple-element.67), channel_id=1, source_target_pairs={{0,1},{1,0},{2,3},{3,2},{4,5},{5,4},{6,7},{7,6},{8,9},{9,8},{10,11... | collective-permute-start | bytes 245768 | tf_op jit(solution)/shard_map/ppermute | solution.py:466
  49.4 14.9 %collective-permute-start.17 = (bf16[768,256]{1,0:T(8,128)(2,1)S(1)}, bf16[768,256]{1,0:T(8,128)(2,1)S(1)}, u32[]{:S(2)}, u32[]{:S(2)}) collective-permute-start(bf16[768,256]{1,0:T(8,128)(2,1)S(1)} %pad_maximum_fusion), channel_id=1, source_target_pairs={{0,1},{1,0},{2,3},{3,2},{4,5},{5,4},{6,7},{7,6},{8,9},{9,8},{10,11... | collective-permute-start | bytes 1179656 | tf_op jit(solution)/shard_map/ppermute | solution.py:466
  50.6 4.6 %collective-permute-start.12 = (bf16[160,256]{1,0:T(8,128)(2,1)S(1)}, bf16[160,256]{1,0:T(8,128)(2,1)S(1)}, u32[]{:S(2)}, u32[]{:S(2)}) collective-permute-start(bf16[160,256]{1,0:T(8,128)(2,1)S(1)} %add_messages.5.own_ref), channel_id=1, source_target_pairs={{0,8},{8,0},{16,24},{24,16},{1,9},{9,1},{17,25},{25,17},{2,10},{10... | collective-permute-start | bytes 245768 | tf_op jit(solution)/shard_map/ppermute | solution.py:466
  51.9 5.3 %collective-permute-start.18 = (bf16[256,256]{1,0:T(8,128)(2,1)S(1)}, bf16[256,256]{1,0:T(8,128)(2,1)S(1)}, u32[]{:S(2)}, u32[]{:S(2)}) collective-permute-start(bf16[256,256]{1,0:T(8,128)(2,1)S(1)} %collective-permute-done.15.refs_2_), channel_id=1, source_target_pairs={{0,2},{1,3},{2,0},{3,1},{4,6},{5,7},{6,4},{7,5},{8,10},{9,11},{10,... | collective-permute-start | bytes 393224 | tf_op jit(solution)/shard_map/ppermute | solution.py:466
  52.6 14.3 %collective-permute-start.22 = (bf16[768,256]{1,0:T(8,128)(2,1)S(1)}, bf16[768,256]{1,0:T(8,128)(2,1)S(1)}, u32[]{:S(2)}, u32[]{:S(2)}) collective-permute-start(bf16[768,256]{1,0:T(8,128)(2,1)S(1)} %pad_maximum_fusion.1), channel_id=1, source_target_pairs={{0,1},{1,0},{2,3},{3,2},{4,5},{5,4},{6,7},{7,6},{8,9},{9,8},{10,11... | collective-permute-start | bytes 1179656 | tf_op jit(solution)/shard_map/ppermute | solution.py:466
  55.2 4.5 %collective-permute-start.13 = (bf16[160,256]{1,0:T(8,128)(2,1)S(1)}, bf16[160,256]{1,0:T(8,128)(2,1)S(1)}, u32[]{:S(2)}, u32[]{:S(2)}) collective-permute-start(bf16[160,256]{1,0:T(8,128)(2,1)S(1)} %add_messages.6.own_ref), channel_id=1, source_target_pairs={{0,16},{8,24},{16,0},{24,8},{1,17},{9,25},{17,1},{25,9},{2,18},{10... | collective-permute-start | bytes 245768 | tf_op jit(solution)/shard_map/ppermute | solution.py:466
  56.8 5.8 %collective-permute-start.23 = (bf16[256,256]{1,0:T(8,128)(2,1)S(1)}, bf16[256,256]{1,0:T(8,128)(2,1)S(1)}, u32[]{:S(2)}, u32[]{:S(2)}) collective-permute-start(bf16[256,256]{1,0:T(8,128)(2,1)S(1)} %collective-permute-done.20.refs_3_), channel_id=1, source_target_pairs={{0,2},{1,3},{2,0},{3,1},{4,6},{5,7},{6,4},{7,5},{8,10},{9,11},{10,... | collective-permute-start | bytes 393224 | tf_op jit(solution)/shard_map/ppermute | solution.py:466
  57.2 7.1 %collective-permute-start.19 = (bf16[256,256]{1,0:T(8,128)(2,1)S(1)}, bf16[256,256]{1,0:T(8,128)(2,1)S(1)}, u32[]{:S(2)}, u32[]{:S(2)}) collective-permute-start(bf16[256,256]{1,0:T(8,128)(2,1)S(1)} %collective-permute-done.18.refs_6_), channel_id=1, source_target_pairs={{0,1},{1,0},{2,3},{3,2},{4,5},{5,4},{6,7},{7,6},{8,9},{9,8},{10,11... | collective-permute-start | bytes 393224 | tf_op jit(solution)/shard_map/ppermute | solution.py:466
  59.8 4.5 %collective-permute-start.14 = (bf16[160,256]{1,0:T(8,128)(2,1)S(1)}, bf16[160,256]{1,0:T(8,128)(2,1)S(1)}, u32[]{:S(2)}, u32[]{:S(2)}) collective-permute-start(bf16[160,256]{1,0:T(8,128)(2,1)S(1)} %add_messages.7.own_ref), channel_id=1, source_target_pairs={{0,2},{1,3},{2,0},{3,1},{4,6},{5,7},{6,4},{7,5},{8,10},{9,11},{10,... | collective-permute-start | bytes 245768 | tf_op jit(solution)/shard_map/ppermute | solution.py:466
  62.7 4.2 %collective-permute-start.24 = (bf16[256,256]{1,0:T(8,128)(2,1)S(1)}, bf16[256,256]{1,0:T(8,128)(2,1)S(1)}, u32[]{:S(2)}, u32[]{:S(2)}) collective-permute-start(bf16[256,256]{1,0:T(8,128)(2,1)S(1)} %collective-permute-done.23.refs_7_), channel_id=1, source_target_pairs={{0,1},{1,0},{2,3},{3,2},{4,5},{5,4},{6,7},{7,6},{8,9},{9,8},{10,11... | collective-permute-start | bytes 393224 | tf_op jit(solution)/shard_map/ppermute | solution.py:466
  69.1 12.3 %collective-permute-start.26 = (bf16[512,256]{1,0:T(8,128)(2,1)S(1)}, bf16[512,256]{1,0:T(8,128)(2,1)S(1)}, u32[]{:S(2)}, u32[]{:S(2)}) collective-permute-start(bf16[512,256]{1,0:T(8,128)(2,1)S(1)} %get-tuple-element.80), channel_id=1, source_target_pairs={{0,8},{8,0},{16,24},{24,16},{1,9},{9,1},{17,25},{25,17},{2,10},{10... | collective-permute-start | bytes 786440 | tf_op jit(solution)/shard_map/ppermute | solution.py:466
  70.4 11.6 %collective-permute-start.27 = (bf16[512,256]{1,0:T(8,128)(2,1)S(1)}, bf16[512,256]{1,0:T(8,128)(2,1)S(1)}, u32[]{:S(2)}, u32[]{:S(2)}) collective-permute-start(bf16[512,256]{1,0:T(8,128)(2,1)S(1)} %get-tuple-element.81), channel_id=1, source_target_pairs={{0,16},{8,24},{16,0},{24,8},{1,17},{9,25},{17,1},{25,9},{2,18},{10... | collective-permute-start | bytes 786440 | tf_op jit(solution)/shard_map/ppermute | solution.py:466
  71.2 10.7 %collective-permute-start.28 = (bf16[512,256]{1,0:T(8,128)(2,1)S(1)}, bf16[512,256]{1,0:T(8,128)(2,1)S(1)}, u32[]{:S(2)}, u32[]{:S(2)}) collective-permute-start(bf16[512,256]{1,0:T(8,128)(2,1)S(1)} %get-tuple-element.77), channel_id=1, source_target_pairs={{0,24},{8,16},{16,8},{24,0},{1,25},{9,17},{17,9},{25,1},{2,26},{10... | collective-permute-start | bytes 786440 | tf_op jit(solution)/shard_map/ppermute | solution.py:466
  72.7 6.1 %collective-permute-start.25 = (bf16[160,256]{1,0:T(8,128)(2,1)S(1)}, bf16[160,256]{1,0:T(8,128)(2,1)S(1)}, u32[]{:S(2)}, u32[]{:S(2)}) collective-permute-start(bf16[160,256]{1,0:T(8,128)(2,1)S(1)} %add_messages.8.own_ref), channel_id=1, source_target_pairs={{0,4},{1,5},{2,6},{3,7},{4,0},{5,1},{6,2},{7,3},{8,12},{9,13},{10,... | collective-permute-start | bytes 245768 | tf_op jit(solution)/shard_map/ppermute | solution.py:466
  78.8 1.3 %collective-permute-start.29 = (bf16[160,256]{1,0:T(8,128)(2,1)S(1)}, bf16[160,256]{1,0:T(8,128)(2,1)S(1)}, u32[]{:S(2)}, u32[]{:S(2)}) collective-permute-start(bf16[160,256]{1,0:T(8,128)(2,1)S(1)} %add_messages.9.own_ref), channel_id=1, source_target_pairs={{0,1},{1,0},{2,3},{3,2},{4,5},{5,4},{6,7},{7,6},{8,9},{9,8},{10,11... | collective-permute-start | bytes 245768 | tf_op jit(solution)/shard_map/ppermute | solution.py:466
